TPU v7x, 32 devices: a whole 2x2x4 slice. The times are simulated.
32 devices in a mesh: fsdp: 16 (over z, y, core), rep: 2 (over x).
Axes of the slice: x: 2, y: 2, z: 4, core: 2. Of those that a mesh axis runs over, the one named last changes fastest.
Arguments:
- class_ids: int32 [32], P(('fsdp', 'rep')), may hold values from 0 to 999
- null_mask: int32 [32], P(('fsdp', 'rep')), may hold values 0 or 1
- code_ids: int32 [32, 256], P(('fsdp', 'rep')), may hold values from 0 to 16383
- lengths: int32 [32], P(('fsdp', 'rep')), may hold values from 0 to 256, as said below
- code_table: float32 [16384, 768], P('fsdp'), may hold values from -6 to 6
- code_first: float32 [16384, 768], P('fsdp'), may hold values from -1.1920929e-07 to 1.1920929e-07
- code_second: float32 [16384, 768], P('fsdp'), may hold values from 4.1392115e-16 to 1.6556846e-15
- class_table: float32 [1001, 768], P(None, 'fsdp'), may hold values from -6 to 6
- class_first: float32 [1001, 768], P(None, 'fsdp'), may hold values from -5.2154064e-08 to 5.2154064e-08
- class_second: float32 [1001, 768], P(None, 'fsdp'), may hold values from 7.9393464e-17 to 3.1757385e-16
- qkv_weight: float32 [2304, 768], P('fsdp'), may hold values from -0.21875 to 0.21875
- qkv_first: float32 [2304, 768], P('fsdp'), may hold values from -1.9073486e-06 to 1.9073486e-06
- qkv_second: float32 [2304, 768], P('fsdp'), may hold values from 1.2115784e-13 to 4.846314e-13
- out_weight: float32 [768, 768], P('fsdp'), may hold values from -0.625 to 0.625
- out_first: float32 [768, 768], P('fsdp'), may hold values from -1.9073486e-06 to 1.9073486e-06
- out_second: float32 [768, 768], P('fsdp'), may hold values from 1.2115784e-13 to 4.846314e-13
- gate_up: float32 [4096, 768], P('fsdp'), may hold values from -0.21875 to 0.21875
- gate_up_first: float32 [4096, 768], P('fsdp'), may hold values from -1.9073486e-06 to 1.9073486e-06
- gate_up_second: float32 [4096, 768], P('fsdp'), may hold values from 1.2115784e-13 to 4.846314e-13
- down_weight: float32 [768, 2048], P('fsdp'), may hold values from -0.125 to 0.125
- down_first: float32 [768, 2048], P('fsdp'), may hold values from -1.9073486e-06 to 1.9073486e-06
- down_second: float32 [768, 2048], P('fsdp'), may hold values from 1.2115784e-13 to 4.846314e-13
- head_weight: float32 [16384, 768], P('fsdp'), may hold values from -0.21875 to 0.21875
- head_first: float32 [16384, 768], P('fsdp'), may hold values from -1.9073486e-06 to 1.9073486e-06
- head_second: float32 [16384, 768], P('fsdp'), may hold values from 1.2115784e-13 to 4.846314e-13
- norm_gains: float32 [3, 768], P(None, 'fsdp'), may hold values from 0.5 to 1.5
- gains_first: float32 [3, 768], P(None, 'fsdp'), may hold values from -1.9073486e-06 to 1.9073486e-06
- gains_second: float32 [3, 768], P(None, 'fsdp'), may hold values from 1.2115784e-13 to 4.846314e-13
Outputs:
- loss_sum: float32 [], replicated
- token_count: float32 [], replicated
- grad_norm: float32 [], replicated
- new_code_table: float32 [16384, 768], P('fsdp')
- new_code_first: float32 [16384, 768], P('fsdp')
- new_code_second: float32 [16384, 768], P('fsdp')
- new_class_table: float32 [1001, 768], P(None, 'fsdp')
- new_class_first: float32 [1001, 768], P(None, 'fsdp')
- new_class_second: float32 [1001, 768], P(None, 'fsdp')
- new_qkv_weight: float32 [2304, 768], P('fsdp')
- new_qkv_first: float32 [2304, 768], P('fsdp')
- new_qkv_second: float32 [2304, 768], P('fsdp')
- new_out_weight: float32 [768, 768], P('fsdp')
- new_out_first: float32 [768, 768], P('fsdp')
- new_out_second: float32 [768, 768], P('fsdp')
- new_gate_up: float32 [4096, 768], P('fsdp')
- new_gate_up_first: float32 [4096, 768], P('fsdp')
- new_gate_up_second: float32 [4096, 768], P('fsdp')
- new_down_weight: float32 [768, 2048], P('fsdp')
- new_down_first: float32 [768, 2048], P('fsdp')
- new_down_second: float32 [768, 2048], P('fsdp')
- new_head_weight: float32 [16384, 768], P('fsdp')
- new_head_first: float32 [16384, 768], P('fsdp')
- new_head_second: float32 [16384, 768], P('fsdp')
- new_norm_gains: float32 [3, 768], P(None, 'fsdp')
- new_gains_first: float32 [3, 768], P(None, 'fsdp')
- new_gains_second: float32 [3, 768], P(None, 'fsdp')
Inputs may be any that keep to these rules, and one draw needn't show every extreme that they name: `lengths`: image slot 0 is empty (0) and the last image slot counts all 256 positions; a counted prefix of an image slot is 0 or at least 42.
All inputs are finite; a program needn't handle non-finite values. No bound on the sum of `null_mask` on one device may be relied on, other than what follows from the above.
Results may differ from a plain program's by a relative error of at most 0.018.
Values may be sent and summed in bfloat16 or wider, within the bound.
A program may use at most 384 MiB of HBM per device.

v0:
```python
import jax
import jax.numpy as jnp
from jax import lax
from jax.sharding import PartitionSpec as P

HEAD_DIM = 64
CLIP_INV = 500
STEP = 10


NORM_EPS = 1e-05
BETA_ONE = 0.5
BETA_TWO = 0.5
ADAM_EPS = 1e-08


def rotary_tables(length, width):
    half = width // 2
    freq = 10000.0 ** (-jnp.arange(half, dtype=jnp.float32) * 2.0 / width)
    angles = jnp.arange(length, dtype=jnp.float32)[:, None] * freq[None, :]
    cosine = jnp.concatenate([jnp.cos(angles), jnp.cos(angles)], -1)
    sine = jnp.concatenate([jnp.sin(angles), jnp.sin(angles)], -1)
    return (cosine, sine)


def rotate(values, cosine, sine):
    half = values.shape[-1] // 2
    swapped = jnp.concatenate([-values[..., half:], values[..., :half]], -1)
    return values * cosine[:, None, :] + swapped * sine[:, None, :]


def rotate_back(grads, cosine, sine):
    half = grads.shape[-1] // 2
    scaled = grads * sine[:, None, :]
    return grads * cosine[:, None, :] + jnp.concatenate(
        [scaled[..., half:], -scaled[..., :half]], -1
    )


def norm_forward(stream, gain):
    inverse = lax.rsqrt(jnp.mean(stream * stream, -1, keepdims=True) + NORM_EPS)
    return (stream * inverse * gain, inverse)


def norm_backward(stream, inverse, gain, grad_out):
    weighted = grad_out * gain
    inner = jnp.mean(weighted * stream, -1, keepdims=True)
    grad_in = inverse * weighted - stream * inverse * inverse * inverse * inner
    grad_gain = jnp.sum(grad_out * stream * inverse, axis=(0, 1))
    return (grad_in, grad_gain)


def attention_scores(queries, keys_rot):
    length = queries.shape[1]
    scores = jnp.einsum(
        "bqhd,bkhd->bhqk", queries, keys_rot, preferred_element_type=jnp.float32
    ) * HEAD_DIM ** (-0.5)
    causal = jnp.arange(length)[:, None] >= jnp.arange(length)[None, :]
    return jnp.where(causal, scores, -1e30)


def forward(weights, classes, code_ids, lengths):
    code_w, class_w, qkv_w, out_w, gate_w, down_w, head_w, gain_w = weights
    batch, length = code_ids.shape
    width = qkv_w.shape[1]
    hidden_width = down_w.shape[1]
    heads = width // HEAD_DIM
    gains32 = gain_w.astype(jnp.float32)
    stream0 = jnp.concatenate([class_w[classes][:, None, :], code_w[code_ids[:, :-1]]], 1).astype(
        jnp.float32
    )
    normed1, inverse1 = norm_forward(stream0, gains32[0])
    normed1 = normed1.astype(jnp.bfloat16)
    mixed = jnp.einsum("btd,ed->bte", normed1, qkv_w, preferred_element_type=jnp.float32)
    cosine, sine = rotary_tables(length, HEAD_DIM)
    split4 = (batch, length, heads, HEAD_DIM)
    queries = rotate(mixed[..., :width].reshape(split4), cosine, sine).astype(jnp.bfloat16)
    keys_rot = rotate(mixed[..., width : 2 * width].reshape(split4), cosine, sine).astype(
        jnp.bfloat16
    )
    values = mixed[..., 2 * width :].reshape(split4).astype(jnp.bfloat16)
    scores = attention_scores(queries, keys_rot)
    top = jnp.max(scores, -1, keepdims=True)
    expo = jnp.exp(scores - top)
    totals = jnp.sum(expo, -1, keepdims=True)
    score_lse = top + jnp.log(totals)
    probs = (expo / totals).astype(jnp.bfloat16)
    attended = jnp.einsum("bhqk,bkhd->bqhd", probs, values, preferred_element_type=jnp.float32)
    attended = attended.astype(jnp.bfloat16).reshape(batch, length, width)
    stream1 = stream0 + jnp.einsum(
        "btd,ed->bte", attended, out_w, preferred_element_type=jnp.float32
    )
    normed2, inverse2 = norm_forward(stream1, gains32[1])
    normed2 = normed2.astype(jnp.bfloat16)
    gated = jnp.einsum("btd,fd->btf", normed2, gate_w, preferred_element_type=jnp.float32)
    hidden = (jax.nn.silu(gated[..., :hidden_width]) * gated[..., hidden_width:]).astype(
        jnp.bfloat16
    )
    stream2 = stream1 + jnp.einsum(
        "btf,df->btd", hidden, down_w, preferred_element_type=jnp.float32
    )
    normed3, inverse3 = norm_forward(stream2, gains32[2])
    normed3 = normed3.astype(jnp.bfloat16)
    logits = jnp.einsum("btd,vd->btv", normed3, head_w, preferred_element_type=jnp.float32)
    ltop = jnp.max(logits, -1, keepdims=True)
    logit_lse = jnp.log(jnp.sum(jnp.exp(logits - ltop), -1)) + ltop[..., 0]
    picked = jnp.take_along_axis(logits, code_ids[..., None], -1)[..., 0]
    counted = jnp.arange(length)[None, :] < lengths[:, None]
    loss_local = jnp.sum(jnp.where(counted, logit_lse - picked, 0.0))
    kept = (
        stream0,
        stream1,
        stream2,
        inverse1,
        inverse2,
        inverse3,
        normed1,
        normed2,
        normed3,
        queries,
        keys_rot,
        values,
        score_lse,
        attended,
        gated,
        hidden,
        logits,
        logit_lse,
    )
    return (loss_local, kept)


def backward(weights, kept, classes, code_ids, lengths, inv_count, table_rows):
    qkv_w, out_w, gate_w, down_w, head_w, gain_w = weights
    (
        stream0,
        stream1,
        stream2,
        inverse1,
        inverse2,
        inverse3,
        normed1,
        normed2,
        normed3,
        queries,
        keys_rot,
        values,
        score_lse,
        attended,
        gated,
        hidden,
        logits,
        logit_lse,
    ) = kept
    batch, length = code_ids.shape
    width = qkv_w.shape[1]
    hidden_width = down_w.shape[1]
    vocab = head_w.shape[0]
    gains32 = gain_w.astype(jnp.float32)
    counted = (jnp.arange(length)[None, :] < lengths[:, None]).astype(jnp.float32)
    onehot = (jnp.arange(vocab)[None, None, :] == code_ids[..., None]).astype(jnp.float32)
    soft = jnp.exp(logits - logit_lse[..., None])
    grad_logits = ((soft - onehot) * (counted * inv_count)[..., None]).astype(jnp.bfloat16)
    grad_head = jnp.einsum("btv,btd->vd", grad_logits, normed3, preferred_element_type=jnp.float32)
    grad_normed3 = jnp.einsum(
        "btv,vd->btd", grad_logits, head_w, preferred_element_type=jnp.float32
    )
    grad_stream2, gain_three = norm_backward(stream2, inverse3, gains32[2], grad_normed3)
    grad_branch = grad_stream2.astype(jnp.bfloat16)
    grad_down = jnp.einsum("btd,btf->df", grad_branch, hidden, preferred_element_type=jnp.float32)
    grad_hidden = jnp.einsum("btd,df->btf", grad_branch, down_w, preferred_element_type=jnp.float32)
    gate_part = gated[..., :hidden_width]
    up_part = gated[..., hidden_width:]
    sigma = jax.nn.sigmoid(gate_part)
    grad_gate = grad_hidden * up_part * sigma * (1.0 + gate_part * (1.0 - sigma))
    grad_up = grad_hidden * gate_part * sigma
    grad_gated = jnp.concatenate([grad_gate, grad_up], -1).astype(jnp.bfloat16)
    grad_gate_up = jnp.einsum(
        "btf,btd->fd", grad_gated, normed2, preferred_element_type=jnp.float32
    )
    grad_normed2 = jnp.einsum("btf,fd->btd", grad_gated, gate_w, preferred_element_type=jnp.float32)
    grad_middle, gain_two = norm_backward(stream1, inverse2, gains32[1], grad_normed2)
    grad_stream1 = grad_stream2 + grad_middle
    grad_attn = grad_stream1.astype(jnp.bfloat16)
    grad_out = jnp.einsum("bte,btd->ed", grad_attn, attended, preferred_element_type=jnp.float32)
    split4 = queries.shape
    grad_attended = jnp.einsum("bte,ed->btd", grad_attn, out_w, preferred_element_type=jnp.float32)
    grad_attended = grad_attended.astype(jnp.bfloat16).reshape(split4)
    probs32 = jnp.exp(attention_scores(queries, keys_rot) - score_lse)
    probs = probs32.astype(jnp.bfloat16)
    grad_probs = jnp.einsum(
        "bqhd,bkhd->bhqk", grad_attended, values, preferred_element_type=jnp.float32
    )
    grad_values = jnp.einsum(
        "bhqk,bqhd->bkhd", probs, grad_attended, preferred_element_type=jnp.float32
    )
    grad_scores = probs32 * (grad_probs - jnp.sum(probs32 * grad_probs, -1, keepdims=True))
    grad_scores = grad_scores.astype(jnp.bfloat16)
    scale = HEAD_DIM ** (-0.5)
    grad_queries = (
        jnp.einsum("bhqk,bkhd->bqhd", grad_scores, keys_rot, preferred_element_type=jnp.float32)
        * scale
    )
    grad_keys = (
        jnp.einsum("bhqk,bqhd->bkhd", grad_scores, queries, preferred_element_type=jnp.float32)
        * scale
    )
    cosine, sine = rotary_tables(length, HEAD_DIM)
    grad_mixed = jnp.concatenate(
        [
            rotate_back(grad_queries, cosine, sine).reshape(batch, length, width),
            rotate_back(grad_keys, cosine, sine).reshape(batch, length, width),
            grad_values.reshape(batch, length, width),
        ],
        -1,
    ).astype(jnp.bfloat16)
    grad_qkv = jnp.einsum("bte,btd->ed", grad_mixed, normed1, preferred_element_type=jnp.float32)
    grad_normed1 = jnp.einsum("bte,ed->btd", grad_mixed, qkv_w, preferred_element_type=jnp.float32)
    grad_first, gain_one = norm_backward(stream0, inverse1, gains32[0], grad_normed1)
    grad_stream0 = grad_stream1 + grad_first
    grad_codes = (
        jnp.zeros((vocab, width), jnp.float32)
        .at[code_ids[:, :-1].reshape(-1)]
        .add(grad_stream0[:, 1:].reshape(-1, width))
    )
    grad_classes = jnp.zeros((table_rows, width), jnp.float32).at[classes].add(grad_stream0[:, 0])
    grad_gains = jnp.stack([gain_one, gain_two, gain_three])
    return (
        grad_codes,
        grad_classes,
        grad_qkv,
        grad_out,
        grad_gate_up,
        grad_down,
        grad_head,
        grad_gains,
    )


def adam_update(weight, first, second, grad, rate, decay):
    first_new = BETA_ONE * first + (1.0 - BETA_ONE) * grad
    second_new = BETA_TWO * second + (1.0 - BETA_TWO) * grad * grad
    first_hat = first_new / (1.0 - BETA_ONE**STEP)
    second_hat = second_new / (1.0 - BETA_TWO**STEP)
    weight_new = weight - rate * (first_hat / (jnp.sqrt(second_hat) + ADAM_EPS) + decay * weight)
    return (weight_new, first_new, second_new)


def local(
    class_ids,
    null_mask,
    code_ids,
    lengths,
    code_table,
    code_first,
    code_second,
    class_table,
    class_first,
    class_second,
    qkv_weight,
    qkv_first,
    qkv_second,
    out_weight,
    out_first,
    out_second,
    gate_up,
    gate_up_first,
    gate_up_second,
    down_weight,
    down_first,
    down_second,
    head_weight,
    head_first,
    head_second,
    norm_gains,
    gains_first,
    gains_second,
):
    masters = (
        code_table,
        class_table,
        qkv_weight,
        out_weight,
        gate_up,
        down_weight,
        head_weight,
        norm_gains,
    )
    firsts = (
        code_first,
        class_first,
        qkv_first,
        out_first,
        gate_up_first,
        down_first,
        head_first,
        gains_first,
    )
    seconds = (
        code_second,
        class_second,
        qkv_second,
        out_second,
        gate_up_second,
        down_second,
        head_second,
        gains_second,
    )
    rates = (0.5, 0.5, 0.05, 0.05, 0.05, 0.05, 0.05, 0.5)
    decays = (0.1, 0.1, 0.1, 0.1, 0.1, 0.1, 0.1, 0.0)
    table_rows = class_table.shape[0]
    classes = jnp.where(null_mask == 1, table_rows - 1, class_ids)
    gathered = (
        lax.all_gather(code_table.astype(jnp.bfloat16), "fsdp", axis=0, tiled=True),
        lax.all_gather(class_table.astype(jnp.bfloat16), "fsdp", axis=1, tiled=True),
        lax.all_gather(qkv_weight.astype(jnp.bfloat16), "fsdp", axis=0, tiled=True),
        lax.all_gather(out_weight.astype(jnp.bfloat16), "fsdp", axis=0, tiled=True),
        lax.all_gather(gate_up.astype(jnp.bfloat16), "fsdp", axis=0, tiled=True),
        lax.all_gather(down_weight.astype(jnp.bfloat16), "fsdp", axis=0, tiled=True),
        lax.all_gather(head_weight.astype(jnp.bfloat16), "fsdp", axis=0, tiled=True),
        lax.all_gather(norm_gains.astype(jnp.bfloat16), "fsdp", axis=1, tiled=True),
    )
    loss_local, kept = forward(gathered, classes, code_ids, lengths)
    length = code_ids.shape[1]
    count_local = jnp.sum((jnp.arange(length)[None, :] < lengths[:, None]).astype(jnp.float32))
    loss_sum, token_count = lax.psum((loss_local, count_local), ("fsdp", "rep"))
    layer_weights = (
        lax.all_gather(qkv_weight.astype(jnp.bfloat16), "fsdp", axis=0, tiled=True),
        lax.all_gather(out_weight.astype(jnp.bfloat16), "fsdp", axis=0, tiled=True),
        lax.all_gather(gate_up.astype(jnp.bfloat16), "fsdp", axis=0, tiled=True),
        lax.all_gather(down_weight.astype(jnp.bfloat16), "fsdp", axis=0, tiled=True),
        lax.all_gather(head_weight.astype(jnp.bfloat16), "fsdp", axis=0, tiled=True),
        lax.all_gather(norm_gains.astype(jnp.bfloat16), "fsdp", axis=1, tiled=True),
    )
    grad_codes, grad_classes, grad_qkv, grad_out, grad_gate_up, grad_down, grad_head, grad_gains = (
        backward(layer_weights, kept, classes, code_ids, lengths, 1.0 / token_count, table_rows)
    )
    pieces = (
        lax.psum_scatter(grad_codes, ("fsdp", "rep"), scatter_dimension=0, tiled=True),
        lax.psum_scatter(grad_classes, ("fsdp", "rep"), scatter_dimension=1, tiled=True),
        lax.psum_scatter(grad_qkv, ("fsdp", "rep"), scatter_dimension=0, tiled=True),
        lax.psum_scatter(grad_out, ("fsdp", "rep"), scatter_dimension=0, tiled=True),
        lax.psum_scatter(grad_gate_up, ("fsdp", "rep"), scatter_dimension=0, tiled=True),
        lax.psum_scatter(grad_down, ("fsdp", "rep"), scatter_dimension=0, tiled=True),
        lax.psum_scatter(grad_head, ("fsdp", "rep"), scatter_dimension=0, tiled=True),
        lax.psum_scatter(grad_gains, ("fsdp", "rep"), scatter_dimension=1, tiled=True),
    )
    reduced = (
        lax.all_gather(pieces[0], "rep", axis=0, tiled=True),
        lax.all_gather(pieces[1], "rep", axis=1, tiled=True),
        lax.all_gather(pieces[2], "rep", axis=0, tiled=True),
        lax.all_gather(pieces[3], "rep", axis=0, tiled=True),
        lax.all_gather(pieces[4], "rep", axis=0, tiled=True),
        lax.all_gather(pieces[5], "rep", axis=0, tiled=True),
        lax.all_gather(pieces[6], "rep", axis=0, tiled=True),
        lax.all_gather(pieces[7], "rep", axis=1, tiled=True),
    )
    squares = jnp.zeros((), jnp.float32)
    for grad_piece in reduced:
        squares = squares + jnp.sum(grad_piece * grad_piece)
    grad_norm = jnp.sqrt(lax.psum(squares, "fsdp"))
    factor = jnp.minimum(1.0, 1.0 / CLIP_INV / (grad_norm + 1e-06))
    results = [loss_sum, token_count, grad_norm]
    for index in range(8):
        results.extend(
            adam_update(
                masters[index],
                firsts[index],
                seconds[index],
                reduced[index] * factor,
                rates[index],
                decays[index],
            )
        )
    return tuple(results)


def solution(mesh):
    return jax.shard_map(
        local,
        mesh=mesh,
        in_specs=(
            P(("fsdp", "rep")),
            P(("fsdp", "rep")),
            P(("fsdp", "rep"), None),
            P(("fsdp", "rep")),
            P("fsdp", None),
            P("fsdp", None),
            P("fsdp", None),
            P(None, "fsdp"),
            P(None, "fsdp"),
            P(None, "fsdp"),
            P("fsdp", None),
            P("fsdp", None),
            P("fsdp", None),
            P("fsdp", None),
            P("fsdp", None),
            P("fsdp", None),
            P("fsdp", None),
            P("fsdp", None),
            P("fsdp", None),
            P("fsdp", None),
            P("fsdp", None),
            P("fsdp", None),
            P("fsdp", None),
            P("fsdp", None),
            P("fsdp", None),
            P(None, "fsdp"),
            P(None, "fsdp"),
            P(None, "fsdp"),
        ),
        out_specs=(
            P(),
            P(),
            P(),
            P("fsdp", None),
            P("fsdp", None),
            P("fsdp", None),
            P(None, "fsdp"),
            P(None, "fsdp"),
            P(None, "fsdp"),
            P("fsdp", None),
            P("fsdp", None),
            P("fsdp", None),
            P("fsdp", None),
            P("fsdp", None),
            P("fsdp", None),
            P("fsdp", None),
            P("fsdp", None),
            P("fsdp", None),
            P("fsdp", None),
            P("fsdp", None),
            P("fsdp", None),
            P("fsdp", None),
            P("fsdp", None),
            P("fsdp", None),
            P(None, "fsdp"),
            P(None, "fsdp"),
            P(None, "fsdp"),
        ),
        check_vma=False,
    )
```

profile of v0, /device:TPU:0, one launch (start us, length us, event | category | flops | bytes accessed | tf_op | source)
XLA Modules:
  0.0 2258.3 jit_solution(862164885469489130)
XLA Ops:
  21.2 42.2 %psum.22 = f32[]{:T(128)} all-reduce(f32[]{:T(128)} %fusion.58), channel_id=1, replica_groups=mesh['fsdp'=16,'rep'=2] {'fsdp','rep'}, use_global_device_ids=true, to_apply=%region_10.11 | all-reduce | flops 1 | bytes 8 | tf_op jit(solution)/shard_map/psum | solution.py:326
  64.7 21.3 all-gather
  90.8 92.3 %all-gather.14.cloned.1.call-done = bf16[16384,768]{1,0:T(8,128)(2,1)} async-done(((bf16[1024,768]{1,0:T(8,128)(2,1)}), bf16[16384,768]{1,0:T(8,128)(2,1)}) %all-gather.14.cloned.1.call-update) | async-done | bytes 25165840 | tf_op jit(solution)/shard_map/all_gather | solution.py:314
  183.1 12.8 gather_fusion
  196.1 37.1 %all-gather.16.cloned.1.call-done = bf16[2304,768]{1,0:T(8,128)(2,1)} async-done(((bf16[144,768]{1,0:T(8,128)(2,1)}), bf16[2304,768]{1,0:T(8,128)(2,1)}) %all-gather.16.cloned.1.call-update) | async-done | bytes 3538960 | tf_op jit(solution)/shard_map/all_gather | solution.py:316
  242.8 30.6 %all-gather.18.cloned.1.call-done = bf16[768,768]{1,0:T(8,128)(2,1)} async-done(((bf16[48,768]{1,0:T(8,128)(2,1)}), bf16[768,768]{1,0:T(8,128)(2,1)}) %all-gather.18.cloned.1.call-update) | async-done | bytes 1179664 | tf_op jit(solution)/shard_map/all_gather | solution.py:317
  276.1 60.7 %all-gather.20.cloned.1.call-done = bf16[4096,768]{1,0:T(8,128)(2,1)} async-done(((bf16[256,768]{1,0:T(8,128)(2,1)}), bf16[4096,768]{1,0:T(8,128)(2,1)}) %all-gather.20.cloned.1.call-update) | async-done | bytes 6291472 | tf_op jit(solution)/shard_map/all_gather | solution.py:318
  345.3 38.1 %all-gather.22.cloned.1.call-done = bf16[768,2048]{1,0:T(8,128)(2,1)} async-done(((bf16[48,2048]{1,0:T(8,128)(2,1)}), bf16[768,2048]{1,0:T(8,128)(2,1)}) %all-gather.22.cloned.1.call-update) | async-done | bytes 3145744 | tf_op jit(solution)/shard_map/all_gather | solution.py:319
  388.6 124.4 %all-gather.24.cloned.1.call-done = bf16[16384,768]{1,0:T(8,128)(2,1)} async-done(((bf16[1024,768]{1,0:T(8,128)(2,1)}), bf16[16384,768]{1,0:T(8,128)(2,1)}) %all-gather.24.cloned.1.call-update) | async-done | bytes 25165840 | tf_op jit(solution)/shard_map/all_gather | solution.py:320
  513.0 18.4 fusion.83
  531.4 8.1 exponential_reduce_fusion
  540.1 21.9 multiply_reduce_fusion.3
  586.0 22.3 scatter_custom_fusion
  609.4 41.0 %fusion.68 = f32[16384,768]{1,0:T(8,128)} fusion(f32[256,768]{1,0:T(8,128)S(1)} %copy-done, f32[768]{0:T(1024)S(1)} %get-tuple-element.56, f32[256]{0:T(256)S(1)} %add_rsqrt_fusion, f32[256,16384]{1,0:T(8,128)} %get-tuple-element.116, f32[256]{0:T(256)S(1)} %copy-done.66, s32[256]{0:T(256)S(1)} %bitcast.143, f32[256]{0:T(256)S(1)} %copy-done.61), kind=kOutput, calls=%fused_computation.188 | convolution fusion | flops 6468206592 | bytes 67902464 | tf_op jit(solution)/shard_map/btv,btd->vd/dot_general | solution.py:164
  660.9 6.3 fusion.16
  675.8 6.4 fusion.10
  682.4 357.6 %reduce-scatter.9.cloned.1.call-done = f32[512,768]{1,0:T(8,128)} async-done(((f32[16384,768]{1,0:T(8,128)}), f32[512,768]{1,0:T(8,128)}) %reduce-scatter.9.cloned.1.call-update) | async-done | bytes 1572880 | tf_op jit(solution)/shard_map/reduce_scatter | solution.py:339
  1040.1 436.8 %reduce-scatter.21.cloned.1.call-done = f32[512,768]{1,0:T(8,128)} async-done(((f32[16384,768]{1,0:T(8,128)}), f32[512,768]{1,0:T(8,128)}) %reduce-scatter.21.cloned.1.call-update) | async-done | bytes 1572880 | tf_op jit(solution)/shard_map/reduce_scatter | solution.py:345
  1481.1 39.4 %all-reduce.1 = (f32[]{:T(128)}, f32[3,768]{1,0:T(4,128)S(1)}) all-reduce(f32[]{:T(128)} %fusion.63, f32[3,768]{1,0:T(4,128)S(1)} %pad_maximum_fusion.9), channel_id=1, replica_groups=mesh['fsdp'=16,'rep'=2] {'fsdp','rep'}, use_global_device_ids=true, to_apply=%region_8.9 | all-reduce | flops 2305 | bytes 18440 | tf_op jit(solution)/shard_map/psum | solution.py:326
  1525.7 54.9 %reduce-scatter.15.cloned.1.call-done = f32[24,768]{1,0:T(8,128)} async-done(((f32[768,768]{1,0:T(8,128)}), f32[24,768]{1,0:T(8,128)}) %reduce-scatter.15.cloned.1.call-update) | async-done | bytes 73744 | tf_op jit(solution)/shard_map/reduce_scatter | solution.py:342
  1586.5 101.6 %reduce-scatter.11.cloned.1.call-done = f32[1001,24]{0,1:T(8,128)} async-done(((f32[1001,768]{0,1:T(8,128)}), f32[1001,24]{0,1:T(8,128)}) %reduce-scatter.11.cloned.1.call-update) | async-done | bytes 96112 | tf_op jit(solution)/shard_map/reduce_scatter | solution.py:340
  1688.1 5.5 all_gather.63
  1694.2 113.6 %reduce-scatter.19.cloned.1.call-done = f32[24,2048]{1,0:T(8,128)} async-done(((f32[768,2048]{1,0:T(8,128)}), f32[24,2048]{1,0:T(8,128)}) %reduce-scatter.19.cloned.1.call-update) | async-done | bytes 196624 | tf_op jit(solution)/shard_map/reduce_scatter | solution.py:344
  1807.8 6.5 all_gather.67
  1815.0 116.7 %reduce-scatter.13.cloned.1.call-done = f32[72,768]{1,0:T(8,128)} async-done(((f32[2304,768]{1,0:T(8,128)}), f32[72,768]{1,0:T(8,128)}) %reduce-scatter.13.cloned.1.call-update) | async-done | bytes 221200 | tf_op jit(solution)/shard_map/reduce_scatter | solution.py:341
  1931.8 6.8 all_gather.64
  1939.3 154.2 %reduce-scatter.17.cloned.1.call-done = f32[128,768]{1,0:T(8,128)} async-done(((f32[4096,768]{1,0:T(8,128)}), f32[128,768]{1,0:T(8,128)}) %reduce-scatter.17.cloned.1.call-update) | async-done | bytes 393232 | tf_op jit(solution)/shard_map/reduce_scatter | solution.py:343
  2093.5 10.4 all_gather.66
  2104.7 34.3 %all-gather.26.cloned.1.call-done = f32[1024,768]{1,0:T(8,128)} async-done(((f32[512,768]{1,0:T(8,128)}), f32[1024,768]{1,0:T(8,128)}) %all-gather.26.cloned.1.call-update) | async-done | bytes 3145744 | tf_op jit(solution)/shard_map/all_gather | solution.py:349
  2146.2 39.1 %all-gather.28.cloned.1.call-done = f32[1024,768]{1,0:T(8,128)} async-done(((f32[512,768]{1,0:T(8,128)}), f32[1024,768]{1,0:T(8,128)}) %all-gather.28.cloned.1.call-update) | async-done | bytes 3145744 | tf_op jit(solution)/shard_map/all_gather | solution.py:355
  2190.0 33.9 %psum.23 = f32[]{:T(128)} all-reduce(f32[]{:T(128)S(6)} %add.352), channel_id=1, replica_groups=mesh['fsdp'=16,'rep'=2] {'fsdp'}, use_global_device_ids=true, to_apply=%region_36.37 | all-reduce | flops 1 | bytes 8 | tf_op jit(solution)/shard_map/psum | solution.py:361
  2237.7 5.3 multiply_subtract_fusion
  (288 shorter events, 132.6 us)
Async XLA Ops:
  7.2 82.4 %all-gather.12.cloned.1.call-start = ((), (), s32[]{:S(2)}) async-start(), calls=%async_computation.7 | async-start | bytes 1671168 | tf_op jit(solution)/shard_map/all_gather | solution.py:315
  8.9 174.2 %all-gather.14.cloned.1.call-start = ((), (), s32[]{:S(2)}) async-start(), calls=%async_computation.8 | async-start | bytes 26738688 | tf_op jit(solution)/shard_map/all_gather | solution.py:314
  12.1 221.1 %all-gather.16.cloned.1.call-start = ((), (), s32[]{:S(2)}) async-start(), calls=%async_computation.9 | async-start | bytes 3760128 | tf_op jit(solution)/shard_map/all_gather | solution.py:316
  14.1 259.2 %all-gather.18.cloned.1.call-start = ((), (), s32[]{:S(2)}) async-start(), calls=%async_computation.10 | async-start | bytes 1253376 | tf_op jit(solution)/shard_map/all_gather | solution.py:317
  15.7 321.1 %all-gather.20.cloned.1.call-start = ((), (), s32[]{:S(2)}) async-start(), calls=%async_computation.11 | async-start | bytes 6684672 | tf_op jit(solution)/shard_map/all_gather | solution.py:318
  17.7 365.7 %all-gather.22.cloned.1.call-start = ((), (), s32[]{:S(2)}) async-start(), calls=%async_computation.12 | async-start | bytes 3342336 | tf_op jit(solution)/shard_map/all_gather | solution.py:319
  18.5 46.2 %copy-start.67 = (f32[3,48]{1,0:T(4,128)S(1)}, f32[3,48]{1,0:T(4,128)}, u32[]{:S(2)}) copy-start(f32[3,48]{1,0:T(4,128)} %param.55) | copy-start | bytes 1732
  18.5 68.9 %copy-start.55 = (s32[1,256]{1,0:T(1,128)S(1)}, s32[1,256]{1,0:T(1,128)}, u32[]{:S(2)}) copy-start(s32[1,256]{1,0:T(1,128)} %param.32) | copy-start | bytes 3076
  18.5 494.5 %all-gather.24.cloned.1.call-start = ((), (), s32[]{:S(2)}) async-start(), calls=%async_computation.13 | async-start | bytes 26738688 | tf_op jit(solution)/shard_map/all_gather | solution.py:320
  19.9 1020.1 %reduce-scatter.9.cloned.1.call-start = ((), (), s32[]{:S(2)}) async-start(), calls=%async_computation.14 | async-start | bytes 51904512 | tf_op jit(solution)/shard_map/reduce_scatter | solution.py:339
  90.8 182.5 %copy-start.50 = (bf16[1,768]{1,0:T(2,128)(2,1)}, bf16[1,768]{1,0:T(2,128)(2,1)S(1)}, u32[]{:S(2)}) copy-start(bf16[1,768]{1,0:T(2,128)(2,1)S(1)} %copy.118) | copy-start | bytes 4612
  276.1 65.6 %copy-start.63 = (f32[256]{0:T(256)}, f32[256]{0:T(256)S(1)}, u32[]{:S(2)}) copy-start(f32[256]{0:T(256)S(1)} %add_rsqrt_fusion.1) | copy-start | bytes 3076
  608.3 868.5 %reduce-scatter.21.cloned.1.call-start = ((), (), s32[]{:S(2)}) async-start(), calls=%async_computation.21 | async-start | bytes 51904512 | tf_op jit(solution)/shard_map/reduce_scatter | solution.py:345
  650.5 930.2 %reduce-scatter.15.cloned.1.call-start = ((), (), s32[]{:S(2)}) async-start(), calls=%async_computation.18 | async-start | bytes 2433024 | tf_op jit(solution)/shard_map/reduce_scatter | solution.py:342
  653.4 1034.7 %reduce-scatter.11.cloned.1.call-start = ((), (), s32[]{:S(2)}) async-start(), calls=%async_computation.16 | async-start | bytes 3244032 | tf_op jit(solution)/shard_map/reduce_scatter | solution.py:340
  660.7 1147.1 %reduce-scatter.19.cloned.1.call-start = ((), (), s32[]{:S(2)}) async-start(), calls=%async_computation.20 | async-start | bytes 6488064 | tf_op jit(solution)/shard_map/reduce_scatter | solution.py:344
  667.3 1264.4 %reduce-scatter.13.cloned.1.call-start = ((), (), s32[]{:S(2)}) async-start(), calls=%async_computation.17 | async-start | bytes 7299072 | tf_op jit(solution)/shard_map/reduce_scatter | solution.py:341
  673.9 1419.5 %reduce-scatter.17.cloned.1.call-start = ((), (), s32[]{:S(2)}) async-start(), calls=%async_computation.19 | async-start | bytes 12976128 | tf_op jit(solution)/shard_map/reduce_scatter | solution.py:343
  682.3 794.6 %copy-start.57 = (s32[1,256]{1,0:T(1,128)S(1)}, s32[1,256]{1,0:T(1,128)}, u32[]{:S(2)}) copy-start(s32[1,256]{1,0:T(1,128)} %param.32) | copy-start | bytes 3076
  682.3 798.1 %copy-start.69 = (f32[768]{0:T(1024)S(1)}, f32[768]{0:T(1024)}, u32[]{:S(2)}) copy-start(f32[768]{0:T(1024)} %get-tuple-element.52) | copy-start | bytes 9220
  682.3 798.1 %copy-start.70 = (f32[768]{0:T(1024)S(1)}, f32[768]{0:T(1024)}, u32[]{:S(2)}) copy-start(f32[768]{0:T(1024)} %get-tuple-element.50) | copy-start | bytes 9220
  682.3 798.1 %copy-start.71 = (f32[768]{0:T(1024)S(1)}, f32[768]{0:T(1024)}, u32[]{:S(2)}) copy-start(f32[768]{0:T(1024)} %get-tuple-element.54) | copy-start | bytes 9220
  682.3 798.2 %copy-start.62 = (f32[256]{0:T(256)S(1)}, f32[256]{0:T(256)}, u32[]{:S(2)}) copy-start(f32[256]{0:T(256)} %log_add_fusion.1) | copy-start | bytes 3076
  682.3 1456.6 %all-gather.26.cloned.1.call-start = ((), (), s32[]{:S(2)}) async-start(), calls=%async_computation.15 | async-start | bytes 4718592 | tf_op jit(solution)/shard_map/all_gather | solution.py:349
  1040.0 1145.3 %all-gather.28.cloned.1.call-start = ((), (), s32[]{:S(2)}) async-start(), calls=%async_computation.22 | async-start | bytes 4718592 | tf_op jit(solution)/shard_map/all_gather | solution.py:355
  2104.7 120.1 %copy-start.41 = (f32[48,768]{1,0:T(8,128)S(1)}, f32[48,768]{1,0:T(8,128)}, u32[]{:S(2)}) copy-start(f32[48,768]{1,0:T(8,128)} %param.43) | copy-start | bytes 442372
  2104.7 122.0 %copy-start.40 = (f32[1001,48]{0,1:T(8,128)S(1)}, f32[1001,48]{0,1:T(8,128)}, u32[]{:S(2)}) copy-start(f32[1001,48]{0,1:T(8,128)} %param.37) | copy-start | bytes 576580
  2142.2 86.5 %copy-start.34 = (f32[48,2048]{1,0:T(8,128)S(1)}, f32[48,2048]{1,0:T(8,128)}, u32[]{:S(2)}) copy-start(f32[48,2048]{1,0:T(8,128)} %param.49) | copy-start | bytes 1179652
  2142.2 86.5 %copy-start.43 = (f32[48,2048]{1,0:T(8,128)S(1)}, f32[48,2048]{1,0:T(8,128)}, u32[]{:S(2)}) copy-start(f32[48,2048]{1,0:T(8,128)} %param.50) | copy-start | bytes 1179652
  2185.3 51.8 %copy-start.72 = (f32[3,48]{1,0:T(4,128)S(1)}, f32[3,48]{1,0:T(4,128)}, u32[]{:S(2)}) copy-start(f32[3,48]{1,0:T(4,128)} %param.56) | copy-start | bytes 1732
  2185.3 51.8 %copy-start.73 = (f32[3,48]{1,0:T(4,128)S(1)}, f32[3,48]{1,0:T(4,128)}, u32[]{:S(2)}) copy-start(f32[3,48]{1,0:T(4,128)} %param.57) | copy-start | bytes 1732
  2188.6 42.5 %copy-start.24 = (f32[144,768]{1,0:T(8,128)S(1)}, f32[144,768]{1,0:T(8,128)}, u32[]{:S(2)}) copy-start(f32[144,768]{1,0:T(8,128)} %param.40) | copy-start | bytes 1327108
  (61 other events, 235.1 us)
Sparse Core Ops, SparseCore 0:
  10.9 42.3 all-gather.11
  55.5 127.5 all-gather.13
  185.9 47.2 all-gather.15
  235.9 37.3 all-gather.17
  276.0 60.7 all-gather.19
  339.6 43.7 all-gather.21
  385.5 127.3 all-gather.23
  608.4 431.4 reduce-scatter.8
  1046.4 430.3 reduce-scatter.20
  1482.6 98.0 reduce-scatter.14
  1587.5 100.4 reduce-scatter.10
  1694.5 113.2 reduce-scatter.18
  1813.5 118.2 reduce-scatter.12
  1938.7 154.7 reduce-scatter.16
  2094.9 44.0 all-gather.25
  2140.3 44.9 all-gather.27
where the time goes:
time: 2270 us; the launch traced here: 2260 us
  waiting for transfers between devices  1790 us (79%)
  blocking collectives  176 us (8%)
  matrix products  133 us (6%)
  other arithmetic  90.5 us (4%)
  local copies, waits for them, and re-layouts  40.9 us (2%)
  between operations  25.2 us (1%)
    reduce_scatter x1, waiting for transfers between devices, local(): lax.psum_scatter(grad_head, ('fsdp', 'rep'), scatter_dimension=0, tiled=T...  437 us
    reduce_scatter x1, waiting for transfers between devices, local(): lax.psum_scatter(grad_codes, ('fsdp', 'rep'), scatter_dimension=0, tiled=...  358 us
    reduce_scatter x1, waiting for transfers between devices, local(): lax.psum_scatter(grad_gate_up, ('fsdp', 'rep'), scatter_dimension=0, tile...  154 us
    all_gather x1, waiting for transfers between devices, local(): lax.all_gather(head_weight.astype(jnp.bfloat16), 'fsdp', axis=0, tiled=True)  124 us
    reduce_scatter x1, waiting for transfers between devices, local(): lax.psum_scatter(grad_qkv, ('fsdp', 'rep'), scatter_dimension=0, tiled=True)  117 us
    reduce_scatter x1, waiting for transfers between devices, local(): lax.psum_scatter(grad_down, ('fsdp', 'rep'), scatter_dimension=0, tiled=T...  114 us
    reduce_scatter x1, waiting for transfers between devices, local(): lax.psum_scatter(grad_classes, ('fsdp', 'rep'), scatter_dimension=1, tile...  102 us
    all_gather x1, waiting for transfers between devices, local(): lax.all_gather(code_table.astype(jnp.bfloat16), 'fsdp', axis=0, tiled=True)  92.3 us
  transfers between devices with their start and end apart: 16, of which 15 were waited for; matrix products, arithmetic and copies ran while one was open for 6% of the time, Pallas kernels for 0%

commit v1 on v0

v1 whole, which is shorter than its diff:
```python
import jax
import jax.numpy as jnp
from jax import lax
from jax.sharding import PartitionSpec as P

HEAD_DIM = 64
CLIP_INV = 500
STEP = 10
NORM_EPS = 1e-05
BETA_ONE = 0.5
BETA_TWO = 0.5
ADAM_EPS = 1e-08
BF = jnp.bfloat16
F32 = jnp.float32


def rotary_tables(length, width):
    half = width // 2
    freq = 10000.0 ** (-jnp.arange(half, dtype=F32) * 2.0 / width)
    angles = jnp.arange(length, dtype=F32)[:, None] * freq[None, :]
    cosine = jnp.concatenate([jnp.cos(angles), jnp.cos(angles)], -1)
    sine = jnp.concatenate([jnp.sin(angles), jnp.sin(angles)], -1)
    return (cosine, sine)


def rotate(values, cosine, sine):
    half = values.shape[-1] // 2
    swapped = jnp.concatenate([-values[..., half:], values[..., :half]], -1)
    return values * cosine[:, None, :] + swapped * sine[:, None, :]


def rotate_back(grads, cosine, sine):
    half = grads.shape[-1] // 2
    scaled = grads * sine[:, None, :]
    return grads * cosine[:, None, :] + jnp.concatenate(
        [scaled[..., half:], -scaled[..., :half]], -1
    )


def norm_forward(stream, gain):
    inverse = lax.rsqrt(jnp.mean(stream * stream, -1, keepdims=True) + NORM_EPS)
    return (stream * inverse * gain, inverse)


def norm_backward(stream, inverse, gain, grad_out):
    weighted = grad_out * gain
    inner = jnp.mean(weighted * stream, -1, keepdims=True)
    grad_in = inverse * weighted - stream * inverse * inverse * inverse * inner
    grad_gain = jnp.sum(grad_out * stream * inverse, axis=(0, 1))
    return (grad_in, grad_gain)


def attention_scores(queries, keys_rot):
    length = queries.shape[1]
    scores = jnp.einsum(
        "bqhd,bkhd->bhqk", queries, keys_rot, preferred_element_type=F32
    ) * HEAD_DIM ** (-0.5)
    causal = jnp.arange(length)[:, None] >= jnp.arange(length)[None, :]
    return jnp.where(causal, scores, -1e30)


def column_blocks(width, total):
    return [(at, min(width, total - at)) for at in range(0, total, width)]


def pack_rows(qkv, gate, out, down):
    width = qkv.shape[-1]
    parts = [qkv, gate, out]
    for at, size in column_blocks(width, down.shape[-1]):
        block = down[..., at : at + size]
        if size < width:
            pad = [(0, 0)] * (block.ndim - 1) + [(0, width - size)]
            block = jnp.pad(block, pad)
        parts.append(block)
    return jnp.concatenate(parts, -2)


def unpack_rows(packed, rows, hidden_width):
    width = packed.shape[-1]
    at, parts = 0, []
    for count in rows[:3]:
        parts.append(packed[..., at : at + count, :])
        at += count
    blocks = []
    for _, size in column_blocks(width, hidden_width):
        blocks.append(packed[..., at : at + rows[3], :size])
        at += rows[3]
    parts.append(jnp.concatenate(blocks, -1))
    return parts


def adam_update(weight, first, second, grad, rate, decay):
    first_new = BETA_ONE * first + (1.0 - BETA_ONE) * grad
    second_new = BETA_TWO * second + (1.0 - BETA_TWO) * grad * grad
    first_hat = first_new / (1.0 - BETA_ONE**STEP)
    second_hat = second_new / (1.0 - BETA_TWO**STEP)
    weight_new = weight - rate * (first_hat / (jnp.sqrt(second_hat) + ADAM_EPS) + decay * weight)
    return (weight_new, first_new, second_new)


def dot(subscripts, left, right):
    return jnp.einsum(subscripts, left, right, preferred_element_type=F32)


def local(*args):
    class_ids, null_mask, code_ids, lengths = args[:4]
    masters, firsts, seconds = args[4::3], args[5::3], args[6::3]
    code_table, class_table, qkv_weight, out_weight, gate_up, down_weight, head_weight, gains = (
        masters
    )
    rates = (0.5, 0.5, 0.05, 0.05, 0.05, 0.05, 0.05, 0.5)
    decays = (0.1, 0.1, 0.1, 0.1, 0.1, 0.1, 0.1, 0.0)
    n = lax.axis_size("fsdp")
    me = lax.axis_index("fsdp")
    batch, length = code_ids.shape
    width = qkv_weight.shape[1]
    hidden_width = down_weight.shape[1]
    table_rows, own_width = class_table.shape
    own_rows = code_table.shape[0]
    heads = width // HEAD_DIM
    rows = (qkv_weight.shape[0], gate_up.shape[0], out_weight.shape[0], down_weight.shape[0])

    classes = jnp.where(null_mask == 1, table_rows - 1, class_ids)
    facts = jnp.concatenate([code_ids, classes[:, None], lengths[:, None]], 1)
    facts = lax.all_gather(facts, "fsdp", axis=0, tiled=True)
    all_codes, all_classes, all_lengths = facts[:, :length], facts[:, length], facts[:, length + 1]
    images = n * batch
    tokens = images * length
    all_counted = (jnp.arange(length)[None, :] < all_lengths[:, None]).astype(F32)
    token_count = lax.psum(jnp.sum(all_counted), "rep")
    counted = (jnp.arange(length)[None, :] < lengths[:, None]).astype(F32)

    packed = pack_rows(
        qkv_weight.astype(BF), gate_up.astype(BF), out_weight.astype(BF), down_weight.astype(BF)
    )
    packed = lax.all_gather(packed, "fsdp", axis=0)
    parts = unpack_rows(packed, rows, hidden_width)
    qkv_w, gate_w, out_w, down_w = (p.reshape(-1, p.shape[-1]) for p in parts)
    gains32 = lax.all_gather(gains.astype(BF), "fsdp", axis=1, tiled=True).astype(F32)

    own_ids = jnp.arange(own_rows) + me * own_rows
    previous = jnp.concatenate(
        [jnp.full((images, 1), -1, all_codes.dtype), all_codes[:, :-1]], 1
    ).reshape(tokens)
    lookup = (previous[:, None] == own_ids[None, :]).astype(BF)
    rows_found = dot("tv,vd->td", lookup, code_table.astype(BF)).astype(BF)
    rows_found = rows_found.reshape(images, length, width)
    class_found = class_table.astype(BF)[all_classes]
    class_rows = lax.dynamic_update_slice(
        jnp.zeros((images, width), BF), class_found, (0, me * own_width)
    )
    first_spot = (jnp.arange(length) == 0)[None, :, None]
    rows_found = jnp.where(first_spot, class_rows[:, None, :], rows_found)
    stream0 = lax.psum_scatter(rows_found, "fsdp", scatter_dimension=0, tiled=True).astype(F32)

    normed1, inverse1 = norm_forward(stream0, gains32[0])
    normed1 = normed1.astype(BF)
    mixed = dot("btd,ed->bte", normed1, qkv_w)
    cosine, sine = rotary_tables(length, HEAD_DIM)
    split4 = (batch, length, heads, HEAD_DIM)
    queries = rotate(mixed[..., :width].reshape(split4), cosine, sine).astype(BF)
    keys_rot = rotate(mixed[..., width : 2 * width].reshape(split4), cosine, sine).astype(BF)
    values = mixed[..., 2 * width :].reshape(split4).astype(BF)
    scores = attention_scores(queries, keys_rot)
    top = jnp.max(scores, -1, keepdims=True)
    expo = jnp.exp(scores - top)
    probs32 = expo / jnp.sum(expo, -1, keepdims=True)
    probs = probs32.astype(BF)
    attended = dot("bhqk,bkhd->bqhd", probs, values).astype(BF).reshape(batch, length, width)
    stream1 = stream0 + dot("btd,ed->bte", attended, out_w)
    normed2, inverse2 = norm_forward(stream1, gains32[1])
    normed2 = normed2.astype(BF)
    gated = dot("btd,fd->btf", normed2, gate_w)
    gate_part = gated[..., :hidden_width]
    up_part = gated[..., hidden_width:]
    hidden = (jax.nn.silu(gate_part) * up_part).astype(BF)
    stream2 = stream1 + dot("btf,df->btd", hidden, down_w)
    normed3, inverse3 = norm_forward(stream2, gains32[2])
    normed3 = normed3.astype(BF)

    head_b = head_weight.astype(BF)
    normed3_all = lax.all_gather(normed3, "fsdp", axis=0, tiled=True).reshape(tokens, width)
    logits = dot("td,vd->tv", normed3_all, head_b)
    onehot = all_codes.reshape(tokens)[:, None] == own_ids[None, :]
    local_top = jnp.max(logits, -1)
    local_sum = jnp.sum(jnp.exp(logits - local_top[:, None]), -1)
    local_pick = jnp.sum(jnp.where(onehot, logits, 0.0), -1)
    stats = lax.all_gather(jnp.stack([local_top, local_sum, local_pick]), "fsdp", axis=0)
    ltop = jnp.max(stats[:, 0], 0)
    lse = jnp.log(jnp.sum(stats[:, 1] * jnp.exp(stats[:, 0] - ltop[None]), 0)) + ltop
    picked = jnp.sum(stats[:, 2], 0)
    loss_sum = lax.psum(jnp.sum(jnp.where(all_counted.reshape(tokens) > 0, lse - picked, 0.0)), "rep")
    weight_t = all_counted.reshape(tokens) * (1.0 / token_count)
    soft = jnp.exp(logits - lse[:, None])
    grad_logits = ((soft - onehot.astype(F32)) * weight_t[:, None]).astype(BF)
    grad_normed3 = dot("tv,vd->td", grad_logits, head_b).astype(BF).reshape(images, length, width)
    grad_normed3 = lax.psum_scatter(grad_normed3, "fsdp", scatter_dimension=0, tiled=True)
    grad_normed3 = grad_normed3.astype(F32)
    grad_head = dot("tv,td->vd", grad_logits, normed3_all)

    grad_stream2, gain_three = norm_backward(stream2, inverse3, gains32[2], grad_normed3)
    grad_branch = grad_stream2.astype(BF)
    grad_down = dot("btd,btf->df", grad_branch, hidden)
    grad_hidden = dot("btd,df->btf", grad_branch, down_w)
    sigma = jax.nn.sigmoid(gate_part)
    grad_gate = grad_hidden * up_part * sigma * (1.0 + gate_part * (1.0 - sigma))
    grad_up = grad_hidden * gate_part * sigma
    grad_gated = jnp.concatenate([grad_gate, grad_up], -1).astype(BF)
    grad_gate_up = dot("btf,btd->fd", grad_gated, normed2)
    grad_normed2 = dot("btf,fd->btd", grad_gated, gate_w)
    grad_middle, gain_two = norm_backward(stream1, inverse2, gains32[1], grad_normed2)
    grad_stream1 = grad_stream2 + grad_middle
    grad_attn = grad_stream1.astype(BF)
    grad_out = dot("bte,btd->ed", grad_attn, attended)
    grad_attended = dot("bte,ed->btd", grad_attn, out_w).astype(BF).reshape(split4)
    grad_probs = dot("bqhd,bkhd->bhqk", grad_attended, values)
    grad_values = dot("bhqk,bqhd->bkhd", probs, grad_attended)
    grad_scores = probs32 * (grad_probs - jnp.sum(probs32 * grad_probs, -1, keepdims=True))
    grad_scores = grad_scores.astype(BF)
    scale = HEAD_DIM ** (-0.5)
    grad_queries = dot("bhqk,bkhd->bqhd", grad_scores, keys_rot) * scale
    grad_keys = dot("bhqk,bqhd->bkhd", grad_scores, queries) * scale
    grad_mixed = jnp.concatenate(
        [
            rotate_back(grad_queries, cosine, sine).reshape(batch, length, width),
            rotate_back(grad_keys, cosine, sine).reshape(batch, length, width),
            grad_values.reshape(batch, length, width),
        ],
        -1,
    ).astype(BF)
    grad_qkv = dot("bte,btd->ed", grad_mixed, normed1)
    grad_normed1 = dot("bte,ed->btd", grad_mixed, qkv_w)
    grad_first, gain_one = norm_backward(stream0, inverse1, gains32[0], grad_normed1)
    grad_stream0 = grad_stream1 + grad_first

    blocks = [
        g.astype(BF).reshape(n, -1, g.shape[-1]) for g in (grad_qkv, grad_gate_up, grad_out, grad_down)
    ]
    layer_part = lax.psum_scatter(pack_rows(*blocks), "fsdp", scatter_dimension=0, tiled=False)
    rows_all = lax.all_gather(grad_stream0.astype(BF), "fsdp", axis=0, tiled=True)
    grad_codes = dot("tv,td->vd", lookup, rows_all.reshape(tokens, width))
    class_part = lax.dynamic_slice(rows_all[:, 0], (0, me * own_width), (images, own_width))
    class_spot = (all_classes[:, None] == jnp.arange(table_rows)[None, :]).astype(BF)
    grad_classes = dot("iv,id->vd", class_spot, class_part)
    summed = lax.psum(
        (grad_codes.astype(BF), grad_head.astype(BF), layer_part, grad_classes), "rep"
    )
    grad_codes, grad_head, layer_part, grad_classes = (s.astype(F32) for s in summed)
    grad_gains = lax.psum(jnp.stack([gain_one, gain_two, gain_three]), ("fsdp", "rep"))
    grad_gains = lax.dynamic_slice(grad_gains, (0, me * own_width), (3, own_width))
    grad_qkv, grad_gate_up, grad_out, grad_down = unpack_rows(layer_part, rows, hidden_width)
    reduced = (
        grad_codes, grad_classes, grad_qkv, grad_out, grad_gate_up, grad_down, grad_head, grad_gains
    )
    squares = jnp.zeros((), F32)
    for grad_piece in reduced:
        squares = squares + jnp.sum(grad_piece * grad_piece)
    grad_norm = jnp.sqrt(lax.psum(squares, "fsdp"))
    factor = jnp.minimum(1.0, 1.0 / CLIP_INV / (grad_norm + 1e-06))
    results = [loss_sum, token_count, grad_norm]
    for index in range(8):
        results.extend(
            adam_update(
                masters[index],
                firsts[index],
                seconds[index],
                reduced[index] * factor,
                rates[index],
                decays[index],
            )
        )
    return tuple(results)


def solution(mesh):
    split = P(("fsdp", "rep"))
    by_row, by_column = P("fsdp", None), P(None, "fsdp")
    weights = (by_row,) * 3 + (by_column,) * 3 + (by_row,) * 15 + (by_column,) * 3
    return jax.shard_map(
        local,
        mesh=mesh,
        in_specs=(split, split, P(("fsdp", "rep"), None), split) + weights,
        out_specs=(P(), P(), P()) + weights,
        check_vma=False,
    )
```

time: 2270 us -> 951 us (0.42)
  waiting for transfers between devices: 1790 us -> 581 us
  matrix products: 133 us -> 84.6 us
  blocking collectives: 176 us -> 142 us
  other arithmetic: 90.5 us -> 62.9 us
    reduce_scatter x7 -> x3, waiting for transfers between devices: 1340 us -> 284 us  [the longest x1 139 us: local(): lax.psum_scatter(pack_rows(*blocks), 'fsdp', scatter_dimension=0, tiled=F...]
    all_gather x9 -> x3, waiting for transfers between devices: 457 us -> 205 us  [the longest x1 114 us: local(): packed = lax.all_gather(packed, 'fsdp', axis=0)]
    psum x0 -> x2, waiting for transfers between devices: none -> 91.7 us  [local(): lax.psum((grad_codes.astype(BF), grad_head.astype(BF), layer_part, grad_c...]
    dot_general x21 -> x23, matrix products: 133 us -> 80.5 us  [dot(): return jnp.einsum(subscripts, left, right, preferred_element_type=F32)]
    psum x2, blocking collectives: 81.6 us -> 45.4 us  [the longest x1 39.9 us: local(): lax.psum(jnp.stack([gain_one, gain_two, gain_three]), ('fsdp', 'rep'))]
    all_gather x7 -> x3, blocking collectives: 60.3 us -> 63 us  [the longest x1 23.1 us: local(): facts = lax.all_gather(facts, 'fsdp', axis=0, tiled=True)]
  transfers between devices with their start and end apart: 16 -> 8, of which waited for: 15 -> 7; matrix products, arithmetic and copies ran while one was open for 6% -> 5% of each run, Pallas kernels for 0% -> 0%
where the time goes in v1:
time: 951 us; the launch traced here: 946 us
  waiting for transfers between devices  581 us (61%)
  blocking collectives  142 us (15%)
  matrix products  84.6 us (9%)
  other arithmetic  62.9 us (7%)
  local copies, waits for them, and re-layouts  48.7 us (5%)
  between operations  25.2 us (3%)
    reduce_scatter x1, waiting for transfers between devices, local(): lax.psum_scatter(pack_rows(*blocks), 'fsdp', scatter_dimension=0, tiled=F...  139 us
    all_gather x1, waiting for transfers between devices, local(): packed = lax.all_gather(packed, 'fsdp', axis=0)  114 us
    psum x2, waiting for transfers between devices, local(): lax.psum((grad_codes.astype(BF), grad_head.astype(BF), layer_part, grad_c...  91.7 us
    reduce_scatter x1, waiting for transfers between devices, local(): lax.psum_scatter(grad_normed3, 'fsdp', scatter_dimension=0, tiled=True)  83.3 us
    dot_general x23, matrix products, dot(): return jnp.einsum(subscripts, left, right, preferred_element_type=F32)  80.5 us
    reduce_scatter x1, waiting for transfers between devices, local(): lax.psum_scatter(rows_found, 'fsdp', scatter_dimension=0, tiled=True)  62 us
    all_gather x1, waiting for transfers between devices, local(): lax.all_gather(normed3, 'fsdp', axis=0, tiled=True).reshape(tokens, width)  58.8 us
    psum x1, blocking collectives, local(): lax.psum(jnp.stack([gain_one, gain_two, gain_three]), ('fsdp', 'rep'))  39.9 us
  transfers between devices with their start and end apart: 8, of which 7 were waited for; matrix products, arithmetic and copies ran while one was open for 5% of the time, Pallas kernels for 0%

profile of v1, /device:TPU:0, one launch (start us, length us, event | category | flops | bytes accessed | tf_op | source)
XLA Modules:
  0.0 945.6 jit_solution(13565036090508866987)
XLA Ops:
  10.0 23.1 %all-gather.2 = s32[16,1,258]{2,1,0:T(1,128)S(1)} all-gather(s32[1,1,258]{2,1,0:T(1,128)S(1)} %add_bitcast_fusion), channel_id=1, replica_groups=mesh['fsdp'=16,'rep'=2] {'fsdp'}, dimensions={0}, use_global_device_ids=true | all-gather | bytes 17544 | tf_op jit(solution)/shard_map/all_gather | solution.py:125
  35.8 10.8 %fusion.13 = bf16[4096,768]{1,0:T(8,128)(2,1)S(1)} fusion(s32[4096]{0:T(1024)S(1)} %bitcast.235, s32[1024]{0:T(1024)S(1)} %iota_add_fusion, f32[1024,768]{1,0:T(8,128)} %param.32), kind=kOutput, calls=%fused_computation.18 | convolution fusion | flops 6450577408 | bytes 9457664 | tf_op jit(solution)/shard_map/tv,vd->td/dot_general | solution.py:102
  46.6 3.1 broadcast_select_fusion
  52.2 17.8 %all-gather.3 = bf16[16,48,3]{1,2,0:T(4,128)(2,1)S(1)} all-gather(bf16[1,48,3]{1,2,0:T(4,128)(2,1)S(1)} %convert_bitcast_fusion), channel_id=1, replica_groups=mesh['fsdp'=16,'rep'=2] {'fsdp'}, dimensions={0}, use_global_device_ids=true | all-gather | bytes 4896 | tf_op jit(solution)/shard_map/all_gather | solution.py:139
  70.4 62.0 %reduce-scatter.4.cloned.1.call-done = bf16[1,256,768]{2,1,0:T(8,128)(2,1)} async-done(((bf16[16,256,768]{2,1,0:T(8,128)(2,1)}), bf16[1,256,768]{2,1,0:T(8,128)(2,1)}) %reduce-scatter.4.cloned.1.call-update) | async-done | bytes 393232 | tf_op jit(solution)/shard_map/reduce_scatter | solution.py:154
  133.6 114.2 %all-gather.13.cloned.1.call-done = bf16[9472,768]{1,0:T(8,128)(2,1)} async-done(((bf16[592,768]{1,0:T(8,128)(2,1)}), bf16[9472,768]{1,0:T(8,128)(2,1)}) %all-gather.13.cloned.1.call-update) | async-done | bytes 14549008 | tf_op jit(solution)/shard_map/all_gather | solution.py:136
  252.1 4.9 fusion.116
  257.0 6.4 slice.193
  269.7 4.1 fusion.122
  287.1 58.8 %all-gather.9.cloned.1.call-done = bf16[16,256,768]{2,1,0:T(8,128)(2,1)} async-done(((bf16[1,256,768]{2,1,0:T(8,128)(2,1)}), bf16[16,256,768]{2,1,0:T(8,128)(2,1)}) %all-gather.9.cloned.1.call-update) | async-done | bytes 6291472 | tf_op jit(solution)/shard_map/all_gather | solution.py:182
  345.9 9.8 %fusion.123 = (f32[4096]{0:T(1024)S(1)}, f32[4096,1024]{0,1:T(8,128)S(1)}) fusion(bf16[4096,768]{1,0:T(8,128)(2,1)} %bitcast.238, f32[1024,768]{1,0:T(8,128)} %param.50), kind=kOutput, calls=%fused_computation.257 | convolution fusion | flops 6447427584 | bytes 26230784 | tf_op jit(solution)/shard_map/td,vd->tv/dot_general | solution.py:102
  355.8 4.5 exponential_reduce_fusion
  361.5 22.1 %all-gather.4 = f32[16,3,4096]{2,1,0:T(4,128)S(1)} all-gather(f32[1,3,4096]{2,1,0:T(4,128)S(1)} %maximum_bitcast_fusion), channel_id=3, replica_groups=mesh['fsdp'=16,'rep'=2] {'fsdp'}, dimensions={0}, use_global_device_ids=true | all-gather | bytes 835584 | tf_op jit(solution)/shard_map/all_gather | solution.py:188
  385.2 5.6 all-reduce.3
  391.6 8.2 fusion.8
  399.8 9.0 convolution_convert_fusion.1
  409.1 83.3 %reduce-scatter.6.cloned.1.call-done = bf16[1,256,768]{2,1,0:T(8,128)(2,1)} async-done(((bf16[16,256,768]{2,1,0:T(8,128)(2,1)}), bf16[1,256,768]{2,1,0:T(8,128)(2,1)}) %reduce-scatter.6.cloned.1.call-update) | async-done | bytes 393232 | tf_op jit(solution)/shard_map/reduce_scatter | solution.py:197
  493.7 5.0 fusion.33
  504.5 2.6 convolution_convert_fusion.6
  524.1 3.0 constant_dynamic-update-slice_fusion.1
  532.3 11.8 %convolution_convert_fusion.4 = bf16[1024,768]{1,0:T(8,128)(2,1)} fusion(bf16[4096,1024]{0,1:T(8,128)(2,1)} %copy-done.9, bf16[4096,768]{1,0:T(8,128)(2,1)} %bitcast.239), kind=kOutput, calls=%fused_computation.52 | convolution fusion | flops 6443237376 | bytes 16252928 | tf_op jit(solution)/shard_map/tv,td->vd/dot_general | solution.py:102
  544.2 32.0 %all-gather.11.cloned.1.call-done = bf16[16,256,768]{2,1,0:T(8,128)(2,1)} async-done(((bf16[1,256,768]{2,1,0:T(8,128)(2,1)}), bf16[16,256,768]{2,1,0:T(8,128)(2,1)}) %all-gather.11.cloned.1.call-update) | async-done | bytes 6291472 | tf_op jit(solution)/shard_map/all_gather | solution.py:240
  578.2 10.8 %fusion.21 = bf16[1024,768]{1,0:T(8,128)(2,1)} fusion(bf16[4096,768]{1,0:T(8,128)(2,1)} %bitcast.237, s32[4096]{0:T(1024)S(1)} %bitcast.236, s32[1024]{0:T(1024)S(1)} %iota_add_fusion), kind=kOutput, calls=%fused_computation.51 | convolution fusion | flops 6447431680 | bytes 7884800 | tf_op jit(solution)/shard_map/tv,td->vd/dot_general | solution.py:102
  589.0 138.7 %reduce-scatter.8.cloned.1.call-done = bf16[1,592,768]{2,1,0:T(8,128)(2,1)} async-done(((bf16[16,592,768]{2,1,0:T(8,128)(2,1)}), bf16[1,592,768]{2,1,0:T(8,128)(2,1)}) %reduce-scatter.8.cloned.1.call-update) | async-done | bytes 909328 | tf_op jit(solution)/shard_map/reduce_scatter | solution.py:239
  727.8 39.9 %psum.62 = f32[3,768]{1,0:T(4,128)S(1)} all-reduce(f32[3,768]{1,0:T(4,128)S(1)} %pad_maximum_fusion.10), channel_id=1, replica_groups=mesh['fsdp'=16,'rep'=2] {'fsdp','rep'}, use_global_device_ids=true, to_apply=%region_36.37 | all-reduce | flops 2304 | bytes 18432 | tf_op jit(solution)/shard_map/psum | solution.py:249
  769.9 91.7 %all-reduce.10.cloned.1.call-done = (bf16[1024,768]{1,0:T(8,128)(2,1)}, bf16[592,768]{1,0:T(8,128)(2,1)}, bf16[1024,768]{1,0:T(8,128)(2,1)}) async-done(((bf16[1024,768]{1,0:T(8,128)(2,1)}, bf16[592,768]{1,0:T(8,128)(2,1)}, bf16[1024,768]{1,0:T(8,128)(2,1)}), (bf16[1024,768]{1,0:T(8,128)(2,1)}, bf16[592,768]{1,0:T(8,128)(2,1)}, bf16[1024,768]{1,0:T(8,128)(2,1)})) %all-reduce.10.cloned.1.call-update) | async-done | bytes 4055056 | tf_op jit(solution)/shard_map/psum | solution.py:245
  878.1 33.7 %psum.63 = f32[]{:T(128)} all-reduce(f32[]{:T(128)S(6)} %add.284), channel_id=1, replica_groups=mesh['fsdp'=16,'rep'=2] {'fsdp'}, use_global_device_ids=true, to_apply=%region_38.39 | all-reduce | flops 1 | bytes 8 | tf_op jit(solution)/shard_map/psum | solution.py:258
  916.0 2.6 multiply_subtract_fusion.4
  918.6 2.6 multiply_subtract_fusion.3
  921.2 3.4 multiply_subtract_fusion.2
  924.6 5.5 multiply_subtract_fusion
  931.6 4.8 multiply_subtract_fusion.1
  (255 shorter events, 84.6 us)
Async XLA Ops:
  7.2 125.2 %reduce-scatter.4.cloned.1.call-start = ((), (), s32[]{:S(2)}) async-start(), calls=%async_computation.3 | async-start | bytes 6684672 | tf_op jit(solution)/shard_map/reduce_scatter | solution.py:154
  49.7 198.1 %all-gather.13.cloned.1.call-start = ((), (), s32[]{:S(2)}) async-start(), calls=%async_computation.9 | async-start | bytes 15458304 | tf_op jit(solution)/shard_map/all_gather | solution.py:136
  52.1 293.8 %all-gather.9.cloned.1.call-start = ((), (), s32[]{:S(2)}) async-start(), calls=%async_computation.4 | async-start | bytes 6684672 | tf_op jit(solution)/shard_map/all_gather | solution.py:182
  252.1 11.3 %copy-start.2 = (bf16[16,144,768]{2,1,0:T(8,128)(2,1)}, bf16[16,144,768]{2,1,0:T(8,128)(2,1)S(1)}, u32[]{:S(2)}) copy-start(bf16[16,144,768]{2,1,0:T(8,128)(2,1)S(1)} %slice.183) | copy-start | bytes 10616836
  257.0 19.3 %copy-start.4 = (bf16[16,48,768]{2,1,0:T(8,128)(2,1)}, bf16[16,48,768]{2,1,0:T(8,128)(2,1)S(1)}, u32[]{:S(2)}) copy-start(bf16[16,48,768]{2,1,0:T(8,128)(2,1)S(1)} %get-tuple-element.76) | copy-start | bytes 3538948
  257.0 6.4 copy-start.13
  269.7 7.3 slice-start
  277.0 6.2 copy-start.6
  285.8 206.6 %reduce-scatter.6.cloned.1.call-start = ((), (), s32[]{:S(2)}) async-start(), calls=%async_computation.5 | async-start | bytes 6684672 | tf_op jit(solution)/shard_map/reduce_scatter | solution.py:197
  355.7 5.7 copy-start
  391.6 8.3 copy-start.25
  399.8 9.0 copy-start.9
  408.9 89.9 %slice-start.2 = ((s8[6291456]{0:T(1024)(128)(4,1)}), s8[2097152]{0:T(1024)(128)(4,1)S(1)}, s32[]{:S(2)}) async-start(s8[6291456]{0:T(1024)(128)(4,1)} %bitcast.189), calls=%async_computation.13 | async-start | bytes 4194304
  408.9 167.3 %all-gather.11.cloned.1.call-start = ((), (), s32[]{:S(2)}) async-start(), calls=%async_computation.6 | async-start | bytes 6684672 | tf_op jit(solution)/shard_map/all_gather | solution.py:240
  493.6 5.1 slice-start.3
  493.7 5.1 copy-start.7
  515.0 212.7 %reduce-scatter.8.cloned.1.call-start = ((), (), s32[]{:S(2)}) async-start(), calls=%async_computation.8 | async-start | bytes 15458304 | tf_op jit(solution)/shard_map/reduce_scatter | solution.py:239
  532.3 44.9 %copy-start.52 = (s32[16]{0:T(128)S(1)}, s32[16]{0:T(128)}, u32[]{:S(2)}) copy-start(s32[16]{0:T(128)} %get-tuple-element.37) | copy-start | bytes 196
  532.3 236.0 %all-reduce.8.cloned.1.call-start = ((), (), s32[]{:S(2)}) async-start(), calls=%async_computation.7 | async-start | bytes 393216 | tf_op jit(solution)/shard_map/psum | solution.py:245
  578.1 283.5 %all-reduce.10.cloned.1.call-start = ((), (), s32[]{:S(2)}) async-start(), calls=%async_computation.10 | async-start | bytes 8110080 | tf_op jit(solution)/shard_map/psum | solution.py:245
  861.7 6.8 copy-start.11
  863.2 6.6 copy-start.10
  866.3 46.2 %copy-start.51 = (f32[3,48]{1,0:T(4,128)S(1)}, f32[3,48]{1,0:T(4,128)}, u32[]{:S(2)}) copy-start(f32[3,48]{1,0:T(4,128)} %param.53) | copy-start | bytes 1732
  912.5 6.1 copy-start.33
  914.0 10.6 %copy-start.28 = (f32[1024,768]{1,0:T(8,128)S(1)}, f32[1024,768]{1,0:T(8,128)}, u32[]{:S(2)}) copy-start(f32[1024,768]{1,0:T(8,128)} %param.52) | copy-start | bytes 9437188
  916.0 5.2 copy-start.24
  918.6 6.0 copy-start.27
  924.6 5.5 copy-start.29
  924.6 5.5 copy-start.30
  924.6 7.0 copy-start.31
  931.6 4.8 copy-start.48
  931.6 4.8 copy-start.49
  (39 other events, 100.1 us)
Sparse Core Ops, SparseCore 0:
  49.8 82.5 reduce-scatter.3
  135.5 112.2 all-gather.12
  285.9 60.0 all-gather.8
  409.0 83.3 reduce-scatter.5
  515.1 60.9 all-gather.10
  580.1 147.5 reduce-scatter.7
  730.7 21.4 all-reduce.7
  755.5 106.0 all-reduce.9

commit v2 on v1

--- a/solution.py
+++ b/solution.py
@@ -1,6 +1,10 @@
+import functools
+
 import jax
 import jax.numpy as jnp
 from jax import lax
+from jax.experimental import pallas as pl
+from jax.experimental.pallas import tpu as pltpu
 from jax.sharding import PartitionSpec as P
 
 HEAD_DIM = 64
@@ -12,6 +16,7 @@
 ADAM_EPS = 1e-08
 BF = jnp.bfloat16
 F32 = jnp.float32
+MESH = pl.DeviceIdType.MESH
 
 
 def rotary_tables(length, width):
@@ -89,6 +94,233 @@
     return parts
 
 
+def geometry(n):
+    chips = n // 2
+    y_size = 1 << ((chips.bit_length() - 1) // 2)
+    return chips // y_size, y_size
+
+
+def where_am_i(z_size, y_size):
+    me = lax.axis_index("fsdp")
+    return me, me // (2 * y_size), (me // 2) % y_size, me % 2
+
+
+def front_kernel(z_size, y_size, reps, own_width, parts, facts, code_b, class_b, *refs):
+    count = len(parts)
+    weights, refs = refs[:count], refs[count:]
+    wholes, refs = refs[:count], refs[count:]
+    (stream, facts_all, turned, acc, core_out, core_in, y_in, z_in,
+     fact_sems, z_sems, y_sems, x_sems, c_sems, own_sems, rc_sems, ry_sems, rz_sems) = refs
+    n = z_size * y_size * 2
+    me, z, y, core = where_am_i(z_size, y_size)
+    x = lax.axis_index("rep")
+    length = stream.shape[0]
+    width = stream.shape[1]
+    own_rows = code_b.shape[0]
+
+    def at(dz, dy, other=0):
+        c = 1 - core if other else core
+        return (lax.rem(z + dz, z_size) * y_size + lax.rem(y + dy, y_size)) * 2 + c
+
+    barrier = pltpu.get_barrier_semaphore()
+    for k in range(1, n):
+        pl.semaphore_signal(barrier, inc=1, device_id=(lax.rem(me + k, n), x), device_id_type=MESH)
+    for k in range(1, reps):
+        pl.semaphore_signal(barrier, inc=1, device_id=(me, lax.rem(x + k, reps)), device_id_type=MESH)
+    pl.semaphore_wait(barrier, n - 1 + reps - 1)
+
+    def send(src, dst, sems, index, device):
+        copy = pltpu.make_async_remote_copy(
+            src_ref=src, dst_ref=dst, send_sem=sems.at[(0,) + index], recv_sem=sems.at[(1,) + index],
+            device_id=device, device_id_type=MESH,
+        )
+        copy.start()
+
+    def arrival(dst, sems, index):
+        pltpu.make_async_copy(dst, dst, sems.at[(1,) + index]).wait()
+
+    def departure(src, sems, index):
+        pltpu.make_async_copy(src, src, sems.at[(0,) + index]).wait()
+
+    for k in range(1, n):
+        send(facts, facts_all.at[me], fact_sems, (k,), (lax.rem(me + k, n), x))
+    facts_all[me] = facts[...]
+
+    peers_z = [(dz, at(dz, 0)) for dz in range(1, z_size)]
+    peers_y = [(dy, at(0, dy)) for dy in range(1, y_size)]
+    spots = [(dz, dy) for dz in range(z_size) for dy in range(y_size)]
+    for k, part in enumerate(parts):
+        pltpu.make_async_copy(weights[k], wholes[k].at[me], own_sems.at[k]).start()
+
+        @pl.when(x == part)
+        def _():
+            for dz, peer in peers_z:
+                send(weights[k], wholes[k].at[me], z_sems, (k, dz), (peer, x))
+            for dy, peer in peers_y:
+                send(weights[k], wholes[k].at[me], y_sems, (k, 0, dy), (peer, x))
+
+        send(weights[k], wholes[k].at[me], c_sems, (k, 0, 0), (at(0, 0, 1), x))
+
+    def to_others(k, dz, dy):
+        block = wholes[k].at[at(dz, dy)]
+        for dx in range(1, reps):
+            send(block, block, x_sems, (k, dz, dy, dx), (me, lax.rem(x + dx, reps)))
+        send(block, block, c_sems, (k, dz, dy), (at(0, 0, 1), x))
+
+    def after_z(dz):
+        for k, part in enumerate(parts):
+
+            @pl.when(x == part)
+            def _():
+                block = wholes[k].at[at(z_size - dz, 0)]
+                arrival(block, z_sems, (k, dz))
+                for dy, peer in peers_y:
+                    send(block, block, y_sems, (k, z_size - dz, dy), (peer, x))
+                to_others(k, z_size - dz, 0)
+
+    def after_y(dz, dy):
+        for k, part in enumerate(parts):
+
+            @pl.when(x == part)
+            def _():
+                arrival(wholes[k].at[at(dz, y_size - dy)], y_sems, (k, dz, dy))
+                to_others(k, dz, y_size - dy)
+
+    def after_x(dz, dy):
+        for k, part in enumerate(parts):
+
+            @pl.when(x != part)
+            def _():
+                block = wholes[k].at[at(dz, dy)]
+                arrival(block, x_sems, (k, dz, dy, lax.rem(x - part + reps, reps)))
+                send(block, block, c_sems, (k, dz, dy), (at(0, 0, 1), x))
+
+    for k in range(1, n):
+        arrival(facts_all.at[lax.rem(me - k + n, n)], fact_sems, (k,))
+    turned[...] = jnp.transpose(facts_all[...].reshape(n * 8, 128))
+    lane = lax.broadcasted_iota(jnp.int32, (128, n * 8), 1)
+    class_rows = class_b[...].astype(F32)
+    class_iota = lax.broadcasted_iota(jnp.int32, class_rows.shape, 0).astype(F32)
+    row_iota = lax.broadcasted_iota(jnp.int32, (length // 2, own_rows), 1) + me * own_rows
+    row_iota = row_iota.astype(F32)
+
+    def found(image, out):
+        cls = jnp.sum(jnp.where(lane[:1] == image * 8 + 4, turned[:1, :], 0.0), -1, keepdims=True)
+        row = jnp.sum(jnp.where(class_iota == cls, class_rows, 0.0), 0, keepdims=True)
+        row = jnp.concatenate([row, jnp.zeros((1, width - row.shape[1]), F32)], -1)
+        row = pltpu.roll(jnp.broadcast_to(row, (8, width)), me * own_width, 1)
+        for half in range(2):
+            ids = jnp.sum(jnp.where(lane == image * 8 + half, turned[...], 0.0), -1, keepdims=True)
+            spot = jnp.where(row_iota == ids, 1.0, 0.0).astype(BF)
+            rows = jnp.dot(spot, code_b[...], preferred_element_type=F32)
+            out[pl.ds(half * (length // 2), length // 2)] = rows.astype(BF)
+            if half == 0:
+                first = lax.broadcasted_iota(jnp.int32, (16, width), 0) == 0
+                head = jnp.where(first, jnp.concatenate([row, row], 0), rows[:16])
+                out[pl.ds(0, 16)] = head.astype(BF)
+
+    order = [(dz, dy) for dz in range(z_size - 1, -1, -1) for dy in range(y_size - 1, -1, -1)]
+    for dz, dy in order:
+        slot = dz * y_size + dy
+        found(at(dz, dy, 1), core_out.at[slot])
+        send(core_out.at[slot], core_in.at[slot], rc_sems, (slot,), (at(0, 0, 1), x))
+        found(at(dz, dy), acc.at[slot])
+    for dz, dy in order:
+        slot = dz * y_size + dy
+        arrival(core_in.at[slot], rc_sems, (slot,))
+        acc[slot] = (acc[slot].astype(F32) + core_in[slot].astype(F32)).astype(BF)
+        if dy:
+            send(acc.at[slot], y_in.at[dz, dy], ry_sems, (dz, dy), (at(0, dy), x))
+    for dz in range(1, z_size):
+        after_z(dz)
+    for dy in range(1, y_size):
+        after_y(0, dy)
+    for dz in range(z_size - 1, -1, -1):
+        slot = dz * y_size
+        total = acc[slot].astype(F32)
+        for dy in range(1, y_size):
+            arrival(y_in.at[dz, dy], ry_sems, (dz, dy))
+            total = total + y_in[dz, dy].astype(F32)
+        acc[slot] = total.astype(BF)
+        if dz:
+            send(acc.at[slot], z_in.at[dz], rz_sems, (dz,), (at(dz, 0), x))
+    for dz in range(z_size - 1, 0, -1):
+        for dy in range(1, y_size):
+            after_y(dz, dy)
+    total = acc[0].astype(F32)
+    for dz in range(1, z_size):
+        arrival(z_in.at[dz], rz_sems, (dz,))
+        total = total + z_in[dz].astype(F32)
+    stream[...] = total
+    for dz, dy in spots[1:]:
+        after_x(dz, dy)
+
+    for k in range(1, n):
+        departure(facts, fact_sems, (k,))
+    for dz, dy in spots:
+        slot = dz * y_size + dy
+        departure(core_out.at[slot], rc_sems, (slot,))
+        if dy:
+            departure(acc.at[slot], ry_sems, (dz, dy))
+        elif dz:
+            departure(acc.at[slot], rz_sems, (dz,))
+    for k, part in enumerate(parts):
+        pltpu.make_async_copy(weights[k], wholes[k].at[me], own_sems.at[k]).wait()
+        for dz, dy in spots:
+            arrival(wholes[k].at[at(dz, dy, 1)], c_sems, (k, dz, dy))
+            departure(weights[k], c_sems, (k, dz, dy))
+
+        @pl.when(x == part)
+        def _():
+            for dz in range(1, z_size):
+                departure(weights[k], z_sems, (k, dz))
+            for dz, dy in spots:
+                if dy:
+                    departure(weights[k], y_sems, (k, dz, dy))
+                if dz or dy:
+                    for dx in range(1, reps):
+                        departure(weights[k], x_sems, (k, dz, dy, dx))
+
+
+def front(facts, code_b, class_b, weights, parts, own_width, length, reps, n):
+    z_size, y_size = geometry(n)
+    width = code_b.shape[1]
+    count = len(weights)
+    spots = z_size * y_size
+    block = (length, width)
+    vmem, hbm = pl.BlockSpec(memory_space=pltpu.VMEM), pl.BlockSpec(memory_space=pl.ANY)
+    dma = pltpu.SemaphoreType.DMA
+    outs = pl.pallas_call(
+        functools.partial(front_kernel, z_size, y_size, reps, own_width, parts),
+        out_shape=[jax.ShapeDtypeStruct((n,) + w.shape, w.dtype) for w in weights]
+        + [jax.ShapeDtypeStruct(block, F32), jax.ShapeDtypeStruct((n, 8, 128), F32)],
+        in_specs=[vmem] * 3 + [hbm] * count,
+        out_specs=[hbm] * count + [vmem] * 2,
+        scratch_shapes=[
+            pltpu.VMEM((128, n * 8), F32),
+            pltpu.VMEM((spots,) + block, BF),
+            pltpu.VMEM((spots,) + block, BF),
+            pltpu.VMEM((spots,) + block, BF),
+            pltpu.VMEM((z_size, y_size) + block, BF),
+            pltpu.VMEM((z_size,) + block, BF),
+            dma((2, n)),
+            dma((2, count, z_size)),
+            dma((2, count, z_size, y_size)),
+            dma((2, count, z_size, y_size, reps)),
+            dma((2, count, z_size, y_size)),
+            dma((count,)),
+            dma((2, spots)),
+            dma((2, z_size, y_size)),
+            dma((2, z_size)),
+        ],
+        compiler_params=pltpu.CompilerParams(
+            collective_id=0, has_side_effects=True, vmem_limit_bytes=60 * 2**20
+        ),
+        name="front",
+    )(facts, code_b, class_b, *weights)
+    return outs[:count], outs[count], outs[count + 1]
+
+
 def adam_update(weight, first, second, grad, rate, decay):
     first_new = BETA_ONE * first + (1.0 - BETA_ONE) * grad
     second_new = BETA_TWO * second + (1.0 - BETA_TWO) * grad * grad
@@ -121,37 +353,46 @@
     rows = (qkv_weight.shape[0], gate_up.shape[0], out_weight.shape[0], down_weight.shape[0])
 
     classes = jnp.where(null_mask == 1, table_rows - 1, class_ids)
-    facts = jnp.concatenate([code_ids, classes[:, None], lengths[:, None]], 1)
-    facts = lax.all_gather(facts, "fsdp", axis=0, tiled=True)
-    all_codes, all_classes, all_lengths = facts[:, :length], facts[:, length], facts[:, length + 1]
+    previous = jnp.concatenate([jnp.full((1, 1), -1, code_ids.dtype), code_ids[:, :-1]], 1)
+    pair = jnp.stack([classes[0], lengths[0]])[None].astype(F32)
+    own_gains = gains.astype(BF).astype(F32)
+    facts = jnp.concatenate(
+        [
+            previous.astype(F32).reshape(2, -1),
+            code_ids.astype(F32).reshape(2, -1),
+            jnp.pad(pair, ((0, 0), (0, length // 2 - 2))),
+            jnp.pad(own_gains, ((0, 0), (0, length // 2 - own_width))),
+        ],
+        0,
+    )
+    class_b = jnp.pad(class_table.astype(BF), ((0, -table_rows % 16), (0, 128 - own_width)))
+    code_b = code_table.astype(BF)
+    reps = lax.axis_size("rep")
+    parts = tuple(k % reps for k in range(4))
+    wholes, stream0, facts = front(
+        facts,
+        code_b,
+        class_b,
+        [w.astype(BF) for w in (gate_up, qkv_weight, out_weight, down_weight)],
+        parts,
+        own_width,
+        length,
+        reps,
+        n,
+    )
+    gate_w, qkv_w, out_w, down_w = (w.reshape(-1, w.shape[-1]) for w in wholes)
+    stream0 = stream0[None]
     images = n * batch
     tokens = images * length
+    gains32 = facts[:, 5:8, :own_width].transpose(1, 0, 2).reshape(3, width)
+    all_codes = facts[:, 2:4].reshape(images, length).astype(jnp.int32)
+    previous = facts[:, 0:2].reshape(tokens).astype(jnp.int32)
+    all_classes = facts[:, 4, 0].astype(jnp.int32)
+    all_lengths = facts[:, 4, 1].astype(jnp.int32)
     all_counted = (jnp.arange(length)[None, :] < all_lengths[:, None]).astype(F32)
     token_count = lax.psum(jnp.sum(all_counted), "rep")
-    counted = (jnp.arange(length)[None, :] < lengths[:, None]).astype(F32)
-
-    packed = pack_rows(
-        qkv_weight.astype(BF), gate_up.astype(BF), out_weight.astype(BF), down_weight.astype(BF)
-    )
-    packed = lax.all_gather(packed, "fsdp", axis=0)
-    parts = unpack_rows(packed, rows, hidden_width)
-    qkv_w, gate_w, out_w, down_w = (p.reshape(-1, p.shape[-1]) for p in parts)
-    gains32 = lax.all_gather(gains.astype(BF), "fsdp", axis=1, tiled=True).astype(F32)
-
     own_ids = jnp.arange(own_rows) + me * own_rows
-    previous = jnp.concatenate(
-        [jnp.full((images, 1), -1, all_codes.dtype), all_codes[:, :-1]], 1
-    ).reshape(tokens)
     lookup = (previous[:, None] == own_ids[None, :]).astype(BF)
-    rows_found = dot("tv,vd->td", lookup, code_table.astype(BF)).astype(BF)
-    rows_found = rows_found.reshape(images, length, width)
-    class_found = class_table.astype(BF)[all_classes]
-    class_rows = lax.dynamic_update_slice(
-        jnp.zeros((images, width), BF), class_found, (0, me * own_width)
-    )
-    first_spot = (jnp.arange(length) == 0)[None, :, None]
-    rows_found = jnp.where(first_spot, class_rows[:, None, :], rows_found)
-    stream0 = lax.psum_scatter(rows_found, "fsdp", scatter_dimension=0, tiled=True).astype(F32)
 
     normed1, inverse1 = norm_forward(stream0, gains32[0])
     normed1 = normed1.astype(BF)

time: 951 us -> 849 us (0.89)
  waiting for transfers between devices: 581 us -> 412 us
  Pallas kernels: 0 us -> 115 us
  blocking collectives: 142 us -> 112 us
  local copies, waits for them, and re-layouts: 48.7 us -> 31 us
  matrix products: 84.6 us -> 73.4 us
    pallas_call x0 -> x1, Pallas kernels: none -> 115 us  [front(): pl.pallas_call(functools.partial(front_kernel, z_size, y_size, reps, own_...]
    all_gather x1 -> x0, waiting for transfers between devices: 114 us -> none  [local(): packed = lax.all_gather(packed, 'fsdp', axis=0)]
    reduce_scatter x1 -> x0, waiting for transfers between devices: 62 us -> none  [local(): lax.psum_scatter(rows_found, 'fsdp', scatter_dimension=0, tiled=True)]
    all_gather x2 -> x0, blocking collectives: 40.9 us -> none  [the longest x1 23.1 us: local(): facts = lax.all_gather(facts, 'fsdp', axis=0, tiled=True)]
    all_gather x1, blocking collectives: 22.1 us -> 32.6 us  [local(): lax.all_gather(jnp.stack([local_top, local_sum, local_pick]), 'fsdp', axi...]
    convert_element_type x3 -> x12, other arithmetic: 0.97 us -> 11.4 us  [the longest x4 6.9 us: local(): w.astype(BF)]
    dot_general x23 -> x22, matrix products: 80.5 us -> 70.4 us  [dot(): return jnp.einsum(subscripts, left, right, preferred_element_type=F32)]
    unnamed x139 -> x124, local copies, waits for them, and re-layouts: 21.7 us -> 21.6 us
  transfers between devices with their start and end apart: 8 -> 6, of which waited for: 7 -> 5; matrix products, arithmetic and copies ran while one was open for 5% -> 5% of each run, Pallas kernels for 0% -> 0%
where the time goes in v2:
time: 849 us; the launch traced here: 839 us
  waiting for transfers between devices  412 us (49%)
  Pallas kernels  115 us (14%)
  blocking collectives  112 us (13%)
  matrix products  73.4 us (9%)
  other arithmetic  70.1 us (8%)
  local copies, waits for them, and re-layouts  31 us (4%)
  between operations  25.4 us (3%)
    reduce_scatter x1, waiting for transfers between devices, local(): lax.psum_scatter(pack_rows(*blocks), 'fsdp', scatter_dimension=0, tiled=F...  139 us
    pallas_call x1, Pallas kernels, front(): pl.pallas_call(functools.partial(front_kernel, z_size, y_size, reps, own_...  115 us
    psum x2, waiting for transfers between devices, local(): lax.psum((grad_codes.astype(BF), grad_head.astype(BF), layer_part, grad_c...  91.1 us
    reduce_scatter x1, waiting for transfers between devices, local(): lax.psum_scatter(grad_normed3, 'fsdp', scatter_dimension=0, tiled=True)  83.3 us
    dot_general x22, matrix products, dot(): return jnp.einsum(subscripts, left, right, preferred_element_type=F32)  70.4 us
    all_gather x1, waiting for transfers between devices, local(): lax.all_gather(normed3, 'fsdp', axis=0, tiled=True).reshape(tokens, width)  66.4 us
    psum x1, blocking collectives, local(): lax.psum(jnp.stack([gain_one, gain_two, gain_three]), ('fsdp', 'rep'))  39.9 us
    psum x1, blocking collectives, local(): grad_norm = jnp.sqrt(lax.psum(squares, 'fsdp'))  33.7 us
  transfers between devices with their start and end apart: 6, of which 5 were waited for; matrix products, arithmetic and copies ran while one was open for 5% of the time, Pallas kernels for 0%

profile of v2, /device:TPU:0, one launch (start us, length us, event | category | flops | bytes accessed | tf_op | source)
XLA Modules:
  0.0 839.0 jit_solution(9186316288425228829)
XLA Ops:
  17.6 1.9 convert_element_type.233.refs_0_
  22.4 114.7 %front.1 = (bf16[16,256,768]{2,1,0:T(8,128)(2,1)}, bf16[16,144,768]{2,1,0:T(8,128)(2,1)}, bf16[16,48,768]{2,1,0:T(8,128)(2,1)}, bf16[16,48,2048]{2,1,0:T(8,128)(...) custom-call(f32[8,128]{1,0:T(8,128)} %fusion.68.facts, bf16[1024,768]{1,0:T(8,128)(2,1)} %convert_element_type.231.code_b, ...), custom_call_target="tpu_custom_call" | custom-call | tf_op jit(solution)/shard_map/front/pallas_call | solution.py:293
  139.4 3.4 convolution_bitcast_fusion.1
  146.7 2.9 fusion.92
  164.0 66.4 %all-gather.8.cloned.1.call-done = bf16[4096,768]{1,0:T(8,128)(2,1)} async-done(((bf16[256,768]{1,0:T(8,128)(2,1)}), bf16[4096,768]{1,0:T(8,128)(2,1)}) %all-gather.8.cloned.1.call-update) | async-done | bytes 6291472 | tf_op jit(solution)/shard_map/all_gather | solution.py:423
  230.4 9.8 %fusion.93 = (f32[4096]{0:T(1024)S(1)}, f32[4096,1024]{0,1:T(8,128)S(1)}) fusion(bf16[4096,768]{1,0:T(8,128)(2,1)} %all-gather.8.cloned.1.call-done, f32[1024,768]{1,0:T(8,128)} %param.50), kind=kOutput, calls=%fused_computation.224 | convolution fusion | flops 6447427584 | bytes 26230784 | tf_op jit(solution)/shard_map/td,vd->tv/dot_general | solution.py:334
  240.2 4.5 exponential_reduce_fusion
  245.9 32.6 %all-gather.2 = f32[16,3,4096]{2,1,0:T(4,128)S(1)} all-gather(f32[1,3,4096]{2,1,0:T(4,128)S(1)} %maximum_bitcast_fusion), channel_id=3, replica_groups=mesh['fsdp'=16,'rep'=2] {'fsdp'}, dimensions={0}, use_global_device_ids=true | all-gather | bytes 835584 | tf_op jit(solution)/shard_map/all_gather | solution.py:429
  280.1 5.6 all-reduce.4
  286.5 8.2 fusion.4
  294.7 9.0 %convolution_convert_fusion.1 = bf16[4096,768]{1,0:T(8,128)(2,1)} fusion(bf16[4096,1024]{0,1:T(8,128)(2,1)S(1)} %fusion.4, f32[1024,768]{1,0:T(8,128)S(1)} %copy-done.21), kind=kOutput, calls=%fused_computation.13 | convolution fusion | flops 6446383104 | bytes 17825792 | tf_op jit(solution)/shard_map/tv,vd->td/dot_general | solution.py:334
  303.9 83.3 %reduce-scatter.3.cloned.1.call-done = bf16[1,256,768]{2,1,0:T(8,128)(2,1)} async-done(((bf16[16,256,768]{2,1,0:T(8,128)(2,1)}), bf16[1,256,768]{2,1,0:T(8,128)(2,1)}) %reduce-scatter.3.cloned.1.call-update) | async-done | bytes 393232 | tf_op jit(solution)/shard_map/reduce_scatter | solution.py:438
  388.4 5.1 fusion.24
  393.6 2.0 multiply_reduce_fusion.1
  397.5 2.6 convolution_convert_fusion.6
  408.5 2.5 convolution_convert_fusion.3
  412.3 2.2 constant_dynamic-update-slice_fusion.2
  415.4 1.9 convolution_convert_fusion
  417.3 3.1 constant_dynamic-update-slice_fusion.1
  425.5 11.8 %convolution_convert_fusion.4 = bf16[1024,768]{1,0:T(8,128)(2,1)} fusion(bf16[4096,1024]{0,1:T(8,128)(2,1)} %copy-done.9, bf16[4096,768]{1,0:T(8,128)(2,1)} %all-gather.8.cloned.1.call-done), kind=kOutput, calls=%fused_computation.44 | convolution fusion | flops 6443237376 | bytes 16252928 | tf_op jit(solution)/shard_map/tv,td->vd/dot_general | solution.py:334
  437.4 32.0 %all-gather.6.cloned.1.call-done = bf16[16,256,768]{2,1,0:T(8,128)(2,1)} async-done(((bf16[1,256,768]{2,1,0:T(8,128)(2,1)}), bf16[16,256,768]{2,1,0:T(8,128)(2,1)}) %all-gather.6.cloned.1.call-update) | async-done | bytes 6291472 | tf_op jit(solution)/shard_map/all_gather | solution.py:481
  471.4 10.8 %fusion.14 = bf16[1024,768]{1,0:T(8,128)(2,1)} fusion(bf16[4096,768]{1,0:T(8,128)(2,1)} %bitcast.199, s32[4096]{0:T(1024)S(1)} %bitcast.195, s32[1024]{0:T(1024)S(1)} %iota_add_fusion), kind=kOutput, calls=%fused_computation.43 | convolution fusion | flops 6447431680 | bytes 7884800 | tf_op jit(solution)/shard_map/tv,td->vd/dot_general | solution.py:334
  482.2 139.3 %reduce-scatter.5.cloned.1.call-done = bf16[1,592,768]{2,1,0:T(8,128)(2,1)} async-done(((bf16[16,592,768]{2,1,0:T(8,128)(2,1)}), bf16[1,592,768]{2,1,0:T(8,128)(2,1)}) %reduce-scatter.5.cloned.1.call-update) | async-done | bytes 909328 | tf_op jit(solution)/shard_map/reduce_scatter | solution.py:480
  621.6 39.9 %psum.62 = f32[3,768]{1,0:T(4,128)S(1)} all-reduce(f32[3,768]{1,0:T(4,128)S(1)} %pad_maximum_fusion.9), channel_id=1, replica_groups=mesh['fsdp'=16,'rep'=2] {'fsdp','rep'}, use_global_device_ids=true, to_apply=%region_35.36 | all-reduce | flops 2304 | bytes 18432 | tf_op jit(solution)/shard_map/psum | solution.py:490
  663.7 91.1 %all-reduce.11.cloned.1.call-done = (bf16[1024,768]{1,0:T(8,128)(2,1)}, bf16[592,768]{1,0:T(8,128)(2,1)}, bf16[1024,768]{1,0:T(8,128)(2,1)}) async-done(((bf16[1024,768]{1,0:T(8,128)(2,1)}, bf16[592,768]{1,0:T(8,128)(2,1)}, bf16[1024,768]{1,0:T(8,128)(2,1)}), (bf16[1024,768]{1,0:T(8,128)(2,1)}, bf16[592,768]{1,0:T(8,128)(2,1)}, bf16[1024,768]{1,0:T(8,128)(2,1)})) %all-reduce.11.cloned.1.call-update) | async-done | bytes 4055056 | tf_op jit(solution)/shard_map/psum | solution.py:486
  771.3 33.7 %psum.63 = f32[]{:T(128)} all-reduce(f32[]{:T(128)S(6)} %add.283), channel_id=1, replica_groups=mesh['fsdp'=16,'rep'=2] {'fsdp'}, use_global_device_ids=true, to_apply=%region_37.38 | all-reduce | flops 1 | bytes 8 | tf_op jit(solution)/shard_map/psum | solution.py:499
  807.1 2.0 multiply_subtract_fusion.6
  809.1 2.6 multiply_subtract_fusion.4
  811.8 2.6 multiply_subtract_fusion.3
  814.4 3.4 multiply_subtract_fusion.2
  817.8 5.5 multiply_subtract_fusion
  824.8 4.8 multiply_subtract_fusion.1
  (227 shorter events, 72.5 us)
Async XLA Ops:
  7.2 12.4 %copy-start.4 = (f32[1024,768]{1,0:T(8,128)S(1)}, f32[1024,768]{1,0:T(8,128)}, u32[]{:S(2)}) copy-start(f32[1024,768]{1,0:T(8,128)} %param.32) | copy-start | bytes 9437188
  7.2 223.1 %all-gather.8.cloned.1.call-start = ((), (), s32[]{:S(2)}) async-start(), calls=%async_computation.6 | async-start | bytes 6684672 | tf_op jit(solution)/shard_map/all_gather | solution.py:423
  15.9 5.0 copy-start.47
  146.7 4.8 copy-start.30
  149.7 5.1 slice-start.1
  153.1 5.6 copy-start.6
  157.3 4.2 copy-start.16
  162.4 224.7 %reduce-scatter.3.cloned.1.call-start = ((), (), s32[]{:S(2)}) async-start(), calls=%async_computation.2 | async-start | bytes 6684672 | tf_op jit(solution)/shard_map/reduce_scatter | solution.py:438
  240.2 5.7 copy-start
  286.5 8.3 copy-start.21
  294.7 9.1 %copy-start.9 = (bf16[4096,1024]{0,1:T(8,128)(2,1)}, bf16[4096,1024]{0,1:T(8,128)(2,1)S(1)}, u32[]{:S(2)}) copy-start(bf16[4096,1024]{0,1:T(8,128)(2,1)S(1)} %fusion.4) | copy-start | bytes 25165828
  303.8 89.7 %slice-start.2 = ((s8[6291456]{0:T(1024)(128)(4,1)}), s8[2097152]{0:T(1024)(128)(4,1)S(1)}, s32[]{:S(2)}) async-start(s8[6291456]{0:T(1024)(128)(4,1)} %bitcast.163), calls=%async_computation.10 | async-start | bytes 4194304
  303.8 165.5 %all-gather.6.cloned.1.call-start = ((), (), s32[]{:S(2)}) async-start(), calls=%async_computation.3 | async-start | bytes 6684672 | tf_op jit(solution)/shard_map/all_gather | solution.py:481
  388.4 5.1 slice-start.3
  388.4 5.1 copy-start.7
  408.2 213.3 %reduce-scatter.5.cloned.1.call-start = ((), (), s32[]{:S(2)}) async-start(), calls=%async_computation.5 | async-start | bytes 15458304 | tf_op jit(solution)/shard_map/reduce_scatter | solution.py:480
  425.5 236.7 %all-reduce.9.cloned.1.call-start = ((), (), s32[]{:S(2)}) async-start(), calls=%async_computation.4 | async-start | bytes 393216 | tf_op jit(solution)/shard_map/psum | solution.py:486
  471.3 283.5 %all-reduce.11.cloned.1.call-start = ((), (), s32[]{:S(2)}) async-start(), calls=%async_computation.7 | async-start | bytes 8110080 | tf_op jit(solution)/shard_map/psum | solution.py:486
  754.8 6.8 copy-start.11
  756.4 6.6 copy-start.10
  759.4 46.2 %copy-start.46 = (f32[3,48]{1,0:T(4,128)S(1)}, f32[3,48]{1,0:T(4,128)}, u32[]{:S(2)}) copy-start(f32[3,48]{1,0:T(4,128)} %param.53) | copy-start | bytes 1732
  805.7 6.1 copy-start.27
  807.1 10.6 %copy-start.24 = (f32[1024,768]{1,0:T(8,128)S(1)}, f32[1024,768]{1,0:T(8,128)}, u32[]{:S(2)}) copy-start(f32[1024,768]{1,0:T(8,128)} %param.52) | copy-start | bytes 9437188
  809.1 5.2 copy-start.20
  811.8 6.0 copy-start.23
  817.8 5.5 copy-start.5
  817.8 5.5 copy-start.25
  817.8 7.0 copy-start.26
  824.8 4.8 copy-start.33
  824.8 4.8 copy-start.34
  824.8 4.8 copy-start.42
  824.8 4.8 copy-start.43
  (33 other events, 80.0 us)
Sparse Core Ops, SparseCore 0:
  162.6 67.7 all-gather.7
  303.9 83.1 reduce-scatter.2
  408.3 60.9 all-gather.5
  473.9 147.5 reduce-scatter.4
  624.2 21.4 all-reduce.8
  648.7 106.0 all-reduce.10

commit v3 on v2

--- a/solution.py
+++ b/solution.py
@@ -1,4 +1,5 @@
 import functools
+import math
 
 import jax
 import jax.numpy as jnp
@@ -105,12 +106,27 @@
     return me, me // (2 * y_size), (me // 2) % y_size, me % 2
 
 
+def send(src, dst, sems, index, device):
+    pltpu.make_async_remote_copy(
+        src_ref=src, dst_ref=dst, send_sem=sems.at[(0,) + index], recv_sem=sems.at[(1,) + index],
+        device_id=device, device_id_type=MESH,
+    ).start()
+
+
+def arrival(dst, sems, index):
+    pltpu.make_async_copy(dst, dst, sems.at[(1,) + index]).wait()
+
+
+def departure(src, sems, index):
+    pltpu.make_async_copy(src, src, sems.at[(0,) + index]).wait()
+
+
 def front_kernel(z_size, y_size, reps, own_width, parts, facts, code_b, class_b, *refs):
     count = len(parts)
     weights, refs = refs[:count], refs[count:]
     wholes, refs = refs[:count], refs[count:]
     (stream, facts_all, turned, acc, core_out, core_in, y_in, z_in,
-     fact_sems, z_sems, y_sems, x_sems, c_sems, own_sems, rc_sems, ry_sems, rz_sems) = refs
+     fact_sems, rep_sems, z_sems, y_sems, x_sems, c_sems, own_sems, rc_sems, ry_sems, rz_sems) = refs
     n = z_size * y_size * 2
     me, z, y, core = where_am_i(z_size, y_size)
     x = lax.axis_index("rep")
@@ -129,22 +145,9 @@
         pl.semaphore_signal(barrier, inc=1, device_id=(me, lax.rem(x + k, reps)), device_id_type=MESH)
     pl.semaphore_wait(barrier, n - 1 + reps - 1)
 
-    def send(src, dst, sems, index, device):
-        copy = pltpu.make_async_remote_copy(
-            src_ref=src, dst_ref=dst, send_sem=sems.at[(0,) + index], recv_sem=sems.at[(1,) + index],
-            device_id=device, device_id_type=MESH,
-        )
-        copy.start()
-
-    def arrival(dst, sems, index):
-        pltpu.make_async_copy(dst, dst, sems.at[(1,) + index]).wait()
-
-    def departure(src, sems, index):
-        pltpu.make_async_copy(src, src, sems.at[(0,) + index]).wait()
-
-    for k in range(1, n):
-        send(facts, facts_all.at[me], fact_sems, (k,), (lax.rem(me + k, n), x))
-    facts_all[me] = facts[...]
+    for k in range(1, n):
+        send(facts, facts_all.at[x, me], fact_sems, (k,), (lax.rem(me + k, n), x))
+    facts_all[x, me] = facts[...]
 
     peers_z = [(dz, at(dz, 0)) for dz in range(1, z_size)]
     peers_y = [(dy, at(0, dy)) for dy in range(1, y_size)]
@@ -196,8 +199,10 @@
                 send(block, block, c_sems, (k, dz, dy), (at(0, 0, 1), x))
 
     for k in range(1, n):
-        arrival(facts_all.at[lax.rem(me - k + n, n)], fact_sems, (k,))
-    turned[...] = jnp.transpose(facts_all[...].reshape(n * 8, 128))
+        arrival(facts_all.at[x, lax.rem(me - k + n, n)], fact_sems, (k,))
+    for k in range(1, reps):
+        send(facts_all.at[x], facts_all.at[x], rep_sems, (k,), (me, lax.rem(x + k, reps)))
+    turned[...] = jnp.transpose(facts_all[x].reshape(n * 8, 128))
     lane = lax.broadcasted_iota(jnp.int32, (128, n * 8), 1)
     class_rows = class_b[...].astype(F32)
     class_iota = lax.broadcasted_iota(jnp.int32, class_rows.shape, 0).astype(F32)
@@ -255,6 +260,10 @@
     for dz, dy in spots[1:]:
         after_x(dz, dy)
 
+    for k in range(1, reps):
+        arrival(facts_all.at[x], rep_sems, (k,))
+        departure(facts_all.at[x], rep_sems, (k,))
+
     for k in range(1, n):
         departure(facts, fact_sems, (k,))
     for dz, dy in spots:
@@ -293,7 +302,7 @@
     outs = pl.pallas_call(
         functools.partial(front_kernel, z_size, y_size, reps, own_width, parts),
         out_shape=[jax.ShapeDtypeStruct((n,) + w.shape, w.dtype) for w in weights]
-        + [jax.ShapeDtypeStruct(block, F32), jax.ShapeDtypeStruct((n, 8, 128), F32)],
+        + [jax.ShapeDtypeStruct(block, F32), jax.ShapeDtypeStruct((reps, n, 8, 128), F32)],
         in_specs=[vmem] * 3 + [hbm] * count,
         out_specs=[hbm] * count + [vmem] * 2,
         scratch_shapes=[
@@ -304,6 +313,7 @@
             pltpu.VMEM((z_size, y_size) + block, BF),
             pltpu.VMEM((z_size,) + block, BF),
             dma((2, n)),
+            dma((2, reps)),
             dma((2, count, z_size)),
             dma((2, count, z_size, y_size)),
             dma((2, count, z_size, y_size, reps)),
@@ -319,6 +329,630 @@
         name="front",
     )(facts, code_b, class_b, *weights)
     return outs[:count], outs[count], outs[count + 1]
+
+
+class Place:
+    def __init__(self, z_size, y_size, reps):
+        self.z_size, self.y_size, self.reps = z_size, y_size, reps
+        self.n = z_size * y_size * 2
+        self.me, self.z, self.y, self.core = where_am_i(z_size, y_size)
+        self.x = lax.axis_index("rep")
+
+    def at(self, dz, dy, other=0):
+        c = 1 - self.core if other else self.core
+        z, y = lax.rem(self.z + dz, self.z_size), lax.rem(self.y + dy, self.y_size)
+        return (z * self.y_size + y) * 2 + c
+
+    def plane(self, z, dy=0, other=0):
+        c = 1 - self.core if other else self.core
+        return (z * self.y_size + lax.rem(self.y + dy, self.y_size)) * 2 + c
+
+    def twin(self):
+        return (self.at(0, 0, 1), self.x)
+
+    def greet(self, everyone):
+        barrier = pltpu.get_barrier_semaphore()
+        if everyone:
+            group = [lax.rem(self.me + k, self.n) for k in range(1, self.n)]
+        else:
+            group = [self.at(dz, 0) for dz in range(1, self.z_size)]
+            group += [self.at(0, dy) for dy in range(1, self.y_size)] + [self.at(0, 0, 1)]
+        peers = [(p, self.x) for p in group]
+        peers += [(self.me, lax.rem(self.x + k, self.reps)) for k in range(1, self.reps)]
+        for peer in peers:
+            pl.semaphore_signal(barrier, inc=1, device_id=peer, device_id_type=MESH)
+        pl.semaphore_wait(barrier, len(peers))
+
+
+class Spread:
+    def __init__(self, place, whole, z_sems, y_sems, c_sems):
+        self.p, self.whole = place, whole
+        self.z_sems, self.y_sems, self.c_sems = z_sems, y_sems, c_sems
+
+    def block(self, z, dy=0, other=0):
+        return self.whole.at[self.p.plane(z, dy, other)]
+
+    def pass_on(self, z, src, up, down):
+        p = self.p
+        dst = self.block(z)
+        if up:
+
+            @pl.when(p.z + 1 < p.z_size)
+            def _():
+                send(src, dst, self.z_sems, (0, z), (p.plane(p.z + 1), p.x))
+
+        if down:
+
+            @pl.when(p.z >= 1)
+            def _():
+                send(src, dst, self.z_sems, (1, z), (p.plane(p.z - 1), p.x))
+
+        for dy in range(1, p.y_size):
+            send(src, dst, self.y_sems, (z, dy), (p.at(0, dy), p.x))
+        send(src, dst, self.c_sems, (z, 0), p.twin())
+
+    def start(self, own):
+        self.pass_on(self.p.z, own, True, True)
+
+    def step_z(self, s):
+        p = self.p
+
+        @pl.when(p.z - s >= 0)
+        def _():
+            arrival(self.block(p.z - s), self.z_sems, (0, p.z - s))
+            self.pass_on(p.z - s, self.block(p.z - s), True, False)
+
+        @pl.when(p.z + s < p.z_size)
+        def _():
+            arrival(self.block(p.z + s), self.z_sems, (1, p.z + s))
+            self.pass_on(p.z + s, self.block(p.z + s), False, True)
+
+    def take_y(self, z):
+        for dy in range(1, self.p.y_size):
+            block = self.block(z, self.p.y_size - dy)
+            arrival(block, self.y_sems, (z, dy))
+            send(block, block, self.c_sems, (z, dy), self.p.twin())
+
+    def take_twin(self, z):
+        for dy in range(self.p.y_size):
+            arrival(self.block(z, self.p.y_size - dy, 1), self.c_sems, (z, dy))
+
+    def finish(self):
+        p = self.p
+        block = self.block(p.z)
+        for z in range(p.z_size):
+
+            @pl.when(jnp.logical_and(p.z + 1 < p.z_size, z <= p.z))
+            def _():
+                departure(block, self.z_sems, (0, z))
+
+            @pl.when(jnp.logical_and(p.z >= 1, z >= p.z))
+            def _():
+                departure(block, self.z_sems, (1, z))
+
+            for dy in range(p.y_size):
+                departure(block, self.c_sems, (z, dy))
+                if dy:
+                    departure(block, self.y_sems, (z, dy))
+
+
+def head_kernel(z_size, y_size, reps, normed3, head_b, facts, grad_normed3, grad_head, totals,
+                whole, logits, grads, turned, marks, stats_in, lse_all, acc, core_out, core_in, y_in, z_in,
+                loss_in, z_sems, y_sems, c_sems, st_sems, ls_sems, rc_sems, ry_sems, rz_sems, lo_sems):
+    p = Place(z_size, y_size, reps)
+    n, me, x = p.n, p.me, p.x
+    length, width = normed3.shape
+    half = length // 2
+    own_rows = head_b.shape[0]
+    p.greet(True)
+    spread = Spread(p, whole, z_sems, y_sems, c_sems)
+    spread.start(normed3)
+    whole[me] = normed3[...]
+    own_facts = facts.at[x]
+    turned[...] = jnp.transpose(own_facts[...].reshape(n * 8, 128))
+    lane = lax.broadcasted_iota(jnp.int32, (128, n * 8), 1)
+    full_lane = lax.broadcasted_iota(jnp.int32, (length, n * 8), 1)
+    column_iota = (lax.broadcasted_iota(jnp.int32, (length, own_rows), 1) + me * own_rows).astype(F32)
+    token = lax.broadcasted_iota(jnp.int32, (length, 1), 0).astype(F32)
+    every = facts[...].reshape(reps * n * 8, 128)
+    row8 = lax.rem(lax.broadcasted_iota(jnp.int32, every.shape, 0), 8)
+    spot = jnp.logical_and(row8 == 4, lax.broadcasted_iota(jnp.int32, every.shape, 1) == 1)
+    token_count = jnp.sum(jnp.sum(jnp.where(spot, every, 0.0), 0, keepdims=True), 1, keepdims=True)
+    inv_count = 1.0 / token_count
+
+    def codes_of(image):
+        parts = [
+            jnp.sum(jnp.where(lane == image * 8 + 2 + h, turned[...], 0.0), -1, keepdims=True)
+            for h in range(2)
+        ]
+        return jnp.concatenate(parts, 0)
+
+    marks[...] = jnp.zeros_like(marks)
+
+    def forward(image):
+        out = lax.dot_general(
+            whole[image], head_b[...], (((1,), (1,)), ((), ())), preferred_element_type=F32
+        )
+        logits[image] = out
+        top = jnp.max(out, -1, keepdims=True)
+        total = jnp.sum(jnp.exp(out - top), -1, keepdims=True)
+        pick = jnp.sum(jnp.where(column_iota == codes_of(image), out, 0.0), -1, keepdims=True)
+        old = marks[...]
+        old = jnp.where(full_lane == image * 8, top, old)
+        old = jnp.where(full_lane == image * 8 + 1, total, old)
+        marks[...] = jnp.where(full_lane == image * 8 + 2, pick, old)
+
+    def forward_column(z, first, last):
+        def body(j, carry):
+            forward(p.plane(z, lax.rem(y_size - j // 2, y_size), 0) + lax.rem(j, 2) * (1 - 2 * p.core))
+            return carry
+
+        lax.fori_loop(first * 2, last * 2, body, 0)
+
+    def forward_y(z):
+        spread.take_y(z)
+
+    arrival(spread.block(p.z, 0, 1), c_sems, (p.z, 0))
+    forward_column(p.z, 0, 1)
+
+    def one(z, s):
+        arrival(spread.block(z, 0, 1), c_sems, (z, 0))
+        forward_column(z, 0, 1)
+
+    def other(z):
+        for dy in range(1, y_size):
+            arrival(spread.block(z, y_size - dy, 1), c_sems, (z, dy))
+        forward_column(z, 1, y_size)
+
+    def both(s, act):
+        if s == 0:
+            act(p.z)
+            return
+
+        @pl.when(p.z - s >= 0)
+        def _():
+            act(p.z - s)
+
+        @pl.when(p.z + s < z_size)
+        def _():
+            act(p.z + s)
+
+    for s in range(1, z_size + 1):
+        if s < z_size:
+            spread.step_z(s)
+        both(s - 1, spread.take_y)
+        if s < z_size:
+            both(s, lambda z: one(z, s))
+        both(s - 1, other)
+
+    tiles = jnp.transpose(marks[...]).reshape(n, 8, length)
+    stats_in[1] = tiles
+    for k in range(1, n):
+        peer = lax.rem(me + k, n)
+        send(stats_in.at[1, peer], stats_in.at[0, me], st_sems, (k,), (peer, x))
+    stats_in[0, me] = stats_in[1, me]
+    for k in range(1, n):
+        arrival(stats_in.at[0, 0], st_sems, (k,))
+    tops = stats_in[0, :, 0, :]
+    sums = stats_in[0, :, 1, :]
+    picks = stats_in[0, :, 2, :]
+    top = jnp.max(tops, 0, keepdims=True)
+    lse = jnp.log(jnp.sum(sums * jnp.exp(tops - top), 0, keepdims=True)) + top
+    pick = jnp.sum(picks, 0, keepdims=True)
+    here = own_facts[me]
+    counted = lax.broadcasted_iota(jnp.int32, (1, length), 1).astype(F32) < here[4:5, 1:2]
+    loss = jnp.where(counted, lse - pick, 0.0)
+    lse_all[me] = jnp.concatenate([lse, loss, jnp.zeros((6, length), F32)], 0)
+    for k in range(1, n):
+        peer = lax.rem(me + k, n)
+        send(lse_all.at[me], lse_all.at[me], ls_sems, (k,), (peer, x))
+    for k in range(1, n):
+        arrival(lse_all.at[0], ls_sems, (k,))
+    table = lse_all[...].reshape(n * 8, length)
+    row8 = lax.rem(lax.broadcasted_iota(jnp.int32, table.shape, 0), 8)
+    group = jnp.sum(jnp.sum(jnp.where(row8 == 1, table, 0.0), 0, keepdims=True), 1, keepdims=True)
+    loss_in[x] = jnp.broadcast_to(group, (8, 128))
+    for k in range(1, reps):
+        peer = (me, lax.rem(x + k, reps))
+        send(loss_in.at[x], loss_in.at[x], lo_sems, (k,), peer)
+    marks[...] = jnp.transpose(table)
+
+    def backward(image, out):
+        lse_t = jnp.sum(jnp.where(full_lane == image * 8, marks[...], 0.0), -1, keepdims=True)
+        size = jnp.sum(jnp.where(lane[:8] == image * 8 + 4, turned[:8, :], 0.0), -1, keepdims=True)
+        weight = jnp.where(token < size[1:2], inv_count, 0.0)
+        hot = jnp.where(column_iota == codes_of(image), 1.0, 0.0)
+        grad = ((jnp.exp(logits[image] - lse_t) - hot) * weight).astype(BF)
+        grads[image] = grad
+        out[...] = jnp.dot(grad, head_b[...], preferred_element_type=F32).astype(BF)
+
+    last = z_size - 1
+
+    def far(j):
+        return last - j // y_size, lax.rem(j, y_size)
+
+    def first_pass(j, carry):
+        dz, dyy = far(j)
+        dy = y_size - 1 - dyy
+        slot = dz * y_size + dy
+        backward(p.at(dz, dy, 1), core_out.at[slot])
+        send(core_out.at[slot], core_in.at[slot], rc_sems, (slot,), p.twin())
+        backward(p.at(dz, dy), acc.at[slot])
+        return carry
+
+    def twin_sum(slot):
+        arrival(core_in.at[slot], rc_sems, (slot,))
+        acc[slot] = (acc[slot].astype(F32) + core_in[slot].astype(F32)).astype(BF)
+
+    def y_sum(dz):
+        slot = dz * y_size
+        total = acc[slot].astype(F32)
+        for dy in range(1, y_size):
+            arrival(y_in.at[dz, dy], ry_sems, (dz, dy))
+            total = total + y_in[dz, dy].astype(F32)
+        acc[slot] = total.astype(BF)
+
+    def round_of(g, carry):
+        dz = last - g
+
+        def per_dy(i, c):
+            return first_pass(g * y_size + i, c)
+
+        lax.fori_loop(0, y_size, per_dy, 0)
+        for dy in range(y_size - 1, -1, -1):
+            slot = dz * y_size + dy
+            twin_sum(slot)
+            if dy:
+                send(acc.at[slot], y_in.at[dz, dy], ry_sems, (dz, dy), (p.at(0, dy), x))
+
+        @pl.when(g >= 1)
+        def _():
+            y_sum(dz + 1)
+            send(acc.at[(dz + 1) * y_size], z_in.at[dz + 1], rz_sems, (dz + 1,), (p.at(dz + 1, 0), x))
+
+        return carry
+
+    lax.fori_loop(0, z_size, round_of, 0)
+
+    blocks = 4
+    rows = own_rows // blocks
+    for r in range(blocks):
+
+        def add(image, total):
+            return total + lax.dot_general(
+                grads[image, :, r * rows : (r + 1) * rows], whole[image],
+                (((0,), (0,)), ((), ())), preferred_element_type=F32,
+            )
+
+        total = lax.fori_loop(0, n, add, jnp.zeros((rows, width), F32))
+        grad_head[r * rows : (r + 1) * rows] = total.astype(BF)
+    y_sum(0)
+    total = acc[0].astype(F32)
+    for dz in range(1, z_size):
+        arrival(z_in.at[dz], rz_sems, (dz,))
+        total = total + z_in[dz].astype(F32)
+    grad_normed3[...] = total
+    for k in range(1, reps):
+        arrival(loss_in.at[0], lo_sems, (k,))
+    loss_sum = loss_in[0]
+    for k in range(1, reps):
+        loss_sum = loss_sum + loss_in[k]
+    totals[...] = jnp.where(
+        lax.broadcasted_iota(jnp.int32, (8, 128), 0) == 0, loss_sum, token_count
+    )
+
+    spread.finish()
+    for k in range(1, n):
+        departure(stats_in.at[0, 0], st_sems, (k,))
+        departure(lse_all.at[0], ls_sems, (k,))
+    for k in range(1, reps):
+        departure(loss_in.at[0], lo_sems, (k,))
+    for dz in range(z_size):
+        for dy in range(y_size):
+            slot = dz * y_size + dy
+            departure(core_out.at[slot], rc_sems, (slot,))
+            if dy:
+                departure(acc.at[slot], ry_sems, (dz, dy))
+            elif dz:
+                departure(acc.at[slot], rz_sems, (dz,))
+
+
+def head_scratch(n, length, width, own_rows, reps):
+    z_size, y_size = geometry(n)
+    spots = z_size * y_size
+    dma = pltpu.SemaphoreType.DMA
+    buffers = [
+        ((n, length, width), BF),
+        ((n, length, own_rows), F32),
+        ((n, length, own_rows), BF),
+        ((128, n * 8), F32),
+        ((length, n * 8), F32),
+        ((2, n, 8, length), F32),
+        ((n, 8, length), F32),
+        ((spots, length, width), BF),
+        ((spots, length, width), BF),
+        ((spots, length, width), BF),
+        ((z_size, y_size, length, width), BF),
+        ((z_size, length, width), BF),
+        ((reps, 8, 128), F32),
+    ]
+    sems = [
+        dma((2, 2, z_size)), dma((2, z_size, y_size)), dma((2, z_size, y_size)),
+        dma((2, n)), dma((2, n)), dma((2, spots)), dma((2, z_size, y_size)), dma((2, z_size)),
+        dma((2, reps)),
+    ]
+    return buffers, sems
+
+
+def size_of(buffers):
+    return sum(math.prod(shape) * jnp.dtype(kind).itemsize for shape, kind in buffers)
+
+
+def head_phase(normed3, head_b, facts, reps, n):
+    z_size, y_size = geometry(n)
+    length, width = normed3.shape
+    buffers, sems = head_scratch(n, length, width, head_b.shape[0], reps)
+    vmem = pl.BlockSpec(memory_space=pltpu.VMEM)
+    return pl.pallas_call(
+        functools.partial(head_kernel, z_size, y_size, reps),
+        out_shape=[
+            jax.ShapeDtypeStruct((length, width), F32),
+            jax.ShapeDtypeStruct(head_b.shape, BF),
+            jax.ShapeDtypeStruct((8, 128), F32),
+        ],
+        in_specs=[vmem] * 3,
+        out_specs=[vmem] * 3,
+        scratch_shapes=[pltpu.VMEM(shape, kind) for shape, kind in buffers] + sems,
+        compiler_params=pltpu.CompilerParams(
+            collective_id=1, has_side_effects=True, vmem_limit_bytes=60 * 2**20
+        ),
+        name="head",
+    )(normed3, head_b, facts)
+
+
+def tail_kernel(z_size, y_size, split, counts, grad_stream0, facts, *refs):
+    count = len(split)
+    grads, refs = refs[:count], refs[count:]
+    sums, refs = refs[:count], refs[count:]
+    code_sum, first_rows, refs = refs[0], refs[1], refs[2:]
+    accs, refs = refs[:count], refs[count:]
+    core_in, refs = refs[:count], refs[count:]
+    x_in, refs = refs[:count], refs[count:]
+    y_in, refs = refs[:count], refs[count:]
+    z_in, refs = refs[:count], refs[count:]
+    trade, refs = refs[:count], refs[count:]
+    (whole, code_out, code_in, rows_out, z_sems, y_sems, c_sems, own_sems, rc_sems, rx_sems, ry_sems,
+     rz_sems, tr_sems, co_sems, fr_sems) = refs
+    p = Place(z_size, y_size, 2)
+    n, me, x = p.n, p.me, p.x
+    length, width = grad_stream0.shape
+    own_rows = code_out.shape[0]
+    spots = z_size * y_size
+    p.greet(False)
+    mate = (me, 1 - x)
+    spread = Spread(p, whole, z_sems, y_sems, c_sems)
+    spread.start(grad_stream0)
+    whole[me] = grad_stream0[...]
+
+    def slot_of(dz, dy):
+        return dz * y_size + dy
+
+    order = [(dz, dy) for dz in range(z_size - 1, -1, -1) for dy in range(y_size - 1, -1, -1)]
+    for dz, dy in order:
+        slot = slot_of(dz, dy)
+        for k in range(count):
+            send(grads[k].at[p.at(dz, dy, 1)], core_in[k].at[slot], rc_sems, (k, slot), p.twin())
+            pltpu.make_async_copy(grads[k].at[p.at(dz, dy)], accs[k].at[slot], own_sems.at[k, slot]).start()
+
+    def part(k, which):
+        rows = counts[k] // 2
+        return pl.ds(pl.multiple_of(which * rows, rows), rows)
+
+    def ref_of(k, ref, which):
+        return ref.at[part(k, which)] if split[k] else ref
+
+    def send_y(k, dz, dy):
+        slot = slot_of(dz, dy)
+        send(ref_of(k, accs[k].at[slot], x), y_in[k].at[slot], ry_sems, (k, slot), (p.at(0, dy), x))
+
+    for dz, dy in order:
+        slot = slot_of(dz, dy)
+        for k in range(count):
+            pltpu.make_async_copy(grads[k].at[0], accs[k].at[slot], own_sems.at[k, slot]).wait()
+            arrival(core_in[k].at[slot], rc_sems, (k, slot))
+            accs[k][slot] = (accs[k][slot].astype(F32) + core_in[k][slot].astype(F32)).astype(BF)
+            if split[k]:
+                send(accs[k].at[slot, part(k, 1 - x)], x_in[k].at[slot], rx_sems, (k, slot), mate)
+            elif dy:
+                send_y(k, dz, dy)
+
+    def take_x(dz):
+        for dy in range(y_size - 1, -1, -1):
+            slot = slot_of(dz, dy)
+            for k in range(count):
+                if split[k]:
+                    arrival(x_in[k].at[slot], rx_sems, (k, slot))
+                    mine = accs[k].at[slot, part(k, x)]
+                    mine[...] = (mine[...].astype(F32) + x_in[k][slot].astype(F32)).astype(BF)
+                    if dy:
+                        send_y(k, dz, dy)
+
+    def take_y(dz):
+        for k in range(count):
+            mine = ref_of(k, accs[k].at[slot_of(dz, 0)], x)
+            total = mine[...].astype(F32)
+            for dy in range(1, y_size):
+                slot = slot_of(dz, dy)
+                arrival(y_in[k].at[slot], ry_sems, (k, slot))
+                total = total + y_in[k][slot].astype(F32)
+            mine[...] = total.astype(BF)
+            if dz:
+                send(mine, z_in[k].at[dz], rz_sems, (k, dz), (p.at(dz, 0), x))
+
+    spread.step_z(1)
+    take_x(z_size - 1)
+    spread.take_y(p.z)
+    take_y(z_size - 1)
+
+    def both(s, act):
+        @pl.when(p.z - s >= 0)
+        def _():
+            act(p.z - s)
+
+        @pl.when(p.z + s < z_size)
+        def _():
+            act(p.z + s)
+
+    for s in range(2, z_size):
+        dz = z_size - s
+        spread.step_z(s)
+        take_x(dz)
+        both(s - 1, spread.take_y)
+        take_y(dz)
+    both(z_size - 1, spread.take_y)
+    take_x(0)
+    for z in range(z_size):
+        spread.take_twin(z)
+
+    blocks = 4
+    rows = own_rows // blocks
+    iota = lax.broadcasted_iota(jnp.int32, (rows, length // 2), 0) + me * own_rows
+
+    def code_block(r, carry):
+        base = (iota + r * rows).astype(F32)
+
+        def add(image, total):
+            ids = facts[x, image]
+            hot = jnp.concatenate(
+                [jnp.where(base == ids[h : h + 1, :], 1.0, 0.0) for h in range(2)], 1
+            ).astype(BF)
+            return total + jnp.dot(hot, whole[image], preferred_element_type=F32)
+
+        total = lax.fori_loop(0, n, add, jnp.zeros((rows, width), F32))
+        at = pl.ds(pl.multiple_of(r * rows, rows), rows)
+        code_out[at] = total.astype(BF)
+        send(code_out.at[at], code_in.at[at], co_sems, (r,), mate)
+        return carry
+
+    firsts = whole[:, 0:8, :].astype(F32)
+    rows_out[x] = firsts
+    send(rows_out.at[x], rows_out.at[x], fr_sems, (), mate)
+    lax.fori_loop(0, blocks, code_block, 0)
+
+    take_y(0)
+    for k in range(count):
+        mine = ref_of(k, accs[k].at[0], x)
+        total = mine[...].astype(F32)
+        for dz in range(1, z_size):
+            arrival(z_in[k].at[dz], rz_sems, (k, dz))
+            total = total + z_in[k][dz].astype(F32)
+        ref_of(k, trade[k].at[0], x)[...] = total.astype(BF)
+        source = ref_of(k, trade[k].at[0], x)
+        target = source if split[k] else trade[k].at[1]
+        if split[k]:
+            target = trade[k].at[0, part(k, x)]
+        send(source, target, tr_sems, (k,), mate)
+    for k in range(count):
+        if split[k]:
+            arrival(trade[k].at[0, part(k, 1 - x)], tr_sems, (k,))
+            sums[k][...] = trade[k][0].astype(F32)
+        else:
+            arrival(trade[k].at[1], tr_sems, (k,))
+            sums[k][...] = trade[k][0].astype(F32) + trade[k][1].astype(F32)
+    arrival(rows_out.at[1 - x], fr_sems, ())
+    first_rows[...] = rows_out[...]
+    for r in range(blocks):
+        at = pl.ds(r * rows, rows)
+        arrival(code_in.at[at], co_sems, (r,))
+        code_sum[at] = code_out[at].astype(F32) + code_in[at].astype(F32)
+
+    spread.finish()
+    departure(rows_out.at[x], fr_sems, ())
+    for r in range(blocks):
+        departure(code_out.at[pl.ds(r * rows, rows)], co_sems, (r,))
+    for k in range(count):
+        departure(ref_of(k, trade[k].at[0], x), tr_sems, (k,))
+        for dz in range(z_size):
+            if dz:
+                departure(z_in[k].at[dz], rz_sems, (k, dz))
+            for dy in range(y_size):
+                slot = slot_of(dz, dy)
+                departure(core_in[k].at[slot], rc_sems, (k, slot))
+                if split[k]:
+                    departure(x_in[k].at[slot], rx_sems, (k, slot))
+                if dy:
+                    departure(y_in[k].at[slot], ry_sems, (k, slot))
+
+
+def tail_scratch(n, length, width, own_rows, shapes, split):
+    z_size, y_size = geometry(n)
+    spots = z_size * y_size
+    count = len(shapes)
+    dma = pltpu.SemaphoreType.DMA
+    halves = [(s[0] // 2, s[1]) if h else s for s, h in zip(shapes, split)]
+    buffers = [((spots,) + s, BF) for s in shapes] * 2
+    buffers += [((spots,) + s if h else (16, 128), BF) for s, h in zip(halves, split)]
+    buffers += [((spots,) + s, BF) for s in halves]
+    buffers += [((z_size,) + s, BF) for s in halves]
+    buffers += [((2,) + s, BF) for s in shapes]
+    buffers += [((n, length, width), BF), ((own_rows, width), BF), ((own_rows, width), BF),
+                ((2, n, 8, width), F32)]
+    sems = [
+        dma((2, 2, z_size)), dma((2, z_size, y_size)), dma((2, z_size, y_size)),
+        dma((count, spots)), dma((2, count, spots)), dma((2, count, spots)), dma((2, count, spots)),
+        dma((2, count, z_size)), dma((2, count)), dma((2, 4)), dma((2,)),
+    ]
+    return buffers, sems
+
+
+def tail_phase(grad_stream0, facts, grads, split, own_rows, n):
+    z_size, y_size = geometry(n)
+    length, width = grad_stream0.shape
+    shapes = [g.shape[1:] for g in grads]
+    buffers, sems = tail_scratch(n, length, width, own_rows, shapes, split)
+    vmem, hbm = pl.BlockSpec(memory_space=pltpu.VMEM), pl.BlockSpec(memory_space=pl.ANY)
+    outs = pl.pallas_call(
+        functools.partial(tail_kernel, z_size, y_size, split, tuple(s[0] for s in shapes)),
+        out_shape=[jax.ShapeDtypeStruct(s, F32) for s in shapes]
+        + [jax.ShapeDtypeStruct((own_rows, width), F32), jax.ShapeDtypeStruct((2, n, 8, width), F32)],
+        in_specs=[vmem] * 2 + [hbm] * len(grads),
+        out_specs=[vmem] * (len(grads) + 2),
+        scratch_shapes=[pltpu.VMEM(shape, kind) for shape, kind in buffers] + sems,
+        compiler_params=pltpu.CompilerParams(
+            collective_id=2, has_side_effects=True, vmem_limit_bytes=60 * 2**20
+        ),
+        name="tail",
+    )(grad_stream0, facts, *grads)
+    return outs[: len(grads)], outs[len(grads)], outs[len(grads) + 1]
+
+
+def norm_kernel(n, squares, total, given, sems):
+    me, x = lax.axis_index("fsdp"), lax.axis_index("rep")
+    barrier = pltpu.get_barrier_semaphore()
+    for k in range(1, n):
+        pl.semaphore_signal(barrier, inc=1, device_id=(lax.rem(me + k, n), x), device_id_type=MESH)
+    pl.semaphore_wait(barrier, n - 1)
+    for k in range(1, n):
+        send(squares, given.at[me], sems, (k,), (lax.rem(me + k, n), x))
+    given[me] = squares[...]
+    for k in range(1, n):
+        arrival(given.at[0], sems, (k,))
+    total[...] = jnp.sum(given[...], 0)
+    for k in range(1, n):
+        departure(given.at[0], sems, (k,))
+
+
+def sum_over_fsdp(squares, n):
+    vmem = pl.BlockSpec(memory_space=pltpu.VMEM)
+    return pl.pallas_call(
+        functools.partial(norm_kernel, n),
+        out_shape=jax.ShapeDtypeStruct((8, 128), F32),
+        in_specs=[vmem],
+        out_specs=vmem,
+        scratch_shapes=[pltpu.VMEM((n, 8, 128), F32), pltpu.SemaphoreType.DMA((2, n))],
+        compiler_params=pltpu.CompilerParams(collective_id=3, has_side_effects=True),
+        name="norm",
+    )(jnp.broadcast_to(squares, (8, 128)))[0, 0]
 
 
 def adam_update(weight, first, second, grad, rate, decay):
@@ -384,13 +1018,13 @@
     stream0 = stream0[None]
     images = n * batch
     tokens = images * length
+    every_fact, facts = facts, facts[lax.axis_index("rep")]
     gains32 = facts[:, 5:8, :own_width].transpose(1, 0, 2).reshape(3, width)
     all_codes = facts[:, 2:4].reshape(images, length).astype(jnp.int32)
     previous = facts[:, 0:2].reshape(tokens).astype(jnp.int32)
     all_classes = facts[:, 4, 0].astype(jnp.int32)
     all_lengths = facts[:, 4, 1].astype(jnp.int32)
     all_counted = (jnp.arange(length)[None, :] < all_lengths[:, None]).astype(F32)
-    token_count = lax.psum(jnp.sum(all_counted), "rep")
     own_ids = jnp.arange(own_rows) + me * own_rows
     lookup = (previous[:, None] == own_ids[None, :]).astype(BF)
 
@@ -420,24 +1054,32 @@
     normed3 = normed3.astype(BF)
 
     head_b = head_weight.astype(BF)
-    normed3_all = lax.all_gather(normed3, "fsdp", axis=0, tiled=True).reshape(tokens, width)
-    logits = dot("td,vd->tv", normed3_all, head_b)
-    onehot = all_codes.reshape(tokens)[:, None] == own_ids[None, :]
-    local_top = jnp.max(logits, -1)
-    local_sum = jnp.sum(jnp.exp(logits - local_top[:, None]), -1)
-    local_pick = jnp.sum(jnp.where(onehot, logits, 0.0), -1)
-    stats = lax.all_gather(jnp.stack([local_top, local_sum, local_pick]), "fsdp", axis=0)
-    ltop = jnp.max(stats[:, 0], 0)
-    lse = jnp.log(jnp.sum(stats[:, 1] * jnp.exp(stats[:, 0] - ltop[None]), 0)) + ltop
-    picked = jnp.sum(stats[:, 2], 0)
-    loss_sum = lax.psum(jnp.sum(jnp.where(all_counted.reshape(tokens) > 0, lse - picked, 0.0)), "rep")
-    weight_t = all_counted.reshape(tokens) * (1.0 / token_count)
-    soft = jnp.exp(logits - lse[:, None])
-    grad_logits = ((soft - onehot.astype(F32)) * weight_t[:, None]).astype(BF)
-    grad_normed3 = dot("tv,vd->td", grad_logits, head_b).astype(BF).reshape(images, length, width)
-    grad_normed3 = lax.psum_scatter(grad_normed3, "fsdp", scatter_dimension=0, tiled=True)
-    grad_normed3 = grad_normed3.astype(F32)
-    grad_head = dot("tv,td->vd", grad_logits, normed3_all)
+    in_kernel = reps == 2 and size_of(head_scratch(n, length, width, own_rows, reps)[0]) < 52 * 2**20
+    if in_kernel:
+        grad_normed3, grad_head, totals = head_phase(normed3[0], head_b, every_fact, reps, n)
+        grad_normed3 = grad_normed3[None]
+        loss_sum, token_count = totals[0, 0], totals[1, 0]
+        grad_head = grad_head.astype(F32) + lax.ppermute(grad_head, "rep", [(0, 1), (1, 0)]).astype(F32)
+    else:
+        token_count = lax.psum(jnp.sum(all_counted), "rep")
+        normed3_all = lax.all_gather(normed3, "fsdp", axis=0, tiled=True).reshape(tokens, width)
+        logits = dot("td,vd->tv", normed3_all, head_b)
+        onehot = all_codes.reshape(tokens)[:, None] == own_ids[None, :]
+        local_top = jnp.max(logits, -1)
+        local_sum = jnp.sum(jnp.exp(logits - local_top[:, None]), -1)
+        local_pick = jnp.sum(jnp.where(onehot, logits, 0.0), -1)
+        stats = lax.all_gather(jnp.stack([local_top, local_sum, local_pick]), "fsdp", axis=0)
+        ltop = jnp.max(stats[:, 0], 0)
+        lse = jnp.log(jnp.sum(stats[:, 1] * jnp.exp(stats[:, 0] - ltop[None]), 0)) + ltop
+        picked = jnp.sum(stats[:, 2], 0)
+        loss_sum = lax.psum(jnp.sum(jnp.where(all_counted.reshape(tokens) > 0, lse - picked, 0.0)), "rep")
+        weight_t = all_counted.reshape(tokens) * (1.0 / token_count)
+        soft = jnp.exp(logits - lse[:, None])
+        grad_logits = ((soft - onehot.astype(F32)) * weight_t[:, None]).astype(BF)
+        grad_normed3 = dot("tv,vd->td", grad_logits, head_b).astype(BF).reshape(images, length, width)
+        grad_normed3 = lax.psum_scatter(grad_normed3, "fsdp", scatter_dimension=0, tiled=True)
+        grad_normed3 = grad_normed3.astype(F32)
+        grad_head = dot("tv,td->vd", grad_logits, normed3_all)
 
     grad_stream2, gain_three = norm_backward(stream2, inverse3, gains32[2], grad_normed3)
     grad_branch = grad_stream2.astype(BF)
@@ -474,29 +1116,56 @@
     grad_first, gain_one = norm_backward(stream0, inverse1, gains32[0], grad_normed1)
     grad_stream0 = grad_stream1 + grad_first
 
-    blocks = [
-        g.astype(BF).reshape(n, -1, g.shape[-1]) for g in (grad_qkv, grad_gate_up, grad_out, grad_down)
-    ]
-    layer_part = lax.psum_scatter(pack_rows(*blocks), "fsdp", scatter_dimension=0, tiled=False)
-    rows_all = lax.all_gather(grad_stream0.astype(BF), "fsdp", axis=0, tiled=True)
-    grad_codes = dot("tv,td->vd", lookup, rows_all.reshape(tokens, width))
-    class_part = lax.dynamic_slice(rows_all[:, 0], (0, me * own_width), (images, own_width))
-    class_spot = (all_classes[:, None] == jnp.arange(table_rows)[None, :]).astype(BF)
-    grad_classes = dot("iv,id->vd", class_spot, class_part)
-    summed = lax.psum(
-        (grad_codes.astype(BF), grad_head.astype(BF), layer_part, grad_classes), "rep"
-    )
-    grad_codes, grad_head, layer_part, grad_classes = (s.astype(F32) for s in summed)
-    grad_gains = lax.psum(jnp.stack([gain_one, gain_two, gain_three]), ("fsdp", "rep"))
-    grad_gains = lax.dynamic_slice(grad_gains, (0, me * own_width), (3, own_width))
-    grad_qkv, grad_gate_up, grad_out, grad_down = unpack_rows(layer_part, rows, hidden_width)
+    grad_gains = jnp.stack([gain_one, gain_two, gain_three])
+    if in_kernel:
+        gain_blocks = jnp.pad(
+            grad_gains.reshape(3, n, own_width).transpose(1, 0, 2).astype(BF),
+            ((0, 0), (0, 13), (0, 128 - own_width)),
+        )
+        blocks = [
+            g.astype(BF).reshape(n, -1, g.shape[-1])
+            for g in (grad_gate_up, grad_qkv, grad_out, grad_down)
+        ]
+        sums, grad_codes, first_rows = tail_phase(
+            grad_stream0[0].astype(BF),
+            every_fact,
+            blocks + [gain_blocks],
+            (True, False, False, False, False),
+            own_rows,
+            n,
+        )
+        grad_gate_up, grad_qkv, grad_out, grad_down, gain_part = sums
+        grad_gains = gain_part[:3, :own_width]
+        class_part = lax.dynamic_slice(
+            first_rows[:, :, 0].reshape(-1, width), (0, me * own_width), (reps * n, own_width)
+        )
+        every_class = every_fact[:, :, 4, 0].reshape(-1).astype(jnp.int32)
+        class_spot = (every_class[:, None] == jnp.arange(table_rows)[None, :]).astype(BF)
+        grad_classes = dot("iv,id->vd", class_spot, class_part.astype(BF))
+    else:
+        blocks = [
+            g.astype(BF).reshape(n, -1, g.shape[-1]) for g in (grad_qkv, grad_gate_up, grad_out, grad_down)
+        ]
+        layer_part = lax.psum_scatter(pack_rows(*blocks), "fsdp", scatter_dimension=0, tiled=False)
+        rows_all = lax.all_gather(grad_stream0.astype(BF), "fsdp", axis=0, tiled=True)
+        grad_codes = dot("tv,td->vd", lookup, rows_all.reshape(tokens, width))
+        class_part = lax.dynamic_slice(rows_all[:, 0], (0, me * own_width), (images, own_width))
+        class_spot = (all_classes[:, None] == jnp.arange(table_rows)[None, :]).astype(BF)
+        grad_classes = dot("iv,id->vd", class_spot, class_part)
+        summed = lax.psum(
+            (grad_codes.astype(BF), grad_head.astype(BF), layer_part, grad_classes), "rep"
+        )
+        grad_codes, grad_head, layer_part, grad_classes = (s.astype(F32) for s in summed)
+        grad_gains = lax.psum(grad_gains, ("fsdp", "rep"))
+        grad_gains = lax.dynamic_slice(grad_gains, (0, me * own_width), (3, own_width))
+        grad_qkv, grad_gate_up, grad_out, grad_down = unpack_rows(layer_part, rows, hidden_width)
     reduced = (
         grad_codes, grad_classes, grad_qkv, grad_out, grad_gate_up, grad_down, grad_head, grad_gains
     )
     squares = jnp.zeros((), F32)
     for grad_piece in reduced:
         squares = squares + jnp.sum(grad_piece * grad_piece)
-    grad_norm = jnp.sqrt(lax.psum(squares, "fsdp"))
+    grad_norm = jnp.sqrt(sum_over_fsdp(squares, n))
     factor = jnp.minimum(1.0, 1.0 / CLIP_INV / (grad_norm + 1e-06))
     results = [loss_sum, token_count, grad_norm]
     for index in range(8):

time: 849 us -> 564 us (0.66)
  waiting for transfers between devices: 412 us -> 0.01 us
  Pallas kernels: 115 us -> 423 us
  blocking collectives: 112 us -> 0 us
  matrix products: 73.4 us -> 40.9 us
  between operations: 25.4 us -> 11.3 us
  other arithmetic: 70.1 us -> 57.9 us
  local copies, waits for them, and re-layouts: 31 us -> 21.4 us
    pallas_call x0 -> x3, Pallas kernels: none -> 309 us  [the longest x1 178 us: tail_phase(): pl.pallas_call(functools.partial(tail_kernel, z_size, y_size, split, tupl...]
    reduce_scatter x2 -> x0, waiting for transfers between devices: 223 us -> none  [the longest x1 139 us: local(): lax.psum_scatter(pack_rows(*blocks), 'fsdp', scatter_dimension=0, tiled=F...]
    all_gather x2 -> x0, waiting for transfers between devices: 98.4 us -> none  [the longest x1 66.4 us: local(): lax.all_gather(normed3, 'fsdp', axis=0, tiled=True).reshape(tokens, width)]
    psum x2 -> x0, waiting for transfers between devices: 91.1 us -> none  [local(): lax.psum((grad_codes.astype(BF), grad_head.astype(BF), layer_part, grad_c...]
    psum x3 -> x0, blocking collectives: 79.1 us -> none  [the longest x1 39.9 us: local(): lax.psum(jnp.stack([gain_one, gain_two, gain_three]), ('fsdp', 'rep'))]
    all_gather x1 -> x0, blocking collectives: 32.6 us -> none  [local(): lax.all_gather(jnp.stack([local_top, local_sum, local_pick]), 'fsdp', axi...]
    dot_general x22 -> x18, matrix products: 70.4 us -> 37.9 us  [dot(): return jnp.einsum(subscripts, left, right, preferred_element_type=F32)]
    unnamed x124 -> x141, local copies, waits for them, and re-layouts: 21.6 us -> 9.31 us
  transfers between devices with their start and end apart: 6 -> 1, of which waited for: 5 -> 0; matrix products, arithmetic and copies ran while one was open for 5% -> 9% of each run, Pallas kernels for 0% -> 32%
where the time goes in v3:
time: 564 us; the launch traced here: 555 us
  Pallas kernels  423 us (75%)
  other arithmetic  57.9 us (10%)
  matrix products  40.9 us (7%)
  local copies, waits for them, and re-layouts  21.4 us (4%)
  between operations  11.3 us (2%)
    pallas_call x1, Pallas kernels, tail_phase(): pl.pallas_call(functools.partial(tail_kernel, z_size, y_size, split, tupl...  178 us
    pallas_call x1, Pallas kernels, head_phase(): pl.pallas_call(functools.partial(head_kernel, z_size, y_size, reps), out_...  122 us
    pallas_call x1, Pallas kernels, front(): pl.pallas_call(functools.partial(front_kernel, z_size, y_size, reps, own_...  115 us
    dot_general x18, matrix products, dot(): return jnp.einsum(subscripts, left, right, preferred_element_type=F32)  37.9 us
    sub x8, other arithmetic, adam_update(): weight - rate * (first_hat / (jnp.sqrt(second_hat) + ADAM_EPS) + decay *...  20.1 us
    reduce_sum x7, other arithmetic, local(): squares = squares + jnp.sum(grad_piece * grad_piece)  13.1 us
  transfers between devices with their start and end apart: 1, of which 0 were waited for; matrix products, arithmetic and copies ran while one was open for 9% of the time, Pallas kernels for 32%

profile of v3, /device:TPU:0, one launch (start us, length us, event | category | flops | bytes accessed | tf_op | source)
XLA Modules:
  0.0 555.1 jit_solution(6317730085160756995)
XLA Ops:
  4.7 3.3 convert_element_type.176.code_b
  12.5 114.8 %front.1 = (bf16[16,256,768]{2,1,0:T(8,128)(2,1)}, bf16[16,144,768]{2,1,0:T(8,128)(2,1)}, bf16[16,48,768]{2,1,0:T(8,128)(2,1)}, bf16[16,48,2048]{2,1,0:T(8,128)(...) custom-call(f32[8,128]{1,0:T(8,128)} %fusion.39.facts, bf16[1024,768]{1,0:T(8,128)(2,1)} %convert_element_type.176.code_b, ...), custom_call_target="tpu_custom_call" | custom-call | tf_op jit(solution)/shard_map/front/pallas_call | solution.py:302
  130.5 3.4 convolution_bitcast_fusion.1
  137.7 2.9 fusion.61
  140.7 1.9 convolution_convert_fusion.6
  145.7 1.8 convolution_bitcast_fusion
  147.5 2.1 copy-done
  149.6 1.6 multiply_convert_fusion.3
  152.1 3.5 multiply_reduce_fusion.10
  157.9 122.5 %head.1 = (f32[256,768]{1,0:T(8,128)}, bf16[1024,768]{1,0:T(8,128)(2,1)}, f32[8,128]{1,0:T(8,128)}) custom-call(bf16[256,768]{1,0:T(8,128)(2,1)} %multiply_convert_fusion.4.normed3, bf16[1024,768]{1,0:T(8,128)(2,1)} %convert_element_type.193.head_b, f32[2,16,8,128]{3,2,1,0:T(8,128)} %get-tuple-element.44.facts), custom_call_target="tpu_custom_call" | custom-call | tf_op jit(solution)/shard_map/head/pallas_call | solution.py:696
  280.5 2.3 multiply_reduce_fusion.4
  282.9 1.5 multiply_subtract_fusion.3
  284.4 4.0 fusion.12
  288.5 2.4 multiply_reduce_fusion.5
  292.9 2.6 convolution_convert_fusion.4
  297.3 4.6 convolution_convert_fusion
  306.3 1.8 multiply_reduce_fusion.6
  308.2 3.2 convolution_convert_fusion.1
  311.4 2.7 convolution_convert_fusion.2
  318.1 1.5 convolution_convert_fusion.3
  319.7 177.8 %tail.1 = (f32[256,768]{1,0:T(8,128)}, f32[144,768]{1,0:T(8,128)}, f32[48,768]{1,0:T(8,128)}, f32[48,2048]{1,0:T(8,128)}, f32[16,128]{1,0:T(8,128)}, /*index=5*/f32[1024,768]{1,0:T(8,128)}, f32[2,16,8,768]{3,2,1,0:T(8,128)}) custom-call(bf16[256,768]{1,0:T(8,128)(2,1)} %add_convert_fusion.grad_stream0, f32[2,16,8,128]{3,2,1,0:T(8,128)} %get-tuple-element.44.facts, ...), custom_call_target="tpu_custom_call" | custom-call | tf_op jit(solution)/shard_map/tail/pallas_call | solution.py:914
  498.8 1.6 convert_reduce_fusion
  500.4 1.6 multiply_reduce_fusion.15
  502.0 3.3 multiply_reduce_fusion.1
  506.9 1.7 multiply_reduce_fusion.13
  509.3 1.6 multiply_reduce_fusion.16
  511.5 1.9 multiply_reduce_fusion.3
  517.4 3.3 multiply_reduce_fusion
  522.6 8.3 %norm.1 = f32[8,128]{1,0:T(8,128)} custom-call(f32[8,128]{1,0:T(8,128)} %broadcast_in_dim.14.squares), custom_call_target="tpu_custom_call" | custom-call | tf_op jit(solution)/shard_map/norm/pallas_call | solution.py:947
  532.9 7.3 %multiply_subtract_fusion.1 = (f32[1024,768]{1,0:T(8,128)}, f32[1024,768]{1,0:T(8,128)}, f32[1024,768]{1,0:T(8,128)}) fusion(f32[1024,768]{1,0:T(8,128)S(1)} %copy-done.1, f32[1024,768]{1,0:T(8,128)} %get-tuple-element.51, f32[]{:T(128)S(6)} %min.3, f32[1024,768]{1,0:T(8,128)} %param.33, f32[1024,768]{1,0:T(8,128)} %param.34), kind=kLoop, calls=%fused_computation.13 | loop fusion | flops 11796480 | bytes 22020100 | tf_op jit(solution)/shard_map/sub | solution.py:963
  542.6 1.9 multiply_subtract_fusion.2
  547.5 6.0 %multiply_subtract_fusion = (f32[1024,768]{1,0:T(8,128)}, f32[1024,768]{1,0:T(8,128)}, f32[1024,768]{1,0:T(8,128)}) fusion(f32[1024,768]{1,0:T(8,128)S(1)} %copy-done.3, f32[]{:T(128)S(6)} %min.3, bf16[1024,768]{1,0:T(8,128)(2,1)} %collective-permute-done, bf16[1024,768]{1,0:T(8,128)(2,1)S(1)} %copy-done.10, f32[1024,768]{1,0:T(8,128)S(1)} %copy-done.15, ...), kind=kLoop, calls=%fused_computation.12 | loop fusion | flops 14155776 | bytes 22020100 | tf_op jit(solution)/shard_map/sub | solution.py:963
  (212 shorter events, 42.9 us)
Async XLA Ops:
  0.7 7.3 %copy-start.31 = (f32[1001,48]{0,1:T(8,128)S(1)}, f32[1001,48]{0,1:T(8,128)}, u32[]{:S(2)}) copy-start(f32[1001,48]{0,1:T(8,128)} %param.35) | copy-start | bytes 576580
  0.7 7.5 %copy-start.19 = (f32[256,768]{1,0:T(8,128)S(1)}, f32[256,768]{1,0:T(8,128)}, u32[]{:S(2)}) copy-start(f32[256,768]{1,0:T(8,128)} %param.44) | copy-start | bytes 2359300
  4.7 4.3 copy-start.22
  4.7 5.0 copy-start.36
  4.7 5.7 %copy-start.25 = (f32[48,2048]{1,0:T(8,128)S(1)}, f32[48,2048]{1,0:T(8,128)}, u32[]{:S(2)}) copy-start(f32[48,2048]{1,0:T(8,128)} %param.47) | copy-start | bytes 1179652
  4.7 6.4 %copy-start.57 = (s32[1,256]{1,0:T(1,128)S(1)}, s32[1,256]{1,0:T(1,128)}, u32[]{:S(2)}) copy-start(s32[1,256]{1,0:T(1,128)} %param.30) | copy-start | bytes 3076
  140.7 4.0 slice-start
  140.7 5.0 slice-start.1
  151.2 4.5 copy-start.2
  157.9 124.9 %copy-start.9 = (f32[256,768]{1,0:T(8,128)S(1)}, f32[256,768]{1,0:T(8,128)}, u32[]{:S(2)}) copy-start(f32[256,768]{1,0:T(8,128)} %copy-done.8) | copy-start | bytes 2359300
  157.9 124.9 %copy-start.54 = (f32[256]{0:T(256)S(1)}, f32[256]{0:T(256)}, u32[]{:S(2)}) copy-start(f32[256]{0:T(256)} %copy-done.53) | copy-start | bytes 3076
  280.5 236.9 %collective-permute-start = (bf16[1024,768]{1,0:T(8,128)(2,1)}, bf16[1024,768]{1,0:T(8,128)(2,1)}, u32[]{:S(2)}, u32[]{:S(2)}) collective-permute-start(bf16[1024,768]{1,0:T(8,128)(2,1)} %get-tuple-element.57), channel_id=1, source_target_pairs={{0,1},{1,0},{2,3},{3,2},{4,5},{5,4},{6,7},{7,6},{8,9},{9,8},{10,11... | collective-permute-start | bytes 4718600 | tf_op jit(solution)/shard_map/ppermute | solution.py:1062
  282.9 5.6 %slice-start.2 = ((s8[6291456]{0:T(1024)(128)(4,1)}), s8[4194304]{0:T(1024)(128)(4,1)S(1)}, s32[]{:S(2)}) async-start(s8[6291456]{0:T(1024)(128)(4,1)} %bitcast.103), calls=%async_computation.2 | async-start | bytes 8388608
  284.4 4.0 slice-start.3
  284.4 4.0 copy-start.7
  497.5 16.6 %copy-start.27 = (f32[48,2048]{1,0:T(8,128)S(1)}, f32[48,2048]{1,0:T(8,128)}, u32[]{:S(2)}) copy-start(f32[48,2048]{1,0:T(8,128)} %get-tuple-element.56) | copy-start | bytes 1179652
  497.5 18.0 %copy-start.58 = (f32[16,128]{1,0:T(8,128)S(1)}, f32[16,128]{1,0:T(8,128)}, u32[]{:S(2)}) copy-start(f32[16,128]{1,0:T(8,128)} %get-tuple-element.58) | copy-start | bytes 24580
  505.3 27.4 %copy-start.1 = (f32[1024,768]{1,0:T(8,128)S(1)}, f32[1024,768]{1,0:T(8,128)}, u32[]{:S(2)}) copy-start(f32[1024,768]{1,0:T(8,128)} %param.32) | copy-start | bytes 9437188
  532.8 7.5 %copy-start.23 = (f32[144,768]{1,0:T(8,128)S(1)}, f32[144,768]{1,0:T(8,128)}, u32[]{:S(2)}) copy-start(f32[144,768]{1,0:T(8,128)} %param.38) | copy-start | bytes 1327108
  532.8 7.5 %copy-start.24 = (f32[144,768]{1,0:T(8,128)S(1)}, f32[144,768]{1,0:T(8,128)}, u32[]{:S(2)}) copy-start(f32[144,768]{1,0:T(8,128)} %get-tuple-element.53) | copy-start | bytes 1327108
  532.8 7.4 %copy-start.39 = (f32[144,768]{1,0:T(8,128)S(1)}, f32[144,768]{1,0:T(8,128)}, u32[]{:S(2)}) copy-start(f32[144,768]{1,0:T(8,128)} %param.39) | copy-start | bytes 1327108
  532.8 7.4 %copy-start.40 = (f32[144,768]{1,0:T(8,128)S(1)}, f32[144,768]{1,0:T(8,128)}, u32[]{:S(2)}) copy-start(f32[144,768]{1,0:T(8,128)} %param.40) | copy-start | bytes 1327108
  532.8 8.8 %copy-start.37 = (f32[48,768]{1,0:T(8,128)S(1)}, f32[48,768]{1,0:T(8,128)}, u32[]{:S(2)}) copy-start(f32[48,768]{1,0:T(8,128)} %param.41) | copy-start | bytes 442372
  532.8 8.8 %copy-start.38 = (f32[48,768]{1,0:T(8,128)S(1)}, f32[48,768]{1,0:T(8,128)}, u32[]{:S(2)}) copy-start(f32[48,768]{1,0:T(8,128)} %get-tuple-element.54) | copy-start | bytes 442372
  532.8 8.8 %copy-start.48 = (f32[48,768]{1,0:T(8,128)S(1)}, f32[48,768]{1,0:T(8,128)}, u32[]{:S(2)}) copy-start(f32[48,768]{1,0:T(8,128)} %param.42) | copy-start | bytes 442372
  532.8 8.7 %copy-start.49 = (f32[48,768]{1,0:T(8,128)S(1)}, f32[48,768]{1,0:T(8,128)}, u32[]{:S(2)}) copy-start(f32[48,768]{1,0:T(8,128)} %param.43) | copy-start | bytes 442372
  532.9 9.6 %copy-start.21 = (f32[256,768]{1,0:T(8,128)S(1)}, f32[256,768]{1,0:T(8,128)}, u32[]{:S(2)}) copy-start(f32[256,768]{1,0:T(8,128)} %get-tuple-element.55) | copy-start | bytes 2359300
  532.9 9.6 %copy-start.34 = (f32[256,768]{1,0:T(8,128)S(1)}, f32[256,768]{1,0:T(8,128)}, u32[]{:S(2)}) copy-start(f32[256,768]{1,0:T(8,128)} %param.45) | copy-start | bytes 2359300
  532.9 9.6 %copy-start.35 = (f32[256,768]{1,0:T(8,128)S(1)}, f32[256,768]{1,0:T(8,128)}, u32[]{:S(2)}) copy-start(f32[256,768]{1,0:T(8,128)} %param.46) | copy-start | bytes 2359300
  540.3 7.0 %copy-start.16 = (f32[1024,768]{1,0:T(8,128)S(1)}, f32[1024,768]{1,0:T(8,128)}, u32[]{:S(2)}) copy-start(f32[1024,768]{1,0:T(8,128)} %param.52) | copy-start | bytes 9437188
  542.6 4.7 copy-start.10
  542.6 4.7 copy-start.15
  (39 other events, 100.9 us)

commit v4 on v3

--- a/solution.py
+++ b/solution.py
@@ -121,191 +121,39 @@
     pltpu.make_async_copy(src, src, sems.at[(0,) + index]).wait()
 
 
-def front_kernel(z_size, y_size, reps, own_width, parts, facts, code_b, class_b, *refs):
-    count = len(parts)
-    weights, refs = refs[:count], refs[count:]
-    wholes, refs = refs[:count], refs[count:]
-    (stream, facts_all, turned, acc, core_out, core_in, y_in, z_in,
-     fact_sems, rep_sems, z_sems, y_sems, x_sems, c_sems, own_sems, rc_sems, ry_sems, rz_sems) = refs
-    n = z_size * y_size * 2
-    me, z, y, core = where_am_i(z_size, y_size)
-    x = lax.axis_index("rep")
-    length = stream.shape[0]
-    width = stream.shape[1]
-    own_rows = code_b.shape[0]
-
-    def at(dz, dy, other=0):
-        c = 1 - core if other else core
-        return (lax.rem(z + dz, z_size) * y_size + lax.rem(y + dy, y_size)) * 2 + c
-
-    barrier = pltpu.get_barrier_semaphore()
-    for k in range(1, n):
-        pl.semaphore_signal(barrier, inc=1, device_id=(lax.rem(me + k, n), x), device_id_type=MESH)
-    for k in range(1, reps):
-        pl.semaphore_signal(barrier, inc=1, device_id=(me, lax.rem(x + k, reps)), device_id_type=MESH)
-    pl.semaphore_wait(barrier, n - 1 + reps - 1)
-
-    for k in range(1, n):
-        send(facts, facts_all.at[x, me], fact_sems, (k,), (lax.rem(me + k, n), x))
-    facts_all[x, me] = facts[...]
-
-    peers_z = [(dz, at(dz, 0)) for dz in range(1, z_size)]
-    peers_y = [(dy, at(0, dy)) for dy in range(1, y_size)]
-    spots = [(dz, dy) for dz in range(z_size) for dy in range(y_size)]
-    for k, part in enumerate(parts):
-        pltpu.make_async_copy(weights[k], wholes[k].at[me], own_sems.at[k]).start()
-
-        @pl.when(x == part)
-        def _():
-            for dz, peer in peers_z:
-                send(weights[k], wholes[k].at[me], z_sems, (k, dz), (peer, x))
-            for dy, peer in peers_y:
-                send(weights[k], wholes[k].at[me], y_sems, (k, 0, dy), (peer, x))
-
-        send(weights[k], wholes[k].at[me], c_sems, (k, 0, 0), (at(0, 0, 1), x))
-
-    def to_others(k, dz, dy):
-        block = wholes[k].at[at(dz, dy)]
-        for dx in range(1, reps):
-            send(block, block, x_sems, (k, dz, dy, dx), (me, lax.rem(x + dx, reps)))
-        send(block, block, c_sems, (k, dz, dy), (at(0, 0, 1), x))
-
-    def after_z(dz):
-        for k, part in enumerate(parts):
-
-            @pl.when(x == part)
-            def _():
-                block = wholes[k].at[at(z_size - dz, 0)]
-                arrival(block, z_sems, (k, dz))
-                for dy, peer in peers_y:
-                    send(block, block, y_sems, (k, z_size - dz, dy), (peer, x))
-                to_others(k, z_size - dz, 0)
-
-    def after_y(dz, dy):
-        for k, part in enumerate(parts):
-
-            @pl.when(x == part)
-            def _():
-                arrival(wholes[k].at[at(dz, y_size - dy)], y_sems, (k, dz, dy))
-                to_others(k, dz, y_size - dy)
-
-    def after_x(dz, dy):
-        for k, part in enumerate(parts):
-
-            @pl.when(x != part)
-            def _():
-                block = wholes[k].at[at(dz, dy)]
-                arrival(block, x_sems, (k, dz, dy, lax.rem(x - part + reps, reps)))
-                send(block, block, c_sems, (k, dz, dy), (at(0, 0, 1), x))
-
-    for k in range(1, n):
-        arrival(facts_all.at[x, lax.rem(me - k + n, n)], fact_sems, (k,))
-    for k in range(1, reps):
-        send(facts_all.at[x], facts_all.at[x], rep_sems, (k,), (me, lax.rem(x + k, reps)))
-    turned[...] = jnp.transpose(facts_all[x].reshape(n * 8, 128))
-    lane = lax.broadcasted_iota(jnp.int32, (128, n * 8), 1)
-    class_rows = class_b[...].astype(F32)
-    class_iota = lax.broadcasted_iota(jnp.int32, class_rows.shape, 0).astype(F32)
-    row_iota = lax.broadcasted_iota(jnp.int32, (length // 2, own_rows), 1) + me * own_rows
-    row_iota = row_iota.astype(F32)
-
-    def found(image, out):
-        cls = jnp.sum(jnp.where(lane[:1] == image * 8 + 4, turned[:1, :], 0.0), -1, keepdims=True)
-        row = jnp.sum(jnp.where(class_iota == cls, class_rows, 0.0), 0, keepdims=True)
-        row = jnp.concatenate([row, jnp.zeros((1, width - row.shape[1]), F32)], -1)
-        row = pltpu.roll(jnp.broadcast_to(row, (8, width)), me * own_width, 1)
-        for half in range(2):
-            ids = jnp.sum(jnp.where(lane == image * 8 + half, turned[...], 0.0), -1, keepdims=True)
-            spot = jnp.where(row_iota == ids, 1.0, 0.0).astype(BF)
-            rows = jnp.dot(spot, code_b[...], preferred_element_type=F32)
-            out[pl.ds(half * (length // 2), length // 2)] = rows.astype(BF)
-            if half == 0:
-                first = lax.broadcasted_iota(jnp.int32, (16, width), 0) == 0
-                head = jnp.where(first, jnp.concatenate([row, row], 0), rows[:16])
-                out[pl.ds(0, 16)] = head.astype(BF)
-
-    order = [(dz, dy) for dz in range(z_size - 1, -1, -1) for dy in range(y_size - 1, -1, -1)]
-    for dz, dy in order:
-        slot = dz * y_size + dy
-        found(at(dz, dy, 1), core_out.at[slot])
-        send(core_out.at[slot], core_in.at[slot], rc_sems, (slot,), (at(0, 0, 1), x))
-        found(at(dz, dy), acc.at[slot])
-    for dz, dy in order:
-        slot = dz * y_size + dy
-        arrival(core_in.at[slot], rc_sems, (slot,))
-        acc[slot] = (acc[slot].astype(F32) + core_in[slot].astype(F32)).astype(BF)
-        if dy:
-            send(acc.at[slot], y_in.at[dz, dy], ry_sems, (dz, dy), (at(0, dy), x))
-    for dz in range(1, z_size):
-        after_z(dz)
-    for dy in range(1, y_size):
-        after_y(0, dy)
-    for dz in range(z_size - 1, -1, -1):
-        slot = dz * y_size
-        total = acc[slot].astype(F32)
-        for dy in range(1, y_size):
-            arrival(y_in.at[dz, dy], ry_sems, (dz, dy))
-            total = total + y_in[dz, dy].astype(F32)
-        acc[slot] = total.astype(BF)
-        if dz:
-            send(acc.at[slot], z_in.at[dz], rz_sems, (dz,), (at(dz, 0), x))
-    for dz in range(z_size - 1, 0, -1):
-        for dy in range(1, y_size):
-            after_y(dz, dy)
-    total = acc[0].astype(F32)
-    for dz in range(1, z_size):
-        arrival(z_in.at[dz], rz_sems, (dz,))
-        total = total + z_in[dz].astype(F32)
-    stream[...] = total
-    for dz, dy in spots[1:]:
-        after_x(dz, dy)
-
-    for k in range(1, reps):
-        arrival(facts_all.at[x], rep_sems, (k,))
-        departure(facts_all.at[x], rep_sems, (k,))
-
-    for k in range(1, n):
-        departure(facts, fact_sems, (k,))
-    for dz, dy in spots:
-        slot = dz * y_size + dy
-        departure(core_out.at[slot], rc_sems, (slot,))
-        if dy:
-            departure(acc.at[slot], ry_sems, (dz, dy))
-        elif dz:
-            departure(acc.at[slot], rz_sems, (dz,))
-    for k, part in enumerate(parts):
-        pltpu.make_async_copy(weights[k], wholes[k].at[me], own_sems.at[k]).wait()
-        for dz, dy in spots:
-            arrival(wholes[k].at[at(dz, dy, 1)], c_sems, (k, dz, dy))
-            departure(weights[k], c_sems, (k, dz, dy))
-
-        @pl.when(x == part)
-        def _():
-            for dz in range(1, z_size):
-                departure(weights[k], z_sems, (k, dz))
-            for dz, dy in spots:
-                if dy:
-                    departure(weights[k], y_sems, (k, dz, dy))
-                if dz or dy:
-                    for dx in range(1, reps):
-                        departure(weights[k], x_sems, (k, dz, dy, dx))
-
-
-def front(facts, code_b, class_b, weights, parts, own_width, length, reps, n):
+def weight_pieces(rows, reps):
+    gate = rows[0]
+    cut = gate * 15 // 16 // 16 * 16
+    middle = cut // 2 // 16 * 16
+    one = 1 % reps
+    return (
+        (2, 0, rows[2], 2 % reps),
+        (0, cut, gate - cut, one),
+        (0, 0, middle, 0),
+        (3, 0, rows[3], 3 % reps),
+        (0, middle, cut - middle, 0),
+        (1, 0, rows[1], one),
+    )
+
+
+def front(facts, code_table, class_b, weights, own_width, length, reps, n):
     z_size, y_size = geometry(n)
-    width = code_b.shape[1]
+    width = code_table.shape[1]
     count = len(weights)
+    pieces = weight_pieces([w.shape[0] for w in weights], reps)
+    many = len(pieces)
     spots = z_size * y_size
     block = (length, width)
     vmem, hbm = pl.BlockSpec(memory_space=pltpu.VMEM), pl.BlockSpec(memory_space=pl.ANY)
     dma = pltpu.SemaphoreType.DMA
     outs = pl.pallas_call(
-        functools.partial(front_kernel, z_size, y_size, reps, own_width, parts),
-        out_shape=[jax.ShapeDtypeStruct((n,) + w.shape, w.dtype) for w in weights]
+        functools.partial(front_kernel, z_size, y_size, reps, own_width, pieces, count),
+        out_shape=[jax.ShapeDtypeStruct((n,) + w.shape, BF) for w in weights]
         + [jax.ShapeDtypeStruct(block, F32), jax.ShapeDtypeStruct((reps, n, 8, 128), F32)],
-        in_specs=[vmem] * 3 + [hbm] * count,
+        in_specs=[vmem] * (3 + count),
         out_specs=[hbm] * count + [vmem] * 2,
         scratch_shapes=[
+            pltpu.VMEM(code_table.shape, BF),
             pltpu.VMEM((128, n * 8), F32),
             pltpu.VMEM((spots,) + block, BF),
             pltpu.VMEM((spots,) + block, BF),
@@ -314,20 +162,21 @@
             pltpu.VMEM((z_size,) + block, BF),
             dma((2, n)),
             dma((2, reps)),
-            dma((2, count, z_size)),
-            dma((2, count, z_size, y_size)),
-            dma((2, count, z_size, y_size, reps)),
-            dma((2, count, z_size, y_size)),
+            dma((2, many, 2, z_size)),
+            dma((2, many, z_size, y_size)),
+            dma((2, many, z_size, y_size, reps)),
+            dma((2, many, z_size, y_size)),
             dma((count,)),
             dma((2, spots)),
             dma((2, z_size, y_size)),
             dma((2, z_size)),
-        ],
+        ]
+        + [pltpu.VMEM(w.shape, BF) for w in weights],
         compiler_params=pltpu.CompilerParams(
             collective_id=0, has_side_effects=True, vmem_limit_bytes=60 * 2**20
         ),
         name="front",
-    )(facts, code_b, class_b, *weights)
+    )(facts, code_table, class_b, *weights)
     return outs[:count], outs[count], outs[count + 1]
 
 
@@ -365,12 +214,26 @@
 
 
 class Spread:
-    def __init__(self, place, whole, z_sems, y_sems, c_sems):
-        self.p, self.whole = place, whole
-        self.z_sems, self.y_sems, self.c_sems = z_sems, y_sems, c_sems
+    def __init__(self, place, whole, z_sems, y_sems, c_sems, x_sems=None, part=None, rows=None):
+        self.p, self.whole, self.part, self.rows = place, whole, part, rows
+        self.z_sems, self.y_sems, self.c_sems, self.x_sems = z_sems, y_sems, c_sems, x_sems
 
     def block(self, z, dy=0, other=0):
-        return self.whole.at[self.p.plane(z, dy, other)]
+        block = self.whole.at[self.p.plane(z, dy, other)]
+        return block if self.rows is None else block.at[pl.ds(*self.rows)]
+
+    def in_part(self, act):
+        if self.part is None:
+            act()
+        else:
+            pl.when(self.p.x == self.part)(act)
+
+    def hand_over(self, z, dy, src, dst):
+        p = self.p
+        if self.part is not None:
+            for dx in range(1, p.reps):
+                send(src, dst, self.x_sems, (z, dy, dx), (p.me, lax.rem(p.x + dx, p.reps)))
+        send(src, dst, self.c_sems, (z, dy), p.twin())
 
     def pass_on(self, z, src, up, down):
         p = self.p
@@ -389,29 +252,64 @@
 
         for dy in range(1, p.y_size):
             send(src, dst, self.y_sems, (z, dy), (p.at(0, dy), p.x))
-        send(src, dst, self.c_sems, (z, 0), p.twin())
 
     def start(self, own):
-        self.pass_on(self.p.z, own, True, True)
+        self.in_part(lambda: self.pass_on(self.p.z, own, True, True))
+        send(own, self.block(self.p.z), self.c_sems, (self.p.z, 0), self.p.twin())
+
+    def near(self, s, act):
+        p = self.p
+        if s == 0:
+            act(p.z)
+            return
+
+        @pl.when(p.z - s >= 0)
+        def _():
+            act(p.z - s)
+
+        @pl.when(p.z + s < p.z_size)
+        def _():
+            act(p.z + s)
 
     def step_z(self, s):
         p = self.p
 
-        @pl.when(p.z - s >= 0)
-        def _():
-            arrival(self.block(p.z - s), self.z_sems, (0, p.z - s))
-            self.pass_on(p.z - s, self.block(p.z - s), True, False)
-
-        @pl.when(p.z + s < p.z_size)
-        def _():
-            arrival(self.block(p.z + s), self.z_sems, (1, p.z + s))
-            self.pass_on(p.z + s, self.block(p.z + s), False, True)
-
-    def take_y(self, z):
-        for dy in range(1, self.p.y_size):
-            block = self.block(z, self.p.y_size - dy)
-            arrival(block, self.y_sems, (z, dy))
-            send(block, block, self.c_sems, (z, dy), self.p.twin())
+        def take(z, up):
+            block = self.block(z)
+            arrival(block, self.z_sems, (1 - int(up), z))
+            self.pass_on(z, block, up, not up)
+            self.hand_over(z, 0, block, block)
+
+        def act():
+            @pl.when(p.z - s >= 0)
+            def _():
+                take(p.z - s, True)
+
+            @pl.when(p.z + s < p.z_size)
+            def _():
+                take(p.z + s, False)
+
+        self.in_part(act)
+
+    def step_y(self, s):
+        def take(z):
+            for dy in range(1, self.p.y_size):
+                block = self.block(z, self.p.y_size - dy)
+                arrival(block, self.y_sems, (z, dy))
+                self.hand_over(z, dy, block, block)
+
+        self.in_part(lambda: self.near(s, take))
+
+    def step_x(self, s):
+        p = self.p
+
+        def take(z):
+            for dy in range(0 if s else 1, p.y_size):
+                block = self.block(z, p.y_size - dy)
+                arrival(block, self.x_sems, (z, dy, lax.rem(p.x - self.part + p.reps, p.reps)))
+                send(block, block, self.c_sems, (z, dy), p.twin())
+
+        pl.when(p.x != self.part)(lambda: self.near(s, take))
 
     def take_twin(self, z):
         for dy in range(self.p.y_size):
@@ -421,32 +319,180 @@
         p = self.p
         block = self.block(p.z)
         for z in range(p.z_size):
-
-            @pl.when(jnp.logical_and(p.z + 1 < p.z_size, z <= p.z))
-            def _():
-                departure(block, self.z_sems, (0, z))
-
-            @pl.when(jnp.logical_and(p.z >= 1, z >= p.z))
-            def _():
-                departure(block, self.z_sems, (1, z))
-
             for dy in range(p.y_size):
                 departure(block, self.c_sems, (z, dy))
-                if dy:
+
+        def act():
+            for z in range(p.z_size):
+
+                @pl.when(jnp.logical_and(p.z + 1 < p.z_size, z <= p.z))
+                def _():
+                    departure(block, self.z_sems, (0, z))
+
+                @pl.when(jnp.logical_and(p.z >= 1, z >= p.z))
+                def _():
+                    departure(block, self.z_sems, (1, z))
+
+                for dy in range(1, p.y_size):
                     departure(block, self.y_sems, (z, dy))
-
-
-def head_kernel(z_size, y_size, reps, normed3, head_b, facts, grad_normed3, grad_head, totals,
+                if self.part is None:
+                    continue
+                for dy in range(p.y_size):
+                    for dx in range(1, p.reps):
+                        if dy:
+                            departure(block, self.x_sems, (z, dy, dx))
+                        else:
+
+                            @pl.when(z != p.z)
+                            def _():
+                                departure(block, self.x_sems, (z, dy, dx))
+
+        self.in_part(act)
+
+
+def front_kernel(z_size, y_size, reps, own_width, pieces, count, facts, code_table, class_b, *refs):
+    masters, refs = refs[:count], refs[count:]
+    wholes, refs = refs[:count], refs[count:]
+    weights, refs = refs[-count:], refs[:-count]
+    (stream, facts_all, code_b, turned, acc, core_out, core_in, y_in, z_in,
+     fact_sems, rep_sems, z_sems, y_sems, x_sems, c_sems, own_sems, rc_sems, ry_sems, rz_sems) = refs
+    p = Place(z_size, y_size, reps)
+    n, me, x = p.n, p.me, p.x
+    length, width = stream.shape
+    own_rows = code_table.shape[0]
+    p.greet(True)
+
+    for k in range(1, n):
+        send(facts, facts_all.at[x, me], fact_sems, (k,), (lax.rem(me + k, n), x))
+    facts_all[x, me] = facts[...]
+    for k in range(count):
+        weights[k][...] = masters[k][...].astype(BF)
+    spreads = []
+    for i, (k, start, size, part) in enumerate(pieces):
+        sems = [group.at[:, i] for group in (z_sems, y_sems, c_sems, x_sems)]
+        spreads.append(Spread(p, wholes[k], *sems, part, (start, size)))
+        spreads[i].start(weights[k].at[pl.ds(start, size)])
+    for k in range(count):
+        pltpu.make_async_copy(weights[k], wholes[k].at[me], own_sems.at[k]).start()
+    code_b[...] = code_table[...].astype(BF)
+
+    for k in range(1, n):
+        arrival(facts_all.at[x, lax.rem(me - k + n, n)], fact_sems, (k,))
+    for k in range(1, reps):
+        send(facts_all.at[x], facts_all.at[x], rep_sems, (k,), (me, lax.rem(x + k, reps)))
+    turned[...] = jnp.transpose(facts_all[x].reshape(n * 8, 128))
+    lane = lax.broadcasted_iota(jnp.int32, (128, n * 8), 1)
+    class_iota = lax.broadcasted_iota(jnp.int32, (16, class_b.shape[1]), 1).astype(F32)
+    row_iota = lax.broadcasted_iota(jnp.int32, (length // 2, own_rows), 1) + me * own_rows
+    row_iota = row_iota.astype(F32)
+
+    def found(image, out):
+        cls = jnp.sum(jnp.where(lane[:1] == image * 8 + 4, turned[:1, :], 0.0), -1, keepdims=True)
+        spot = jnp.where(class_iota == cls, 1.0, 0.0).astype(BF)
+        row = lax.dot_general(
+            spot, class_b[...], (((1,), (1,)), ((), ())), preferred_element_type=F32
+        )
+        row = jnp.concatenate([row, jnp.zeros((16, width - row.shape[1]), F32)], -1)
+        row = pltpu.roll(row, me * own_width, 1)
+        for half in range(2):
+            ids = jnp.sum(jnp.where(lane == image * 8 + half, turned[...], 0.0), -1, keepdims=True)
+            spot = jnp.where(row_iota == ids, 1.0, 0.0).astype(BF)
+            rows = jnp.dot(spot, code_b[...], preferred_element_type=F32)
+            out[pl.ds(half * (length // 2), length // 2)] = rows.astype(BF)
+            if half == 0:
+                first = lax.broadcasted_iota(jnp.int32, (16, width), 0) == 0
+                head = jnp.where(first, row, rows[:16])
+                out[pl.ds(0, 16)] = head.astype(BF)
+
+    def look_up(dz):
+        def body(j, carry):
+            dy = y_size - 1 - j
+            slot = dz * y_size + dy
+            found(p.at(dz, dy, 1), core_out.at[slot])
+            send(core_out.at[slot], core_in.at[slot], rc_sems, (slot,), p.twin())
+            found(p.at(dz, dy), acc.at[slot])
+            return carry
+
+        lax.fori_loop(0, y_size, body, 0)
+
+    def twin_sum(dz):
+        for dy in range(y_size - 1, -1, -1):
+            slot = dz * y_size + dy
+            arrival(core_in.at[slot], rc_sems, (slot,))
+            acc[slot] = (acc[slot].astype(F32) + core_in[slot].astype(F32)).astype(BF)
+            if dy:
+                send(acc.at[slot], y_in.at[dz, dy], ry_sems, (dz, dy), (p.at(0, dy), x))
+
+    def y_sum(dz):
+        slot = dz * y_size
+        total = acc[slot].astype(F32)
+        for dy in range(1, y_size):
+            arrival(y_in.at[dz, dy], ry_sems, (dz, dy))
+            total = total + y_in[dz, dy].astype(F32)
+        acc[slot] = total.astype(BF)
+        if dz:
+            send(acc.at[slot], z_in.at[dz], rz_sems, (dz,), (p.at(dz, 0), x))
+
+    for s in range(1, z_size + 1):
+        for spread in spreads:
+            if s < z_size:
+                spread.step_z(s)
+        for spread in spreads:
+            spread.step_y(s - 1)
+        look_up(z_size - s)
+        if s >= 2:
+            twin_sum(z_size - s + 1)
+        if s >= 3:
+            y_sum(z_size - s + 2)
+    twin_sum(0)
+    for spread in spreads:
+        spread.step_x(0)
+    y_sum(1)
+    for s in range(1, z_size - 1):
+        for spread in spreads:
+            spread.step_x(s)
+    y_sum(0)
+    total = acc[0].astype(F32)
+    for dz in range(1, z_size):
+        arrival(z_in.at[dz], rz_sems, (dz,))
+        total = total + z_in[dz].astype(F32)
+    stream[...] = total
+    for spread in spreads:
+        spread.step_x(z_size - 1)
+
+    for k in range(1, reps):
+        arrival(facts_all.at[x], rep_sems, (k,))
+        departure(facts_all.at[x], rep_sems, (k,))
+    for k in range(1, n):
+        departure(facts, fact_sems, (k,))
+    for dz in range(z_size):
+        for dy in range(y_size):
+            slot = dz * y_size + dy
+            departure(core_out.at[slot], rc_sems, (slot,))
+            if dy:
+                departure(acc.at[slot], ry_sems, (dz, dy))
+            elif dz:
+                departure(acc.at[slot], rz_sems, (dz,))
+    for k in range(count):
+        pltpu.make_async_copy(weights[k], wholes[k].at[me], own_sems.at[k]).wait()
+    for spread in spreads:
+        for z in range(z_size):
+            spread.take_twin(z)
+        spread.finish()
+
+
+def head_kernel(z_size, y_size, reps, normed3, head_weight, facts, grad_normed3, grad_head, totals,
                 whole, logits, grads, turned, marks, stats_in, lse_all, acc, core_out, core_in, y_in, z_in,
-                loss_in, z_sems, y_sems, c_sems, st_sems, ls_sems, rc_sems, ry_sems, rz_sems, lo_sems):
+                loss_in, head_b, z_sems, y_sems, c_sems, st_sems, ls_sems, rc_sems, ry_sems, rz_sems, lo_sems):
     p = Place(z_size, y_size, reps)
     n, me, x = p.n, p.me, p.x
     length, width = normed3.shape
     half = length // 2
-    own_rows = head_b.shape[0]
+    own_rows = head_weight.shape[0]
     p.greet(True)
     spread = Spread(p, whole, z_sems, y_sems, c_sems)
     spread.start(normed3)
+    head_b[...] = head_weight[...].astype(BF)
     whole[me] = normed3[...]
     own_facts = facts.at[x]
     turned[...] = jnp.transpose(own_facts[...].reshape(n * 8, 128))
@@ -489,9 +535,6 @@
 
         lax.fori_loop(first * 2, last * 2, body, 0)
 
-    def forward_y(z):
-        spread.take_y(z)
-
     arrival(spread.block(p.z, 0, 1), c_sems, (p.z, 0))
     forward_column(p.z, 0, 1)
 
@@ -520,7 +563,7 @@
     for s in range(1, z_size + 1):
         if s < z_size:
             spread.step_z(s)
-        both(s - 1, spread.take_y)
+        spread.step_y(s - 1)
         if s < z_size:
             both(s, lambda z: one(z, s))
         both(s - 1, other)
@@ -675,6 +718,7 @@
         ((z_size, y_size, length, width), BF),
         ((z_size, length, width), BF),
         ((reps, 8, 128), F32),
+        ((own_rows, width), BF),
     ]
     sems = [
         dma((2, 2, z_size)), dma((2, z_size, y_size)), dma((2, z_size, y_size)),
@@ -688,16 +732,16 @@
     return sum(math.prod(shape) * jnp.dtype(kind).itemsize for shape, kind in buffers)
 
 
-def head_phase(normed3, head_b, facts, reps, n):
+def head_phase(normed3, head_weight, facts, reps, n):
     z_size, y_size = geometry(n)
     length, width = normed3.shape
-    buffers, sems = head_scratch(n, length, width, head_b.shape[0], reps)
+    buffers, sems = head_scratch(n, length, width, head_weight.shape[0], reps)
     vmem = pl.BlockSpec(memory_space=pltpu.VMEM)
     return pl.pallas_call(
         functools.partial(head_kernel, z_size, y_size, reps),
         out_shape=[
             jax.ShapeDtypeStruct((length, width), F32),
-            jax.ShapeDtypeStruct(head_b.shape, BF),
+            jax.ShapeDtypeStruct(head_weight.shape, BF),
             jax.ShapeDtypeStruct((8, 128), F32),
         ],
         in_specs=[vmem] * 3,
@@ -707,28 +751,27 @@
             collective_id=1, has_side_effects=True, vmem_limit_bytes=60 * 2**20
         ),
         name="head",
-    )(normed3, head_b, facts)
-
-
-def tail_kernel(z_size, y_size, split, counts, grad_stream0, facts, *refs):
+    )(normed3, head_weight, facts)
+
+
+def tail_kernel(z_size, y_size, own_width, split, counts, grad_stream0, facts, head_one, head_two, *refs):
     count = len(split)
     grads, refs = refs[:count], refs[count:]
     sums, refs = refs[:count], refs[count:]
-    code_sum, first_rows, refs = refs[0], refs[1], refs[2:]
+    code_sum, class_sum, squares, refs = refs[0], refs[1], refs[2], refs[3:]
     accs, refs = refs[:count], refs[count:]
     core_in, refs = refs[:count], refs[count:]
     x_in, refs = refs[:count], refs[count:]
     y_in, refs = refs[:count], refs[count:]
     z_in, refs = refs[:count], refs[count:]
     trade, refs = refs[:count], refs[count:]
-    (whole, code_out, code_in, rows_out, z_sems, y_sems, c_sems, own_sems, rc_sems, rx_sems, ry_sems,
-     rz_sems, tr_sems, co_sems, fr_sems) = refs
+    (whole, code_out, code_in, rows_out, given, z_sems, y_sems, c_sems, own_sems, rc_sems, rx_sems,
+     ry_sems, rz_sems, tr_sems, co_sems, fr_sems, sq_sems) = refs
     p = Place(z_size, y_size, 2)
     n, me, x = p.n, p.me, p.x
     length, width = grad_stream0.shape
     own_rows = code_out.shape[0]
-    spots = z_size * y_size
-    p.greet(False)
+    p.greet(True)
     mate = (me, 1 - x)
     spread = Spread(p, whole, z_sems, y_sems, c_sems)
     spread.start(grad_stream0)
@@ -738,11 +781,16 @@
         return dz * y_size + dy
 
     order = [(dz, dy) for dz in range(z_size - 1, -1, -1) for dy in range(y_size - 1, -1, -1)]
-    for dz, dy in order:
-        slot = slot_of(dz, dy)
-        for k in range(count):
-            send(grads[k].at[p.at(dz, dy, 1)], core_in[k].at[slot], rc_sems, (k, slot), p.twin())
-            pltpu.make_async_copy(grads[k].at[p.at(dz, dy)], accs[k].at[slot], own_sems.at[k, slot]).start()
+    halved = [k for k in range(count) if split[k]]
+    plain = [k for k in range(count) if not split[k]]
+    for kinds in (halved, plain):
+        for dz, dy in order:
+            slot = slot_of(dz, dy)
+            for k in kinds:
+                send(grads[k].at[p.at(dz, dy, 1)], core_in[k].at[slot], rc_sems, (k, slot), p.twin())
+                pltpu.make_async_copy(
+                    grads[k].at[p.at(dz, dy)], accs[k].at[slot], own_sems.at[k, slot]
+                ).start()
 
     def part(k, which):
         rows = counts[k] // 2
@@ -751,34 +799,40 @@
     def ref_of(k, ref, which):
         return ref.at[part(k, which)] if split[k] else ref
 
-    def send_y(k, dz, dy):
-        slot = slot_of(dz, dy)
-        send(ref_of(k, accs[k].at[slot], x), y_in[k].at[slot], ry_sems, (k, slot), (p.at(0, dy), x))
-
-    for dz, dy in order:
-        slot = slot_of(dz, dy)
-        for k in range(count):
-            pltpu.make_async_copy(grads[k].at[0], accs[k].at[slot], own_sems.at[k, slot]).wait()
-            arrival(core_in[k].at[slot], rc_sems, (k, slot))
-            accs[k][slot] = (accs[k][slot].astype(F32) + core_in[k][slot].astype(F32)).astype(BF)
-            if split[k]:
-                send(accs[k].at[slot, part(k, 1 - x)], x_in[k].at[slot], rx_sems, (k, slot), mate)
-            elif dy:
-                send_y(k, dz, dy)
+    def twin_sums(kinds, dz):
+        def body(dy, carry):
+            slot = slot_of(dz, dy)
+            for k in kinds:
+                pltpu.make_async_copy(grads[k].at[0], accs[k].at[slot], own_sems.at[k, slot]).wait()
+                arrival(core_in[k].at[slot], rc_sems, (k, slot))
+                accs[k][slot] = (accs[k][slot].astype(F32) + core_in[k][slot].astype(F32)).astype(BF)
+                if split[k]:
+                    send(accs[k].at[slot, part(k, 1 - x)], x_in[k].at[slot], rx_sems, (k, slot), mate)
+            return carry
+
+        lax.fori_loop(0, y_size, body, 0)
+
+    def send_y(kinds, dz):
+        for dy in range(1, y_size):
+            slot = slot_of(dz, dy)
+            for k in kinds:
+                source = ref_of(k, accs[k].at[slot], x)
+                send(source, y_in[k].at[slot], ry_sems, (k, slot), (p.at(0, dy), x))
 
     def take_x(dz):
-        for dy in range(y_size - 1, -1, -1):
+        def body(dy, carry):
             slot = slot_of(dz, dy)
-            for k in range(count):
-                if split[k]:
-                    arrival(x_in[k].at[slot], rx_sems, (k, slot))
-                    mine = accs[k].at[slot, part(k, x)]
-                    mine[...] = (mine[...].astype(F32) + x_in[k][slot].astype(F32)).astype(BF)
-                    if dy:
-                        send_y(k, dz, dy)
-
-    def take_y(dz):
-        for k in range(count):
+            for k in halved:
+                arrival(x_in[k].at[slot], rx_sems, (k, slot))
+                mine = accs[k].at[slot, part(k, x)]
+                mine[...] = (mine[...].astype(F32) + x_in[k][slot].astype(F32)).astype(BF)
+            return carry
+
+        lax.fori_loop(0, y_size, body, 0)
+        send_y(halved, dz)
+
+    def take_y(kinds, dz):
+        for k in kinds:
             mine = ref_of(k, accs[k].at[slot_of(dz, 0)], x)
             total = mine[...].astype(F32)
             for dy in range(1, y_size):
@@ -789,30 +843,27 @@
             if dz:
                 send(mine, z_in[k].at[dz], rz_sems, (k, dz), (p.at(dz, 0), x))
 
-    spread.step_z(1)
+    def square(value):
+        return jnp.sum(jnp.sum(value * value, 0, keepdims=True), 1, keepdims=True)
+
+    for s in range(1, z_size):
+        twin_sums(halved, z_size - s)
+        if s == z_size - 1:
+            twin_sums(halved, 0)
+        spread.step_z(s)
+        spread.step_y(s - 1)
+        twin_sums(plain, z_size - s)
+    send_y(plain, z_size - 1)
+    twin_sums(plain, 0)
     take_x(z_size - 1)
-    spread.take_y(p.z)
-    take_y(z_size - 1)
-
-    def both(s, act):
-        @pl.when(p.z - s >= 0)
-        def _():
-            act(p.z - s)
-
-        @pl.when(p.z + s < z_size)
-        def _():
-            act(p.z + s)
-
-    for s in range(2, z_size):
-        dz = z_size - s
-        spread.step_z(s)
-        take_x(dz)
-        both(s - 1, spread.take_y)
-        take_y(dz)
-    both(z_size - 1, spread.take_y)
-    take_x(0)
+    spread.step_y(z_size - 1)
+    send_y(plain, z_size - 2)
+    take_x(z_size - 2)
     for z in range(z_size):
         spread.take_twin(z)
+
+    rows_out[x] = whole[:, 0:8, :].astype(F32)
+    send(rows_out.at[x], rows_out.at[x], fr_sems, (), mate)
 
     blocks = 4
     rows = own_rows // blocks
@@ -834,37 +885,62 @@
         send(code_out.at[at], code_in.at[at], co_sems, (r,), mate)
         return carry
 
-    firsts = whole[:, 0:8, :].astype(F32)
-    rows_out[x] = firsts
-    send(rows_out.at[x], rows_out.at[x], fr_sems, (), mate)
-    lax.fori_loop(0, blocks, code_block, 0)
-
-    take_y(0)
+    lax.fori_loop(0, blocks // 2, code_block, 0)
+    take_y(plain, z_size - 1)
+    for dz in range(z_size - 3, -1, -1):
+        send_y(plain, dz)
+        take_x(dz)
+    take_y(halved, z_size - 1)
+    lax.fori_loop(blocks // 2, blocks, code_block, 0)
+    for dz in range(z_size - 2, -1, -1):
+        take_y(plain, dz)
+        take_y(halved, dz)
+
+    total_squares = square(head_one[...].astype(F32) + head_two[...].astype(F32))
+
+    arrival(rows_out.at[1 - x], fr_sems, ())
+    firsts = rows_out[:, :, 0, :].reshape(2 * n, width)
+    shift = lax.rem(width - me * own_width, width)
+    firsts = pltpu.roll(firsts, shift, 1)[:, :128]
+    firsts = jnp.where(lax.broadcasted_iota(jnp.int32, firsts.shape, 1) < own_width, firsts, 0.0)
+    classes = facts[:, :, 4, :].reshape(2 * n, 128)[:, 0:1]
+    class_iota = lax.broadcasted_iota(jnp.int32, (2 * n, class_sum.shape[1]), 1).astype(F32)
+    hot = jnp.where(class_iota == classes, 1.0, 0.0).astype(BF)
+    class_grad = lax.dot_general(
+        firsts.astype(BF), hot, (((0,), (0,)), ((), ())), preferred_element_type=F32
+    )
+    class_sum[...] = class_grad
+    total_squares = total_squares + square(class_grad)
+
     for k in range(count):
         mine = ref_of(k, accs[k].at[0], x)
         total = mine[...].astype(F32)
         for dz in range(1, z_size):
             arrival(z_in[k].at[dz], rz_sems, (k, dz))
             total = total + z_in[k][dz].astype(F32)
-        ref_of(k, trade[k].at[0], x)[...] = total.astype(BF)
         source = ref_of(k, trade[k].at[0], x)
-        target = source if split[k] else trade[k].at[1]
-        if split[k]:
-            target = trade[k].at[0, part(k, x)]
+        source[...] = total.astype(BF)
+        target = trade[k].at[0, part(k, x)] if split[k] else trade[k].at[1]
         send(source, target, tr_sems, (k,), mate)
+    for r in range(blocks):
+        at = pl.ds(r * rows, rows)
+        arrival(code_in.at[at], co_sems, (r,))
+        total = code_out[at].astype(F32) + code_in[at].astype(F32)
+        code_sum[at] = total
+        total_squares = total_squares + square(total)
     for k in range(count):
         if split[k]:
             arrival(trade[k].at[0, part(k, 1 - x)], tr_sems, (k,))
-            sums[k][...] = trade[k][0].astype(F32)
+            total = trade[k][0].astype(F32)
         else:
             arrival(trade[k].at[1], tr_sems, (k,))
-            sums[k][...] = trade[k][0].astype(F32) + trade[k][1].astype(F32)
-    arrival(rows_out.at[1 - x], fr_sems, ())
-    first_rows[...] = rows_out[...]
-    for r in range(blocks):
-        at = pl.ds(r * rows, rows)
-        arrival(code_in.at[at], co_sems, (r,))
-        code_sum[at] = code_out[at].astype(F32) + code_in[at].astype(F32)
+            total = trade[k][0].astype(F32) + trade[k][1].astype(F32)
+        sums[k][...] = total
+        total_squares = total_squares + square(total)
+
+    given[me] = jnp.broadcast_to(total_squares, (8, 128))
+    for k in range(1, n):
+        send(given.at[me], given.at[me], sq_sems, (k,), (lax.rem(me + k, n), x))
 
     spread.finish()
     departure(rows_out.at[x], fr_sems, ())
@@ -882,6 +958,11 @@
                     departure(x_in[k].at[slot], rx_sems, (k, slot))
                 if dy:
                     departure(y_in[k].at[slot], ry_sems, (k, slot))
+    for k in range(1, n):
+        arrival(given.at[0], sq_sems, (k,))
+    squares[...] = jnp.sum(given[...], 0)
+    for k in range(1, n):
+        departure(given.at[0], sq_sems, (k,))
 
 
 def tail_scratch(n, length, width, own_rows, shapes, split):
@@ -896,63 +977,40 @@
     buffers += [((z_size,) + s, BF) for s in halves]
     buffers += [((2,) + s, BF) for s in shapes]
     buffers += [((n, length, width), BF), ((own_rows, width), BF), ((own_rows, width), BF),
-                ((2, n, 8, width), F32)]
+                ((2, n, 8, width), F32), ((n, 8, 128), F32)]
     sems = [
         dma((2, 2, z_size)), dma((2, z_size, y_size)), dma((2, z_size, y_size)),
         dma((count, spots)), dma((2, count, spots)), dma((2, count, spots)), dma((2, count, spots)),
-        dma((2, count, z_size)), dma((2, count)), dma((2, 4)), dma((2,)),
+        dma((2, count, z_size)), dma((2, count)), dma((2, 4)), dma((2,)), dma((2, n)),
     ]
     return buffers, sems
 
 
-def tail_phase(grad_stream0, facts, grads, split, own_rows, n):
+def tail_phase(grad_stream0, facts, heads, grads, split, class_rows, own_width, n):
     z_size, y_size = geometry(n)
     length, width = grad_stream0.shape
+    own_rows = heads[0].shape[0]
     shapes = [g.shape[1:] for g in grads]
     buffers, sems = tail_scratch(n, length, width, own_rows, shapes, split)
     vmem, hbm = pl.BlockSpec(memory_space=pltpu.VMEM), pl.BlockSpec(memory_space=pl.ANY)
+    counts = tuple(s[0] for s in shapes)
     outs = pl.pallas_call(
-        functools.partial(tail_kernel, z_size, y_size, split, tuple(s[0] for s in shapes)),
+        functools.partial(tail_kernel, z_size, y_size, own_width, split, counts),
         out_shape=[jax.ShapeDtypeStruct(s, F32) for s in shapes]
-        + [jax.ShapeDtypeStruct((own_rows, width), F32), jax.ShapeDtypeStruct((2, n, 8, width), F32)],
-        in_specs=[vmem] * 2 + [hbm] * len(grads),
-        out_specs=[vmem] * (len(grads) + 2),
+        + [
+            jax.ShapeDtypeStruct((own_rows, width), F32),
+            jax.ShapeDtypeStruct((128, class_rows), F32),
+            jax.ShapeDtypeStruct((8, 128), F32),
+        ],
+        in_specs=[vmem] * 4 + [hbm] * len(grads),
+        out_specs=[vmem] * (len(grads) + 3),
         scratch_shapes=[pltpu.VMEM(shape, kind) for shape, kind in buffers] + sems,
         compiler_params=pltpu.CompilerParams(
             collective_id=2, has_side_effects=True, vmem_limit_bytes=60 * 2**20
         ),
         name="tail",
-    )(grad_stream0, facts, *grads)
-    return outs[: len(grads)], outs[len(grads)], outs[len(grads) + 1]
-
-
-def norm_kernel(n, squares, total, given, sems):
-    me, x = lax.axis_index("fsdp"), lax.axis_index("rep")
-    barrier = pltpu.get_barrier_semaphore()
-    for k in range(1, n):
-        pl.semaphore_signal(barrier, inc=1, device_id=(lax.rem(me + k, n), x), device_id_type=MESH)
-    pl.semaphore_wait(barrier, n - 1)
-    for k in range(1, n):
-        send(squares, given.at[me], sems, (k,), (lax.rem(me + k, n), x))
-    given[me] = squares[...]
-    for k in range(1, n):
-        arrival(given.at[0], sems, (k,))
-    total[...] = jnp.sum(given[...], 0)
-    for k in range(1, n):
-        departure(given.at[0], sems, (k,))
-
-
-def sum_over_fsdp(squares, n):
-    vmem = pl.BlockSpec(memory_space=pltpu.VMEM)
-    return pl.pallas_call(
-        functools.partial(norm_kernel, n),
-        out_shape=jax.ShapeDtypeStruct((8, 128), F32),
-        in_specs=[vmem],
-        out_specs=vmem,
-        scratch_shapes=[pltpu.VMEM((n, 8, 128), F32), pltpu.SemaphoreType.DMA((2, n))],
-        compiler_params=pltpu.CompilerParams(collective_id=3, has_side_effects=True),
-        name="norm",
-    )(jnp.broadcast_to(squares, (8, 128)))[0, 0]
+    )(grad_stream0, facts, *heads, *grads)
+    return outs[: len(grads)], outs[len(grads)], outs[len(grads) + 1], outs[len(grads) + 2][0, 0]
 
 
 def adam_update(weight, first, second, grad, rate, decay):
@@ -999,16 +1057,13 @@
         ],
         0,
     )
-    class_b = jnp.pad(class_table.astype(BF), ((0, -table_rows % 16), (0, 128 - own_width)))
-    code_b = code_table.astype(BF)
+    class_b = jnp.pad(class_table.T.astype(BF), ((0, 128 - own_width), (0, -table_rows % 128)))
     reps = lax.axis_size("rep")
-    parts = tuple(k % reps for k in range(4))
     wholes, stream0, facts = front(
         facts,
-        code_b,
+        code_table,
         class_b,
-        [w.astype(BF) for w in (gate_up, qkv_weight, out_weight, down_weight)],
-        parts,
+        [gate_up, qkv_weight, out_weight, down_weight],
         own_width,
         length,
         reps,
@@ -1056,10 +1111,11 @@
     head_b = head_weight.astype(BF)
     in_kernel = reps == 2 and size_of(head_scratch(n, length, width, own_rows, reps)[0]) < 52 * 2**20
     if in_kernel:
-        grad_normed3, grad_head, totals = head_phase(normed3[0], head_b, every_fact, reps, n)
+        grad_normed3, grad_head, totals = head_phase(normed3[0], head_weight, every_fact, reps, n)
         grad_normed3 = grad_normed3[None]
         loss_sum, token_count = totals[0, 0], totals[1, 0]
-        grad_head = grad_head.astype(F32) + lax.ppermute(grad_head, "rep", [(0, 1), (1, 0)]).astype(F32)
+        head_pair = (grad_head, lax.ppermute(grad_head, "rep", [(0, 1), (1, 0)]))
+        grad_head = head_pair[0].astype(F32) + head_pair[1].astype(F32)
     else:
         token_count = lax.psum(jnp.sum(all_counted), "rep")
         normed3_all = lax.all_gather(normed3, "fsdp", axis=0, tiled=True).reshape(tokens, width)
@@ -1126,22 +1182,19 @@
             g.astype(BF).reshape(n, -1, g.shape[-1])
             for g in (grad_gate_up, grad_qkv, grad_out, grad_down)
         ]
-        sums, grad_codes, first_rows = tail_phase(
+        sums, grad_codes, grad_classes, squares = tail_phase(
             grad_stream0[0].astype(BF),
             every_fact,
+            head_pair,
             blocks + [gain_blocks],
             (True, False, False, False, False),
-            own_rows,
+            table_rows + -table_rows % 128,
+            own_width,
             n,
         )
         grad_gate_up, grad_qkv, grad_out, grad_down, gain_part = sums
         grad_gains = gain_part[:3, :own_width]
-        class_part = lax.dynamic_slice(
-            first_rows[:, :, 0].reshape(-1, width), (0, me * own_width), (reps * n, own_width)
-        )
-        every_class = every_fact[:, :, 4, 0].reshape(-1).astype(jnp.int32)
-        class_spot = (every_class[:, None] == jnp.arange(table_rows)[None, :]).astype(BF)
-        grad_classes = dot("iv,id->vd", class_spot, class_part.astype(BF))
+        grad_classes = grad_classes[:own_width, :table_rows].T
     else:
         blocks = [
             g.astype(BF).reshape(n, -1, g.shape[-1]) for g in (grad_qkv, grad_gate_up, grad_out, grad_down)
@@ -1162,10 +1215,9 @@
     reduced = (
         grad_codes, grad_classes, grad_qkv, grad_out, grad_gate_up, grad_down, grad_head, grad_gains
     )
-    squares = jnp.zeros((), F32)
-    for grad_piece in reduced:
-        squares = squares + jnp.sum(grad_piece * grad_piece)
-    grad_norm = jnp.sqrt(sum_over_fsdp(squares, n))
+    if not in_kernel:
+        squares = lax.psum(sum(jnp.sum(piece * piece) for piece in reduced), "fsdp")
+    grad_norm = jnp.sqrt(squares)
     factor = jnp.minimum(1.0, 1.0 / CLIP_INV / (grad_norm + 1e-06))
     results = [loss_sum, token_count, grad_norm]
     for index in range(8):

time: 564 us -> 482 us (0.85)
  Pallas kernels: 423 us -> 362 us
  other arithmetic: 57.9 us -> 44.1 us
    pallas_call x2 -> x1, Pallas kernels: 186 us -> 146 us  [tail_phase(): pl.pallas_call(functools.partial(tail_kernel, z_size, y_size, own_width,...]
    pallas_call x1, Pallas kernels: 115 us -> 101 us  [front(): pl.pallas_call(functools.partial(front_kernel, z_size, y_size, reps, own_...]
    reduce_sum x7 -> x0, other arithmetic: 13.1 us -> none  [local(): squares = squares + jnp.sum(grad_piece * grad_piece)]
    convert_element_type x8 -> x1, other arithmetic: 9.06 us -> 0.94 us  [local(): class_table.T.astype(BF)]
    pallas_call x1, Pallas kernels: 122 us -> 116 us  [head_phase(): pl.pallas_call(functools.partial(head_kernel, z_size, y_size, reps), out_...]
    dot_general x18 -> x17, matrix products: 37.9 us -> 38.8 us  [dot(): return jnp.einsum(subscripts, left, right, preferred_element_type=F32)]
  transfers between devices with their start and end apart: 1 -> 1, of which waited for: 0 -> 0; matrix products, arithmetic and copies ran while one was open for 9% -> 10% of each run, Pallas kernels for 32% -> 0%
where the time goes in v4:
time: 482 us; the launch traced here: 474 us
  Pallas kernels  362 us (75%)
  other arithmetic  44.1 us (9%)
  matrix products  41.6 us (9%)
  local copies, waits for them, and re-layouts  18.9 us (4%)
  between operations  5.75 us (1%)
    pallas_call x1, Pallas kernels, tail_phase(): pl.pallas_call(functools.partial(tail_kernel, z_size, y_size, own_width,...  146 us
    pallas_call x1, Pallas kernels, head_phase(): pl.pallas_call(functools.partial(head_kernel, z_size, y_size, reps), out_...  116 us
    pallas_call x1, Pallas kernels, front(): pl.pallas_call(functools.partial(front_kernel, z_size, y_size, reps, own_...  101 us
    dot_general x17, matrix products, dot(): return jnp.einsum(subscripts, left, right, preferred_element_type=F32)  38.8 us
    sub x8, other arithmetic, adam_update(): weight - rate * (first_hat / (jnp.sqrt(second_hat) + ADAM_EPS) + decay *...  24.8 us
  transfers between devices with their start and end apart: 1, of which 0 were waited for; matrix products, arithmetic and copies ran while one was open for 10% of the time, Pallas kernels for 0%

profile of v4, /device:TPU:0, one launch (start us, length us, event | category | flops | bytes accessed | tf_op | source)
XLA Modules:
  0.0 474.0 jit_solution(13807647078841482903)
XLA Ops:
  7.1 100.7 %front.1 = (bf16[16,256,768]{2,1,0:T(8,128)(2,1)}, bf16[16,144,768]{2,1,0:T(8,128)(2,1)}, bf16[16,48,768]{2,1,0:T(8,128)(2,1)}, bf16[16,48,2048]{2,1,0:T(8,128)(...) custom-call(f32[8,128]{1,0:T(8,128)} %fusion.36.facts, f32[1024,768]{1,0:T(8,128)} %code_table.1, ...), custom_call_target="tpu_custom_call" | custom-call | tf_op jit(solution)/shard_map/front/pallas_call | solution.py:149
  110.1 3.4 convolution_bitcast_fusion.1
  116.1 2.8 fusion.57
  118.9 2.4 convolution_convert_fusion.6
  123.3 1.8 convolution_bitcast_fusion
  125.8 3.1 copy-done.43
  130.9 115.6 %head.1 = (f32[256,768]{1,0:T(8,128)}, bf16[1024,768]{1,0:T(8,128)(2,1)}, f32[8,128]{1,0:T(8,128)}) custom-call(bf16[256,768]{1,0:T(8,128)(2,1)} %multiply_convert_fusion.4.normed3, f32[1024,768]{1,0:T(8,128)} %head_weight.1, f32[2,16,8,128]{3,2,1,0:T(8,128)} %get-tuple-element.45.facts), custom_call_target="tpu_custom_call" | custom-call | tf_op jit(solution)/shard_map/head/pallas_call | solution.py:740
  246.6 1.7 collective-permute-start
  248.2 1.9 multiply_reduce_fusion.1
  250.2 1.5 multiply_subtract_fusion.3
  251.7 3.9 fusion.11
  255.7 2.5 multiply_reduce_fusion.2
  259.9 1.5 convolution_convert_fusion.3
  262.4 3.4 convolution_convert_fusion.4
  265.9 2.3 multiply_reduce_fusion
  270.9 3.4 multiply_convert_fusion
  276.2 1.5 copy-done.9
  277.7 2.6 multiply_reduce_fusion.3
  280.4 1.4 stack.26
  283.9 2.2 add_convert_fusion.grad_stream0
  286.0 4.2 convolution_convert_fusion.1
  290.2 2.7 convolution_convert_fusion.2
  293.1 4.6 convolution_convert_fusion
  297.8 145.6 %tail.1 = (f32[256,768]{1,0:T(8,128)}, f32[144,768]{1,0:T(8,128)}, f32[48,768]{1,0:T(8,128)}, f32[48,2048]{1,0:T(8,128)}, f32[16,128]{1,0:T(8,128)}, /*index=5*/...) custom-call(bf16[256,768]{1,0:T(8,128)(2,1)} %add_convert_fusion.grad_stream0, ...), custom_call_target="tpu_custom_call" | custom-call | tf_op jit(solution)/shard_map/tail/pallas_call | solution.py:997
  445.4 1.3 multiply_subtract_fusion.8
  446.7 2.1 multiply_subtract_fusion.6
  448.8 1.8 multiply_subtract_fusion.7
  450.6 2.6 multiply_subtract_fusion.5
  453.2 2.6 multiply_subtract_fusion.4
  455.8 3.1 multiply_subtract_fusion.2
  459.1 5.3 %multiply_subtract_fusion.1 = (f32[1024,768]{1,0:T(8,128)}, f32[1024,768]{1,0:T(8,128)}, f32[1024,768]{1,0:T(8,128)}) fusion(f32[1024,768]{1,0:T(8,128)S(1)} %copy-done.1, f32[1024,768]{1,0:T(8,128)S(1)} %copy-done.14, f32[]{:T(128)S(6)} %min.3, f32[1024,768]{1,0:T(8,128)S(1)} %copy-done.10, f32[1024,768]{1,0:T(8,128)S(1)} %copy-done.11), kind=kLoop, calls=%fused_computation.14 | loop fusion | flops 11796480 | bytes 22020100 | tf_op jit(solution)/shard_map/sub | solution.py:1021
  466.5 6.0 %multiply_subtract_fusion = (f32[1024,768]{1,0:T(8,128)}, f32[1024,768]{1,0:T(8,128)}, f32[1024,768]{1,0:T(8,128)}) fusion(f32[1024,768]{1,0:T(8,128)S(1)} %copy-done.2, f32[]{:T(128)S(6)} %min.3, bf16[1024,768]{1,0:T(8,128)(2,1)} %collective-permute-done.head_two, bf16[1024,768]{1,0:T(8,128)(2,1)S(1)} %copy-done.4, f32[1024,768]{1,0:T(8,128)S(1)} %copy-done.12, ...), kind=kLoop, calls=%fused_computation.12 | loop fusion | flops 14155776 | bytes 22020100 | tf_op jit(solution)/shard_map/sub | solution.py:1021
  (159 shorter events, 26.5 us)
Async XLA Ops:
  114.5 4.4 copy-start.28
  116.0 5.3 %copy-start.19 = (bf16[256,12,64]{0,2,1:T(8,128)(2,1)}, bf16[256,12,64]{0,2,1:T(8,128)(2,1)S(1)}, u32[]{:S(2)}) copy-start(bf16[256,12,64]{0,2,1:T(8,128)(2,1)S(1)} %get-tuple-element.106) | copy-start | bytes 1179652
  116.0 5.3 %copy-start.21 = (bf16[256,12,64]{0,2,1:T(8,128)(2,1)}, bf16[256,12,64]{0,2,1:T(8,128)(2,1)S(1)}, u32[]{:S(2)}) copy-start(bf16[256,12,64]{0,2,1:T(8,128)(2,1)S(1)} %get-tuple-element.107) | copy-start | bytes 1179652
  118.9 4.4 slice-start.1
  125.1 4.9 %copy-start = (f32[1,256,4096]{2,1,0:T(8,128)}, f32[1,256,4096]{2,1,0:T(8,128)S(1)}, u32[]{:S(2)}) copy-start(f32[1,256,4096]{2,1,0:T(8,128)S(1)} %convolution_bitcast_fusion) | copy-start | bytes 12582916
  125.8 4.2 copy-start.7
  246.5 5.1 %copy-start.44 = (bf16[16,48,2048]{2,1,0:T(8,128)(2,1)S(1)}, bf16[16,48,2048]{2,1,0:T(8,128)(2,1)}, u32[]{:S(2)}) copy-start(bf16[16,48,2048]{2,1,0:T(8,128)(2,1)} %get-tuple-element.49) | copy-start | bytes 9437188
  246.6 51.2 %collective-permute-start = (bf16[1024,768]{1,0:T(8,128)(2,1)}, bf16[1024,768]{1,0:T(8,128)(2,1)}, u32[]{:S(2)}, u32[]{:S(2)}) collective-permute-start(bf16[1024,768]{1,0:T(8,128)(2,1)} %get-tuple-element.52.head_one), channel_id=1, source_target_pairs={{0,1},{1,0},{2,3},{3,2},{4,5},{5,4},{6,7},{7,6},{8,9},{9,8},{10,11... | collective-permute-start | bytes 4718600 | tf_op jit(solution)/shard_map/ppermute | solution.py:1117
  250.2 5.5 %slice-start.2 = ((s8[6291456]{0:T(1024)(128)(4,1)}), s8[4194304]{0:T(1024)(128)(4,1)S(1)}, s32[]{:S(2)}) async-start(s8[6291456]{0:T(1024)(128)(4,1)} %bitcast.109), calls=%async_computation.2 | async-start | bytes 8388608
  265.9 4.3 copy-start.38
  276.2 4.2 copy-start.31
  286.0 4.2 copy-start.8
  297.7 147.7 %copy-start.39 = (f32[3,48]{1,0:T(4,128)S(1)}, f32[3,48]{1,0:T(4,128)}, u32[]{:S(2)}) copy-start(f32[3,48]{1,0:T(4,128)} %param.53) | copy-start | bytes 1732
  297.7 147.7 %copy-start.41 = (f32[3,48]{1,0:T(4,128)S(1)}, f32[3,48]{1,0:T(4,128)}, u32[]{:S(2)}) copy-start(f32[3,48]{1,0:T(4,128)} %param.54) | copy-start | bytes 1732
  297.7 147.7 %copy-start.42 = (f32[3,48]{1,0:T(4,128)S(1)}, f32[3,48]{1,0:T(4,128)}, u32[]{:S(2)}) copy-start(f32[3,48]{1,0:T(4,128)} %param.55) | copy-start | bytes 1732
  297.7 149.0 %copy-start.23 = (f32[1001,48]{0,1:T(8,128)S(1)}, f32[1001,48]{0,1:T(8,128)}, u32[]{:S(2)}) copy-start(f32[1001,48]{0,1:T(8,128)} %param.35) | copy-start | bytes 576580
  297.8 149.0 %copy-start.34 = (f32[1001,48]{0,1:T(8,128)S(1)}, f32[1001,48]{0,1:T(8,128)}, u32[]{:S(2)}) copy-start(f32[1001,48]{0,1:T(8,128)} %param.36) | copy-start | bytes 576580
  297.8 151.0 %copy-start.26 = (f32[48,768]{1,0:T(8,128)S(1)}, f32[48,768]{1,0:T(8,128)}, u32[]{:S(2)}) copy-start(f32[48,768]{1,0:T(8,128)} %refs_2_.1) | copy-start | bytes 442372
  297.8 151.0 %copy-start.35 = (f32[48,768]{1,0:T(8,128)S(1)}, f32[48,768]{1,0:T(8,128)}, u32[]{:S(2)}) copy-start(f32[48,768]{1,0:T(8,128)} %param.42) | copy-start | bytes 442372
  297.8 152.8 %copy-start.18 = (f32[48,2048]{1,0:T(8,128)S(1)}, f32[48,2048]{1,0:T(8,128)}, u32[]{:S(2)}) copy-start(f32[48,2048]{1,0:T(8,128)} %refs_3_.1) | copy-start | bytes 1179652
  297.8 155.4 %copy-start.17 = (f32[144,768]{1,0:T(8,128)S(1)}, f32[144,768]{1,0:T(8,128)}, u32[]{:S(2)}) copy-start(f32[144,768]{1,0:T(8,128)} %refs_1_.1) | copy-start | bytes 1327108
  297.8 155.4 %copy-start.27 = (f32[144,768]{1,0:T(8,128)S(1)}, f32[144,768]{1,0:T(8,128)}, u32[]{:S(2)}) copy-start(f32[144,768]{1,0:T(8,128)} %param.39) | copy-start | bytes 1327108
  297.8 158.0 %copy-start.24 = (f32[256,768]{1,0:T(8,128)S(1)}, f32[256,768]{1,0:T(8,128)}, u32[]{:S(2)}) copy-start(f32[256,768]{1,0:T(8,128)} %param.45) | copy-start | bytes 2359300
  297.8 158.0 %copy-start.25 = (f32[256,768]{1,0:T(8,128)S(1)}, f32[256,768]{1,0:T(8,128)}, u32[]{:S(2)}) copy-start(f32[256,768]{1,0:T(8,128)} %param.46) | copy-start | bytes 2359300
  446.7 12.3 %copy-start.14 = (f32[1024,768]{1,0:T(8,128)S(1)}, f32[1024,768]{1,0:T(8,128)}, u32[]{:S(2)}) copy-start(f32[1024,768]{1,0:T(8,128)} %get-tuple-element.54) | copy-start | bytes 9437188
  450.6 5.2 %copy-start.16 = (f32[256,768]{1,0:T(8,128)S(1)}, f32[256,768]{1,0:T(8,128)}, u32[]{:S(2)}) copy-start(f32[256,768]{1,0:T(8,128)} %refs_0_.1) | copy-start | bytes 2359300
  450.6 8.4 %copy-start.11 = (f32[1024,768]{1,0:T(8,128)S(1)}, f32[1024,768]{1,0:T(8,128)}, u32[]{:S(2)}) copy-start(f32[1024,768]{1,0:T(8,128)} %param.34) | copy-start | bytes 9437188
  453.2 5.8 %copy-start.10 = (f32[1024,768]{1,0:T(8,128)S(1)}, f32[1024,768]{1,0:T(8,128)}, u32[]{:S(2)}) copy-start(f32[1024,768]{1,0:T(8,128)} %param.33) | copy-start | bytes 9437188
  459.0 5.4 %copy-start.2 = (f32[1024,768]{1,0:T(8,128)S(1)}, f32[1024,768]{1,0:T(8,128)}, u32[]{:S(2)}) copy-start(f32[1024,768]{1,0:T(8,128)} %head_weight.1) | copy-start | bytes 9437188
  459.0 5.3 %copy-start.4 = (bf16[1024,768]{1,0:T(8,128)(2,1)S(1)}, bf16[1024,768]{1,0:T(8,128)(2,1)}, u32[]{:S(2)}) copy-start(bf16[1024,768]{1,0:T(8,128)(2,1)} %get-tuple-element.52.head_one) | copy-start | bytes 4718596
  459.0 6.6 %copy-start.12 = (f32[1024,768]{1,0:T(8,128)S(1)}, f32[1024,768]{1,0:T(8,128)}, u32[]{:S(2)}) copy-start(f32[1024,768]{1,0:T(8,128)} %param.51) | copy-start | bytes 9437188
  459.0 7.5 %copy-start.13 = (f32[1024,768]{1,0:T(8,128)S(1)}, f32[1024,768]{1,0:T(8,128)}, u32[]{:S(2)}) copy-start(f32[1024,768]{1,0:T(8,128)} %param.52) | copy-start | bytes 9437188
  (23 other events, 68.4 us)

commit v5 on v4

--- a/solution.py
+++ b/solution.py
@@ -29,23 +29,12 @@
     return (cosine, sine)
 
 
-def rotate(values, cosine, sine):
-    half = values.shape[-1] // 2
-    swapped = jnp.concatenate([-values[..., half:], values[..., :half]], -1)
-    return values * cosine[:, None, :] + swapped * sine[:, None, :]
-
-
 def rotate_back(grads, cosine, sine):
     half = grads.shape[-1] // 2
     scaled = grads * sine[:, None, :]
     return grads * cosine[:, None, :] + jnp.concatenate(
         [scaled[..., half:], -scaled[..., :half]], -1
     )
-
-
-def norm_forward(stream, gain):
-    inverse = lax.rsqrt(jnp.mean(stream * stream, -1, keepdims=True) + NORM_EPS)
-    return (stream * inverse * gain, inverse)
 
 
 def norm_backward(stream, inverse, gain, grad_out):
@@ -754,9 +743,12 @@
     )(normed3, head_weight, facts)
 
 
-def tail_kernel(z_size, y_size, own_width, split, counts, grad_stream0, facts, head_one, head_two, *refs):
+def tail_kernel(z_size, y_size, own_width, split, counts, queries, keys, values, grad_attended, turn,
+                qkv_w, stream0, normed1, grad_stream1, gains, facts, head_one, head_two, *refs):
     count = len(split)
-    grads, refs = refs[:count], refs[count:]
+    early = count - 2
+    qkv_at, gain_at = early, early + 1
+    grads, refs = refs[:early], refs[early:]
     sums, refs = refs[:count], refs[count:]
     code_sum, class_sum, squares, refs = refs[0], refs[1], refs[2], refs[3:]
     accs, refs = refs[:count], refs[count:]
@@ -765,32 +757,41 @@
     y_in, refs = refs[:count], refs[count:]
     z_in, refs = refs[:count], refs[count:]
     trade, refs = refs[:count], refs[count:]
-    (whole, code_out, code_in, rows_out, given, z_sems, y_sems, c_sems, own_sems, rc_sems, rx_sems,
+    (whole, code_out, code_in, rows_out, given, grad_mixed, grad_qkv, gain_blocks, grad_stream0, z_sems, y_sems, c_sems, own_sems, rc_sems, rx_sems,
      ry_sems, rz_sems, tr_sems, co_sems, fr_sems, sq_sems) = refs
     p = Place(z_size, y_size, 2)
     n, me, x = p.n, p.me, p.x
-    length, width = grad_stream0.shape
+    length, width = stream0.shape
     own_rows = code_out.shape[0]
     p.greet(True)
     mate = (me, 1 - x)
     spread = Spread(p, whole, z_sems, y_sems, c_sems)
-    spread.start(grad_stream0)
-    whole[me] = grad_stream0[...]
 
     def slot_of(dz, dy):
         return dz * y_size + dy
 
     order = [(dz, dy) for dz in range(z_size - 1, -1, -1) for dy in range(y_size - 1, -1, -1)]
-    halved = [k for k in range(count) if split[k]]
-    plain = [k for k in range(count) if not split[k]]
-    for kinds in (halved, plain):
+    halved = [k for k in range(early) if split[k]]
+    plain = [k for k in range(early) if not split[k]]
+    late = [qkv_at, gain_at]
+
+    def block_of(k, f):
+        if k == qkv_at:
+            rows = counts[k]
+            return grad_qkv.at[pl.ds(pl.multiple_of(f * rows, rows), rows)]
+        return gain_blocks.at[f] if k == gain_at else grads[k].at[f]
+
+    def to_twin(kinds):
         for dz, dy in order:
             slot = slot_of(dz, dy)
             for k in kinds:
-                send(grads[k].at[p.at(dz, dy, 1)], core_in[k].at[slot], rc_sems, (k, slot), p.twin())
+                send(block_of(k, p.at(dz, dy, 1)), core_in[k].at[slot], rc_sems, (k, slot), p.twin())
                 pltpu.make_async_copy(
-                    grads[k].at[p.at(dz, dy)], accs[k].at[slot], own_sems.at[k, slot]
+                    block_of(k, p.at(dz, dy)), accs[k].at[slot], own_sems.at[k, slot]
                 ).start()
+
+    to_twin(halved)
+    to_twin(plain)
 
     def part(k, which):
         rows = counts[k] // 2
@@ -803,7 +804,7 @@
         def body(dy, carry):
             slot = slot_of(dz, dy)
             for k in kinds:
-                pltpu.make_async_copy(grads[k].at[0], accs[k].at[slot], own_sems.at[k, slot]).wait()
+                pltpu.make_async_copy(accs[k].at[slot], accs[k].at[slot], own_sems.at[k, slot]).wait()
                 arrival(core_in[k].at[slot], rc_sems, (k, slot))
                 accs[k][slot] = (accs[k][slot].astype(F32) + core_in[k][slot].astype(F32)).astype(BF)
                 if split[k]:
@@ -846,19 +847,104 @@
     def square(value):
         return jnp.sum(jnp.sum(value * value, 0, keepdims=True), 1, keepdims=True)
 
+    lane = lax.broadcasted_iota(jnp.int32, (length, 128), 1)
+    low = lax.rem(lane, HEAD_DIM) < HEAD_DIM // 2
+    scale = HEAD_DIM ** (-0.5)
+
+    def turn_back(grad):
+        scaled = grad * turn[1]
+        other = jnp.where(
+            low, pltpu.roll(scaled, 128 - HEAD_DIM // 2, 1), -pltpu.roll(scaled, HEAD_DIM // 2, 1)
+        )
+        return grad * turn[0] + other
+
+    def pair(j, carry):
+        at = pl.ds(pl.multiple_of(j * 128, 128), 128)
+        q, k, v, grad = queries[:, at], keys[:, at], values[:, at], grad_attended[:, at]
+        q_two, grad_two = both_heads(q), both_heads(grad)
+        probs = attention_probs(q_two, k)
+        grad_probs = product(grad_two, v, BY_LANES)
+        inner = jnp.sum(probs * grad_probs, -1, keepdims=True)
+        grad_scores = (probs * (grad_probs - inner)).astype(BF)
+        grad_v = product(probs.astype(BF), grad_two, BY_ROWS)
+        grad_q = one_row(jnp.dot(grad_scores, k, preferred_element_type=F32))
+        grad_k = product(grad_scores, q_two, BY_ROWS)
+        grad_mixed[:, at] = turn_back(grad_q * scale).astype(BF)
+        base = pl.multiple_of(j * 128, 128)
+        grad_mixed[:, pl.ds(width + base, 128)] = turn_back(grad_k * scale).astype(BF)
+        grad_mixed[:, pl.ds(2 * width + base, 128)] = grad_v.astype(BF)
+        return carry
+
+    def settle(kinds):
+        for k in kinds:
+            mine = ref_of(k, accs[k].at[0], x)
+            total = mine[...].astype(F32)
+            for dz in range(1, z_size):
+                arrival(z_in[k].at[dz], rz_sems, (k, dz))
+                total = total + z_in[k][dz].astype(F32)
+            source = ref_of(k, trade[k].at[0], x)
+            source[...] = total.astype(BF)
+            target = trade[k].at[0, part(k, x)] if split[k] else trade[k].at[1]
+            send(source, target, tr_sems, (k,), mate)
+
+    def collect(kinds):
+        summed = jnp.zeros((1, 1), F32)
+        for k in kinds:
+            if split[k]:
+                arrival(trade[k].at[0, part(k, 1 - x)], tr_sems, (k,))
+                total = trade[k][0].astype(F32)
+            else:
+                arrival(trade[k].at[1], tr_sems, (k,))
+                total = trade[k][0].astype(F32) + trade[k][1].astype(F32)
+            sums[k][...] = total
+            summed = summed + square(total)
+        return summed
+
+    pairs = width // 128
+    for s in range(z_size):
+        dz = z_size - 1 - s
+        lax.fori_loop(s * pairs // z_size, (s + 1) * pairs // z_size, pair, 0)
+        twin_sums(halved, dz)
+        twin_sums(plain, dz)
+        send_y(plain, dz)
+
+    grad_out = jnp.dot(grad_mixed[...], qkv_w[...], preferred_element_type=F32)
+    stream = stream0[...]
+    inverse = lax.rsqrt(jnp.mean(stream * stream, -1, keepdims=True) + NORM_EPS)
+    weighted = grad_out * gains[3:4, :]
+    inner = jnp.mean(weighted * stream, -1, keepdims=True)
+    grad_first = inverse * weighted - stream * (inverse * inverse * inverse) * inner
+    grad_stream0[...] = (grad_stream1[...] + grad_first).astype(BF)
+    spread.start(grad_stream0)
+    whole[me] = grad_stream0[...]
+    gain_one = jnp.sum(grad_out * stream * inverse, 0, keepdims=True)
+    third = grad_qkv.shape[0] // 6
+    for r in range(6):
+        at = pl.ds(r * third, third)
+        grad_qkv[at, :] = product(grad_mixed[:, r * third : (r + 1) * third], normed1[...], BY_ROWS).astype(BF)
+    row = lax.broadcasted_iota(jnp.int32, (16, width), 0)
+    spare = jnp.concatenate([gains[...], gains[...]], 0)
+    all_gains = jnp.where(row == 0, gain_one, jnp.where(row < 3, spare, 0.0))
+
+    def gain_block(f, carry):
+        turned = pltpu.roll(all_gains, lax.rem(width - f * own_width, width), 1)[:, :128]
+        own = lax.broadcasted_iota(jnp.int32, turned.shape, 1) < own_width
+        gain_blocks[f] = jnp.where(own, turned, 0.0).astype(BF)
+        return carry
+
+    lax.fori_loop(0, n, gain_block, 0)
+    to_twin(late)
     for s in range(1, z_size):
-        twin_sums(halved, z_size - s)
-        if s == z_size - 1:
-            twin_sums(halved, 0)
         spread.step_z(s)
         spread.step_y(s - 1)
-        twin_sums(plain, z_size - s)
-    send_y(plain, z_size - 1)
-    twin_sums(plain, 0)
-    take_x(z_size - 1)
+        twin_sums(late, z_size - s)
+        take_y(plain, z_size - s)
+    twin_sums(late, 0)
     spread.step_y(z_size - 1)
-    send_y(plain, z_size - 2)
-    take_x(z_size - 2)
+    for dz in range(z_size - 1, -1, -1):
+        take_x(dz)
+        send_y(late, dz)
+    take_y(plain, 0)
     for z in range(z_size):
         spread.take_twin(z)
 
@@ -885,16 +971,11 @@
         send(code_out.at[at], code_in.at[at], co_sems, (r,), mate)
         return carry
 
-    lax.fori_loop(0, blocks // 2, code_block, 0)
-    take_y(plain, z_size - 1)
-    for dz in range(z_size - 3, -1, -1):
-        send_y(plain, dz)
-        take_x(dz)
-    take_y(halved, z_size - 1)
-    lax.fori_loop(blocks // 2, blocks, code_block, 0)
-    for dz in range(z_size - 2, -1, -1):
-        take_y(plain, dz)
-        take_y(halved, dz)
+    for r in range(z_size):
+        lax.fori_loop(r * blocks // z_size, (r + 1) * blocks // z_size, code_block, 0)
+        take_y(halved, z_size - 1 - r)
+        take_y(late, z_size - 1 - r)
+    settle(halved + plain)
 
     total_squares = square(head_one[...].astype(F32) + head_two[...].astype(F32))
 
@@ -912,31 +993,15 @@
     class_sum[...] = class_grad
     total_squares = total_squares + square(class_grad)
 
-    for k in range(count):
-        mine = ref_of(k, accs[k].at[0], x)
-        total = mine[...].astype(F32)
-        for dz in range(1, z_size):
-            arrival(z_in[k].at[dz], rz_sems, (k, dz))
-            total = total + z_in[k][dz].astype(F32)
-        source = ref_of(k, trade[k].at[0], x)
-        source[...] = total.astype(BF)
-        target = trade[k].at[0, part(k, x)] if split[k] else trade[k].at[1]
-        send(source, target, tr_sems, (k,), mate)
+    total_squares = total_squares + collect(halved + plain)
+    settle(late)
     for r in range(blocks):
         at = pl.ds(r * rows, rows)
         arrival(code_in.at[at], co_sems, (r,))
         total = code_out[at].astype(F32) + code_in[at].astype(F32)
         code_sum[at] = total
         total_squares = total_squares + square(total)
-    for k in range(count):
-        if split[k]:
-            arrival(trade[k].at[0, part(k, 1 - x)], tr_sems, (k,))
-            total = trade[k][0].astype(F32)
-        else:
-            arrival(trade[k].at[1], tr_sems, (k,))
-            total = trade[k][0].astype(F32) + trade[k][1].astype(F32)
-        sums[k][...] = total
-        total_squares = total_squares + square(total)
+    total_squares = total_squares + collect(late)
 
     given[me] = jnp.broadcast_to(total_squares, (8, 128))
     for k in range(1, n):
@@ -977,7 +1042,8 @@
     buffers += [((z_size,) + s, BF) for s in halves]
     buffers += [((2,) + s, BF) for s in shapes]
     buffers += [((n, length, width), BF), ((own_rows, width), BF), ((own_rows, width), BF),
-                ((2, n, 8, width), F32), ((n, 8, 128), F32)]
+                ((2, n, 8, width), F32), ((n, 8, 128), F32), ((length, 3 * width), BF),
+                ((3 * width, width), BF), ((n, 16, 128), BF), ((length, width), BF)]
     sems = [
         dma((2, 2, z_size)), dma((2, z_size, y_size)), dma((2, z_size, y_size)),
         dma((count, spots)), dma((2, count, spots)), dma((2, count, spots)), dma((2, count, spots)),
@@ -986,11 +1052,11 @@
     return buffers, sems
 
 
-def tail_phase(grad_stream0, facts, heads, grads, split, class_rows, own_width, n):
+def tail_phase(layer, facts, heads, grads, late, split, class_rows, own_width, n):
     z_size, y_size = geometry(n)
-    length, width = grad_stream0.shape
+    length, width = layer[0].shape
     own_rows = heads[0].shape[0]
-    shapes = [g.shape[1:] for g in grads]
+    shapes = [g.shape[1:] for g in grads] + late
     buffers, sems = tail_scratch(n, length, width, own_rows, shapes, split)
     vmem, hbm = pl.BlockSpec(memory_space=pltpu.VMEM), pl.BlockSpec(memory_space=pl.ANY)
     counts = tuple(s[0] for s in shapes)
@@ -1002,15 +1068,124 @@
             jax.ShapeDtypeStruct((128, class_rows), F32),
             jax.ShapeDtypeStruct((8, 128), F32),
         ],
-        in_specs=[vmem] * 4 + [hbm] * len(grads),
-        out_specs=[vmem] * (len(grads) + 3),
+        in_specs=[vmem] * (len(layer) + 3) + [hbm] * len(grads),
+        out_specs=[vmem] * (len(shapes) + 3),
         scratch_shapes=[pltpu.VMEM(shape, kind) for shape, kind in buffers] + sems,
         compiler_params=pltpu.CompilerParams(
             collective_id=2, has_side_effects=True, vmem_limit_bytes=60 * 2**20
         ),
         name="tail",
-    )(grad_stream0, facts, *heads, *grads)
-    return outs[: len(grads)], outs[len(grads)], outs[len(grads) + 1], outs[len(grads) + 2][0, 0]
+    )(*layer, facts, *heads, *grads)
+    many = len(shapes)
+    return outs[:many], outs[many], outs[many + 1], outs[many + 2][0, 0]
+
+
+BY_ROWS = (((0,), (0,)), ((), ()))
+BY_LANES = (((1,), (1,)), ((), ()))
+
+
+def product(left, right, dims):
+    return lax.dot_general(left, right, dims, preferred_element_type=F32)
+
+
+def both_heads(pair):
+    lane = lax.broadcasted_iota(jnp.int32, pair.shape, 1)
+    zero = jnp.zeros_like(pair)
+    first, second = jnp.where(lane < HEAD_DIM, pair, zero), jnp.where(lane < HEAD_DIM, zero, pair)
+    return jnp.concatenate([first, second], 0)
+
+
+def one_row(two):
+    length = two.shape[0] // 2
+    lane = lax.broadcasted_iota(jnp.int32, (length, 128), 1)
+    return jnp.where(lane < HEAD_DIM, two[:length], two[length:])
+
+
+def attention_probs(q_two, k):
+    length = k.shape[0]
+    query = lax.rem(lax.broadcasted_iota(jnp.int32, (2 * length, length), 0), length)
+    causal = query >= lax.broadcasted_iota(jnp.int32, (2 * length, length), 1)
+    scores = jnp.where(causal, product(q_two, k, BY_LANES) * HEAD_DIM ** (-0.5), -1e30)
+    expo = jnp.exp(scores - jnp.max(scores, -1, keepdims=True))
+    return expo / jnp.sum(expo, -1, keepdims=True)
+
+
+def layer_kernel(stream0, gains, turn, qkv_hbm, out_hbm, gate_hbm, down_hbm,
+                 normed1, queries, keys, values, attended, stream1, normed2, gated, hidden, stream2, normed3,
+                 qkv_w, out_w, gate_w, down_w, sems):
+    moves = [
+        pltpu.make_async_copy(src, dst, sems.at[i])
+        for i, (src, dst) in enumerate(
+            ((qkv_hbm, qkv_w), (out_hbm, out_w), (gate_hbm, gate_w), (down_hbm, down_w))
+        )
+    ]
+    for move in moves:
+        move.start()
+    length, width = stream0.shape
+    hidden_width = hidden.shape[1]
+
+    def rms(stream, row):
+        inverse = lax.rsqrt(jnp.mean(stream * stream, -1, keepdims=True) + NORM_EPS)
+        return (stream * inverse * gains[row : row + 1, :]).astype(BF)
+
+    normed1[...] = rms(stream0[...], 0)
+    lane = lax.broadcasted_iota(jnp.int32, (length, 128), 1)
+    low = lax.rem(lane, HEAD_DIM) < HEAD_DIM // 2
+
+    def turned(part):
+        other = jnp.where(
+            low, -pltpu.roll(part, 128 - HEAD_DIM // 2, 1), pltpu.roll(part, HEAD_DIM // 2, 1)
+        )
+        return (part * turn[0] + other * turn[1]).astype(BF)
+
+    moves[0].wait()
+
+    def pair(j, carry):
+        base = pl.multiple_of(j * 128, 128)
+        at = pl.ds(base, 128)
+        x = normed1[...]
+        q = turned(product(x, qkv_w[at, :], BY_LANES))
+        k = turned(product(x, qkv_w[pl.ds(width + base, 128), :], BY_LANES))
+        v = product(x, qkv_w[pl.ds(2 * width + base, 128), :], BY_LANES).astype(BF)
+        queries[:, at], keys[:, at], values[:, at] = q, k, v
+        probs = attention_probs(both_heads(q), k).astype(BF)
+        attended[:, at] = one_row(jnp.dot(probs, v, preferred_element_type=F32)).astype(BF)
+        return carry
+
+    lax.fori_loop(0, width // 128, pair, 0)
+    moves[1].wait()
+    stream1[...] = stream0[...] + product(attended[...], out_w[...], BY_LANES)
+    normed2[...] = rms(stream1[...], 1)
+    moves[2].wait()
+    step = 512
+    for at in range(0, hidden_width, step):
+        gate = product(normed2[...], gate_w[at : at + step, :], BY_LANES)
+        up = product(normed2[...], gate_w[hidden_width + at : hidden_width + at + step, :], BY_LANES)
+        gated[:, at : at + step] = gate
+        gated[:, hidden_width + at : hidden_width + at + step] = up
+        hidden[:, at : at + step] = (gate * (1.0 / (1.0 + jnp.exp(-gate))) * up).astype(BF)
+    moves[3].wait()
+    stream2[...] = stream1[...] + product(hidden[...], down_w[...], BY_LANES)
+    normed3[...] = rms(stream2[...], 2)
+
+
+def layer_forward(stream0, gains, turn, qkv_w, out_w, gate_w, down_w):
+    length, width = stream0.shape
+    hidden_width = down_w.shape[1]
+    vmem, hbm = pl.BlockSpec(memory_space=pltpu.VMEM), pl.BlockSpec(memory_space=pl.ANY)
+    half, full = jax.ShapeDtypeStruct((length, width), BF), jax.ShapeDtypeStruct((length, width), F32)
+    outs = [half] * 5 + [full, half, jax.ShapeDtypeStruct((length, 2 * hidden_width), F32)]
+    outs += [jax.ShapeDtypeStruct((length, hidden_width), BF), full, half]
+    return pl.pallas_call(
+        layer_kernel,
+        out_shape=outs,
+        in_specs=[vmem] * 3 + [hbm] * 4,
+        out_specs=[vmem] * len(outs),
+        scratch_shapes=[pltpu.VMEM(w.shape, BF) for w in (qkv_w, out_w, gate_w, down_w)]
+        + [pltpu.SemaphoreType.DMA((4,))],
+        compiler_params=pltpu.CompilerParams(vmem_limit_bytes=56 * 2**20),
+        name="layer",
+    )(stream0, gains, turn, qkv_w, out_w, gate_w, down_w)
 
 
 def adam_update(weight, first, second, grad, rate, decay):
@@ -1083,30 +1258,20 @@
     own_ids = jnp.arange(own_rows) + me * own_rows
     lookup = (previous[:, None] == own_ids[None, :]).astype(BF)
 
-    normed1, inverse1 = norm_forward(stream0, gains32[0])
-    normed1 = normed1.astype(BF)
-    mixed = dot("btd,ed->bte", normed1, qkv_w)
     cosine, sine = rotary_tables(length, HEAD_DIM)
+    turn = jnp.stack([jnp.concatenate([t, t], -1) for t in (cosine, sine)])
     split4 = (batch, length, heads, HEAD_DIM)
-    queries = rotate(mixed[..., :width].reshape(split4), cosine, sine).astype(BF)
-    keys_rot = rotate(mixed[..., width : 2 * width].reshape(split4), cosine, sine).astype(BF)
-    values = mixed[..., 2 * width :].reshape(split4).astype(BF)
-    scores = attention_scores(queries, keys_rot)
-    top = jnp.max(scores, -1, keepdims=True)
-    expo = jnp.exp(scores - top)
-    probs32 = expo / jnp.sum(expo, -1, keepdims=True)
-    probs = probs32.astype(BF)
-    attended = dot("bhqk,bkhd->bqhd", probs, values).astype(BF).reshape(batch, length, width)
-    stream1 = stream0 + dot("btd,ed->bte", attended, out_w)
-    normed2, inverse2 = norm_forward(stream1, gains32[1])
-    normed2 = normed2.astype(BF)
-    gated = dot("btd,fd->btf", normed2, gate_w)
+    kept = layer_forward(
+        stream0[0], jnp.pad(gains32, ((0, 5), (0, 0))), turn, qkv_w, out_w, gate_w, down_w
+    )
+    (normed1, queries, keys_rot, values, attended, stream1, normed2, gated, hidden, stream2, normed3) = (
+        t[None] for t in kept
+    )
     gate_part = gated[..., :hidden_width]
     up_part = gated[..., hidden_width:]
-    hidden = (jax.nn.silu(gate_part) * up_part).astype(BF)
-    stream2 = stream1 + dot("btf,df->btd", hidden, down_w)
-    normed3, inverse3 = norm_forward(stream2, gains32[2])
-    normed3 = normed3.astype(BF)
+    inverse1, inverse2, inverse3 = (
+        lax.rsqrt(jnp.mean(t * t, -1, keepdims=True) + NORM_EPS) for t in (stream0, stream1, stream2)
+    )
 
     head_b = head_weight.astype(BF)
     in_kernel = reps == 2 and size_of(head_scratch(n, length, width, own_rows, reps)[0]) < 52 * 2**20
@@ -1151,51 +1316,56 @@
     grad_stream1 = grad_stream2 + grad_middle
     grad_attn = grad_stream1.astype(BF)
     grad_out = dot("bte,btd->ed", grad_attn, attended)
-    grad_attended = dot("bte,ed->btd", grad_attn, out_w).astype(BF).reshape(split4)
-    grad_probs = dot("bqhd,bkhd->bhqk", grad_attended, values)
-    grad_values = dot("bhqk,bqhd->bkhd", probs, grad_attended)
-    grad_scores = probs32 * (grad_probs - jnp.sum(probs32 * grad_probs, -1, keepdims=True))
-    grad_scores = grad_scores.astype(BF)
-    scale = HEAD_DIM ** (-0.5)
-    grad_queries = dot("bhqk,bkhd->bqhd", grad_scores, keys_rot) * scale
-    grad_keys = dot("bhqk,bqhd->bkhd", grad_scores, queries) * scale
-    grad_mixed = jnp.concatenate(
-        [
-            rotate_back(grad_queries, cosine, sine).reshape(batch, length, width),
-            rotate_back(grad_keys, cosine, sine).reshape(batch, length, width),
-            grad_values.reshape(batch, length, width),
-        ],
-        -1,
-    ).astype(BF)
-    grad_qkv = dot("bte,btd->ed", grad_mixed, normed1)
-    grad_normed1 = dot("bte,ed->btd", grad_mixed, qkv_w)
-    grad_first, gain_one = norm_backward(stream0, inverse1, gains32[0], grad_normed1)
-    grad_stream0 = grad_stream1 + grad_first
-
-    grad_gains = jnp.stack([gain_one, gain_two, gain_three])
+    grad_attended = dot("bte,ed->btd", grad_attn, out_w).astype(BF)
     if in_kernel:
-        gain_blocks = jnp.pad(
-            grad_gains.reshape(3, n, own_width).transpose(1, 0, 2).astype(BF),
-            ((0, 0), (0, 13), (0, 128 - own_width)),
-        )
+        flat = [t[0] for t in (queries, keys_rot, values, grad_attended)]
+        no_gain = jnp.zeros((width,), F32)
+        gain_rows = jnp.stack([no_gain, gain_two, gain_three, gains32[0]] + [no_gain] * 4)
+        layer = flat + [turn, qkv_w, stream0[0], normed1[0], grad_stream1[0], gain_rows]
         blocks = [
-            g.astype(BF).reshape(n, -1, g.shape[-1])
-            for g in (grad_gate_up, grad_qkv, grad_out, grad_down)
+            g.astype(BF).reshape(n, -1, g.shape[-1]) for g in (grad_gate_up, grad_out, grad_down)
         ]
         sums, grad_codes, grad_classes, squares = tail_phase(
-            grad_stream0[0].astype(BF),
+            layer,
             every_fact,
             head_pair,
-            blocks + [gain_blocks],
+            blocks,
+            [qkv_weight.shape, (16, 128)],
             (True, False, False, False, False),
             table_rows + -table_rows % 128,
             own_width,
             n,
         )
-        grad_gate_up, grad_qkv, grad_out, grad_down, gain_part = sums
+        grad_gate_up, grad_out, grad_down, grad_qkv, gain_part = sums
         grad_gains = gain_part[:3, :own_width]
         grad_classes = grad_classes[:own_width, :table_rows].T
     else:
+        queries, keys_rot, values, grad_attended = (
+            t.reshape(split4) for t in (queries, keys_rot, values, grad_attended)
+        )
+        probs32 = jax.nn.softmax(attention_scores(queries, keys_rot), -1)
+        probs = probs32.astype(BF)
+        grad_probs = dot("bqhd,bkhd->bhqk", grad_attended, values)
+        grad_values = dot("bhqk,bqhd->bkhd", probs, grad_attended)
+        grad_scores = probs32 * (grad_probs - jnp.sum(probs32 * grad_probs, -1, keepdims=True))
+        grad_scores = grad_scores.astype(BF)
+        scale = HEAD_DIM ** (-0.5)
+        grad_queries = dot("bhqk,bkhd->bqhd", grad_scores, keys_rot) * scale
+        grad_keys = dot("bhqk,bqhd->bkhd", grad_scores, queries) * scale
+        grad_mixed = jnp.concatenate(
+            [
+                rotate_back(grad_queries, cosine, sine).reshape(batch, length, width),
+                rotate_back(grad_keys, cosine, sine).reshape(batch, length, width),
+                grad_values.reshape(batch, length, width),
+            ],
+            -1,
+        ).astype(BF)
+        grad_qkv = dot("bte,btd->ed", grad_mixed, normed1)
+        grad_normed1 = dot("bte,ed->btd", grad_mixed, qkv_w)
+        grad_first, gain_one = norm_backward(stream0, inverse1, gains32[0], grad_normed1)
+        grad_stream0 = grad_stream1 + grad_first
+
+        grad_gains = jnp.stack([gain_one, gain_two, gain_three])
         blocks = [
             g.astype(BF).reshape(n, -1, g.shape[-1]) for g in (grad_qkv, grad_gate_up, grad_out, grad_down)
         ]

time: 482 us -> 456 us (0.946)
  matrix products: 41.6 us -> 20.9 us
  Pallas kernels: 362 us -> 376 us
  other arithmetic: 44.1 us -> 32.7 us
  local copies, waits for them, and re-layouts: 18.9 us -> 10.1 us
    dot_general x17 -> x6, matrix products: 38.8 us -> 20.9 us  [dot(): return jnp.einsum(subscripts, left, right, preferred_element_type=F32)]
    pallas_call x0 -> x1, Pallas kernels: none -> 16.2 us  [layer_forward(): pl.pallas_call(layer_kernel, out_shape=outs, in_specs=[vmem] * 3 + [hbm]...]
    convert_element_type x6 -> x0, other arithmetic: 8.26 us -> none  [the longest x1 3.44 us: local(): grad_scores = grad_scores.astype(BF)]
    unnamed x108 -> x82, local copies, waits for them, and re-layouts: 9.46 us -> 1.36 us
  transfers between devices with their start and end apart: 1 -> 1, of which waited for: 0 -> 1; matrix products, arithmetic and copies ran while one was open for 10% -> 7% of each run, Pallas kernels for 0% -> 0%
where the time goes in v5:
time: 456 us; the launch traced here: 448 us
  Pallas kernels  376 us (82%)
  other arithmetic  32.7 us (7%)
  matrix products  20.9 us (5%)
  local copies, waits for them, and re-layouts  10.1 us (2%)
  between operations  5.43 us (1%)
    pallas_call x1, Pallas kernels, tail_phase(): pl.pallas_call(functools.partial(tail_kernel, z_size, y_size, own_width,...  144 us
    pallas_call x1, Pallas kernels, head_phase(): pl.pallas_call(functools.partial(head_kernel, z_size, y_size, reps), out_...  116 us
    pallas_call x1, Pallas kernels, front(): pl.pallas_call(functools.partial(front_kernel, z_size, y_size, reps, own_...  101 us
    sub x8, other arithmetic, adam_update(): weight - rate * (first_hat / (jnp.sqrt(second_hat) + ADAM_EPS) + decay *...  21.1 us
    dot_general x6, matrix products, dot(): return jnp.einsum(subscripts, left, right, preferred_element_type=F32)  20.9 us
    pallas_call x1, Pallas kernels, layer_forward(): pl.pallas_call(layer_kernel, out_shape=outs, in_specs=[vmem] * 3 + [hbm]...  16.2 us
  transfers between devices with their start and end apart: 1, of which 1 were waited for; matrix products, arithmetic and copies ran while one was open for 7% of the time, Pallas kernels for 0%

profile of v5, /device:TPU:0, one launch (start us, length us, event | category | flops | bytes accessed | tf_op | source)
XLA Modules:
  0.0 448.5 jit_solution(13698867909051497371)
XLA Ops:
  4.0 0.9 convert_bitcast_fusion
  5.0 0.8 add_convert_fusion
  5.8 0.7 pad.22.class_b
  7.1 100.7 %front.1 = (bf16[16,256,768]{2,1,0:T(8,128)(2,1)}, bf16[16,144,768]{2,1,0:T(8,128)(2,1)}, bf16[16,48,768]{2,1,0:T(8,128)(2,1)}, bf16[16,48,2048]{2,1,0:T(8,128)(...) custom-call(f32[8,128]{1,0:T(8,128)} %fusion.19.facts, f32[1024,768]{1,0:T(8,128)} %code_table.1, ...), custom_call_target="tpu_custom_call" | custom-call | tf_op jit(solution)/shard_map/front/pallas_call | solution.py:138
  107.8 0.9 dynamic-slice_bitcast_fusion
  110.9 16.2 %layer.1 = (bf16[256,768]{1,0:T(8,128)(2,1)}, bf16[256,768]{1,0:T(8,128)(2,1)}, bf16[256,768]{1,0:T(8,128)(2,1)}, bf16[256,768]{1,0:T(8,128)(2,1)}, bf16[256,768...) custom-call(f32[256,768]{1,0:T(8,128)} %get-tuple-element.55.stream0, ...), custom_call_target="tpu_custom_call" | custom-call | tf_op jit(solution)/shard_map/layer/pallas_call | solution.py:1179
  127.0 115.8 %head.1 = (f32[256,768]{1,0:T(8,128)}, bf16[1024,768]{1,0:T(8,128)(2,1)}, f32[8,128]{1,0:T(8,128)}) custom-call(bf16[256,768]{1,0:T(8,128)(2,1)} %get-tuple-element.61.normed3, f32[1024,768]{1,0:T(8,128)} %head_weight.1, f32[2,16,8,128]{3,2,1,0:T(8,128)} %get-tuple-element.56.facts), custom_call_target="tpu_custom_call" | custom-call | tf_op jit(solution)/shard_map/head/pallas_call | solution.py:729
  242.9 1.6 collective-permute-start
  244.6 1.3 fusion.32
  246.1 1.4 multiply_reduce_fusion
  247.4 1.4 multiply_subtract_fusion.3
  248.8 1.3 multiply_reduce_fusion.3
  250.2 4.7 %fusion.7 = (bf16[256,2048]{1,0:T(8,128)(2,1)S(1)}, bf16[256,2048]{1,0:T(8,128)(2,1)S(1)}) fusion(f32[1,256,4096]{2,1,0:T(8,128)} %bitcast.60, bf16[768,2048]{1,0:T(8,128)(2,1)} %bitcast.56, f32[256,768]{1,0:T(8,128)S(1)} %multiply_subtract_fusion.3), kind=kOutput, calls=%fused_computation.25 | convolution fusion | flops 812318720 | bytes 10223616 | tf_op jit(solution)/shard_map/btd,df->btf/dot_general | solution.py:1201
  255.0 6.2 %multiply_reduce_fusion.1 = (f32[768]{0:T(1024)S(1)}, f32[256]{0:T(256)S(1)}, f32[256,768]{1,0:T(8,128)}) fusion(f32[256,768]{1,0:T(8,128)S(1)} %copy-done.10, f32[256]{0:T(256)S(1)} %add_rsqrt_fusion, f32[768]{0:T(1024)S(1)} %mul.471, bf16[4096,768]{1,0:T(8,128)(2,1)} %bitcast.50, bf16[256,2048]{1,0:T(8,128)(2,1)S(1)} %get-tuple-element.115, ...), kind=kOutput, calls=%fused_computation.29 | convolution fusion | flops 1615985664 | bytes 9969664 | tf_op jit(solution)/shard_map/btf,fd->btd/dot_general | solution.py:1201
  264.2 1.4 stack.37.gains
  265.5 1.7 subtract_add_fusion.grad_stream1
  267.3 1.2 convolution_convert_fusion.3.grad_attended
  268.5 1.5 convolution_convert_fusion.2
  270.0 2.7 convolution_convert_fusion.1
  272.8 4.5 %convolution_convert_fusion = bf16[4096,768]{1,0:T(8,128)(2,1)} fusion(bf16[256,768]{1,0:T(8,128)(2,1)S(1)} %copy-done.36, bf16[256,2048]{1,0:T(8,128)(2,1)S(1)} %copy-done.40, bf16[256,2048]{1,0:T(8,128)(2,1)S(1)} %copy-done.38), kind=kOutput, calls=%fused_computation | convolution fusion | flops 1617952768 | bytes 8781824 | tf_op jit(solution)/shard_map/btf,btd->fd/dot_general | solution.py:1201
  277.3 1.2 collective-permute-done.head_two
  278.5 1.1 copy-done.5
  279.6 143.8 %tail.1 = (f32[256,768]{1,0:T(8,128)}, f32[48,768]{1,0:T(8,128)}, f32[48,2048]{1,0:T(8,128)}, f32[144,768]{1,0:T(8,128)}, f32[16,128]{1,0:T(8,128)}, /*index=5*/...) custom-call(bf16[256,768]{1,0:T(8,128)(2,1)} %get-tuple-element.63.queries, ...), custom_call_target="tpu_custom_call" | custom-call | tf_op jit(solution)/shard_map/tail/pallas_call | solution.py:1063
  423.4 1.2 slice.51
  425.6 7.8 %multiply_subtract_fusion.1 = (f32[1024,768]{1,0:T(8,128)}, f32[1024,768]{1,0:T(8,128)}, f32[1024,768]{1,0:T(8,128)}) fusion(f32[1024,768]{1,0:T(8,128)S(1)} %copy-done.1, f32[1024,768]{1,0:T(8,128)} %get-tuple-element.76, f32[]{:T(128)S(6)} %min.3, f32[1024,768]{1,0:T(8,128)} %param.33, f32[1024,768]{1,0:T(8,128)} %param.34), kind=kLoop, calls=%fused_computation.10 | loop fusion | flops 11796480 | bytes 22020100 | tf_op jit(solution)/shard_map/sub | solution.py:1196
  433.4 2.0 multiply_subtract_fusion.6
  435.4 1.3 multiply_subtract_fusion.4
  436.8 0.8 multiply_subtract_fusion.7
  437.7 1.9 multiply_subtract_fusion.2
  439.6 1.2 multiply_subtract_fusion.5
  440.8 1.3 multiply_subtract_fusion.8
  442.1 4.8 %multiply_subtract_fusion = (f32[1024,768]{1,0:T(8,128)}, f32[1024,768]{1,0:T(8,128)}, f32[1024,768]{1,0:T(8,128)}) fusion(f32[1024,768]{1,0:T(8,128)S(1)} %copy-done.2, f32[]{:T(128)S(6)} %min.3, bf16[1024,768]{1,0:T(8,128)(2,1)S(1)} %copy-done.6, bf16[1024,768]{1,0:T(8,128)(2,1)S(1)} %copy-done.4, f32[1024,768]{1,0:T(8,128)S(1)} %copy-done.8, ...), kind=kLoop, calls=%fused_computation.8 | loop fusion | flops 14155776 | bytes 22020100 | tf_op jit(solution)/shard_map/sub | solution.py:1196
  (107 shorter events, 7.8 us)
Async XLA Ops:
  127.0 118.8 %copy-start.3 = (f32[256,768]{1,0:T(8,128)S(1)}, f32[256,768]{1,0:T(8,128)}, u32[]{:S(2)}) copy-start(f32[256,768]{1,0:T(8,128)} %get-tuple-element.66) | copy-start | bytes 2359300
  242.9 35.6 %collective-permute-start = (bf16[1024,768]{1,0:T(8,128)(2,1)}, bf16[1024,768]{1,0:T(8,128)(2,1)S(1)}, u32[]{:S(2)}, u32[]{:S(2)}) collective-permute-start(bf16[1024,768]{1,0:T(8,128)(2,1)} %get-tuple-element.71.head_one), channel_id=1, source_target_pairs={{0,1},{1,0},{2,3},{3,2},{4,5},{5,4},{6,7},{7,6},{8,9},{9,8},{10,11... | collective-permute-start | bytes 4718600 | tf_op jit(solution)/shard_map/ppermute | solution.py:1282
  250.1 4.8 %copy-start.33 = (f32[256]{0:T(256)}, f32[256]{0:T(256)S(1)}, u32[]{:S(2)}) copy-start(f32[256]{0:T(256)S(1)} %add_rsqrt_fusion) | copy-start | bytes 3076
  250.2 4.8 %copy-start.10 = (f32[256,768]{1,0:T(8,128)S(1)}, f32[256,768]{1,0:T(8,128)}, u32[]{:S(2)}) copy-start(f32[256,768]{1,0:T(8,128)} %get-tuple-element.68) | copy-start | bytes 2359300
  254.9 6.3 %copy-start.37 = (bf16[256,2048]{1,0:T(8,128)(2,1)}, bf16[256,2048]{1,0:T(8,128)(2,1)S(1)}, u32[]{:S(2)}) copy-start(bf16[256,2048]{1,0:T(8,128)(2,1)S(1)} %get-tuple-element.114) | copy-start | bytes 3145732
  254.9 6.3 %copy-start.39 = (bf16[256,2048]{1,0:T(8,128)(2,1)}, bf16[256,2048]{1,0:T(8,128)(2,1)S(1)}, u32[]{:S(2)}) copy-start(bf16[256,2048]{1,0:T(8,128)(2,1)S(1)} %get-tuple-element.115) | copy-start | bytes 3145732
  261.2 6.0 %copy-start.7 = (bf16[16,48,768]{2,1,0:T(8,128)(2,1)S(1)}, bf16[16,48,768]{2,1,0:T(8,128)(2,1)}, u32[]{:S(2)}) copy-start(bf16[16,48,768]{2,1,0:T(8,128)(2,1)} %get-tuple-element.58) | copy-start | bytes 3538948
  267.2 5.5 %copy-start = (f32[256,768]{1,0:T(8,128)}, f32[256,768]{1,0:T(8,128)S(1)}, u32[]{:S(2)}) copy-start(f32[256,768]{1,0:T(8,128)S(1)} %subtract_add_fusion.grad_stream1) | copy-start | bytes 2359300
  279.6 145.8 %copy-start.1 = (f32[1024,768]{1,0:T(8,128)S(1)}, f32[1024,768]{1,0:T(8,128)}, u32[]{:S(2)}) copy-start(f32[1024,768]{1,0:T(8,128)} %code_table.1) | copy-start | bytes 9437188
  425.4 8.0 %copy-start.15 = (f32[1001,48]{0,1:T(8,128)S(1)}, f32[1001,48]{0,1:T(8,128)}, u32[]{:S(2)}) copy-start(f32[1001,48]{0,1:T(8,128)} %param.35) | copy-start | bytes 576580
  425.4 8.0 %copy-start.27 = (f32[1001,48]{0,1:T(8,128)S(1)}, f32[1001,48]{0,1:T(8,128)}, u32[]{:S(2)}) copy-start(f32[1001,48]{0,1:T(8,128)} %param.36) | copy-start | bytes 576580
  425.4 8.0 %copy-start.28 = (f32[1001,48]{0,1:T(8,128)S(1)}, f32[1001,48]{0,1:T(8,128)}, u32[]{:S(2)}) copy-start(f32[1001,48]{0,1:T(8,128)} %param.37) | copy-start | bytes 576580
  425.4 10.0 %copy-start.12 = (f32[144,768]{1,0:T(8,128)S(1)}, f32[144,768]{1,0:T(8,128)}, u32[]{:S(2)}) copy-start(f32[144,768]{1,0:T(8,128)} %refs_1_.1) | copy-start | bytes 1327108
  425.4 10.0 %copy-start.20 = (f32[144,768]{1,0:T(8,128)S(1)}, f32[144,768]{1,0:T(8,128)}, u32[]{:S(2)}) copy-start(f32[144,768]{1,0:T(8,128)} %param.39) | copy-start | bytes 1327108
  425.4 10.0 %copy-start.21 = (f32[144,768]{1,0:T(8,128)S(1)}, f32[144,768]{1,0:T(8,128)}, u32[]{:S(2)}) copy-start(f32[144,768]{1,0:T(8,128)} %param.40) | copy-start | bytes 1327108
  425.4 10.0 %copy-start.22 = (f32[144,768]{1,0:T(8,128)S(1)}, f32[144,768]{1,0:T(8,128)}, u32[]{:S(2)}) copy-start(f32[144,768]{1,0:T(8,128)} %get-tuple-element.78) | copy-start | bytes 1327108
  425.4 11.3 %copy-start.19 = (f32[48,768]{1,0:T(8,128)S(1)}, f32[48,768]{1,0:T(8,128)}, u32[]{:S(2)}) copy-start(f32[48,768]{1,0:T(8,128)} %refs_2_.1) | copy-start | bytes 442372
  425.5 11.3 %copy-start.29 = (f32[48,768]{1,0:T(8,128)S(1)}, f32[48,768]{1,0:T(8,128)}, u32[]{:S(2)}) copy-start(f32[48,768]{1,0:T(8,128)} %param.42) | copy-start | bytes 442372
  425.5 11.3 %copy-start.30 = (f32[48,768]{1,0:T(8,128)S(1)}, f32[48,768]{1,0:T(8,128)}, u32[]{:S(2)}) copy-start(f32[48,768]{1,0:T(8,128)} %param.43) | copy-start | bytes 442372
  425.5 11.3 %copy-start.31 = (f32[48,768]{1,0:T(8,128)S(1)}, f32[48,768]{1,0:T(8,128)}, u32[]{:S(2)}) copy-start(f32[48,768]{1,0:T(8,128)} %get-tuple-element.79) | copy-start | bytes 442372
  425.5 12.1 %copy-start.16 = (f32[256,768]{1,0:T(8,128)S(1)}, f32[256,768]{1,0:T(8,128)}, u32[]{:S(2)}) copy-start(f32[256,768]{1,0:T(8,128)} %param.45) | copy-start | bytes 2359300
  425.5 12.1 %copy-start.17 = (f32[256,768]{1,0:T(8,128)S(1)}, f32[256,768]{1,0:T(8,128)}, u32[]{:S(2)}) copy-start(f32[256,768]{1,0:T(8,128)} %param.46) | copy-start | bytes 2359300
  425.5 12.1 %copy-start.18 = (f32[256,768]{1,0:T(8,128)S(1)}, f32[256,768]{1,0:T(8,128)}, u32[]{:S(2)}) copy-start(f32[256,768]{1,0:T(8,128)} %get-tuple-element.80) | copy-start | bytes 2359300
  425.5 14.0 %copy-start.24 = (f32[48,2048]{1,0:T(8,128)S(1)}, f32[48,2048]{1,0:T(8,128)}, u32[]{:S(2)}) copy-start(f32[48,2048]{1,0:T(8,128)} %param.48) | copy-start | bytes 1179652
  425.5 14.0 %copy-start.25 = (f32[48,2048]{1,0:T(8,128)S(1)}, f32[48,2048]{1,0:T(8,128)}, u32[]{:S(2)}) copy-start(f32[48,2048]{1,0:T(8,128)} %param.49) | copy-start | bytes 1179652
  425.6 14.0 %copy-start.26 = (f32[48,2048]{1,0:T(8,128)S(1)}, f32[48,2048]{1,0:T(8,128)}, u32[]{:S(2)}) copy-start(f32[48,2048]{1,0:T(8,128)} %get-tuple-element.81) | copy-start | bytes 1179652
  433.4 4.2 copy-start.11
  433.4 8.7 %copy-start.9 = (f32[1024,768]{1,0:T(8,128)S(1)}, f32[1024,768]{1,0:T(8,128)}, u32[]{:S(2)}) copy-start(f32[1024,768]{1,0:T(8,128)} %param.52) | copy-start | bytes 9437188
  435.4 6.7 %copy-start.8 = (f32[1024,768]{1,0:T(8,128)S(1)}, f32[1024,768]{1,0:T(8,128)}, u32[]{:S(2)}) copy-start(f32[1024,768]{1,0:T(8,128)} %param.51) | copy-start | bytes 9437188
  437.7 4.4 copy-start.2
  437.7 4.4 copy-start.4
  437.7 4.4 copy-start.6
  (10 other events, 27.3 us)

commit v6 on v5

--- a/solution.py
+++ b/solution.py
@@ -743,89 +743,91 @@
     )(normed3, head_weight, facts)
 
 
-def tail_kernel(z_size, y_size, own_width, split, counts, queries, keys, values, grad_attended, turn,
-                qkv_w, stream0, normed1, grad_stream1, gains, facts, head_one, head_two, *refs):
+def tail_kernel(z_size, y_size, own_width, split, counts, queries, keys, values, attended, normed1, normed2,
+                stream0, stream1, stream2, grad_normed3, turn, gains, facts, head_one, *refs):
     count = len(split)
-    early = count - 2
-    qkv_at, gain_at = early, early + 1
-    grads, refs = refs[:early], refs[early:]
+    weights, refs = refs[: count - 1], refs[count - 1 :]
     sums, refs = refs[:count], refs[count:]
-    code_sum, class_sum, squares, refs = refs[0], refs[1], refs[2], refs[3:]
-    accs, refs = refs[:count], refs[count:]
+    code_out, code_in, class_sum, head_two, squares, refs = *refs[:5], refs[5:]
+    grads, refs = refs[:count], refs[count:]
     core_in, refs = refs[:count], refs[count:]
     x_in, refs = refs[:count], refs[count:]
     y_in, refs = refs[:count], refs[count:]
     z_in, refs = refs[:count], refs[count:]
     trade, refs = refs[:count], refs[count:]
-    (whole, code_out, code_in, rows_out, given, grad_mixed, grad_qkv, gain_blocks, grad_stream0, z_sems, y_sems, c_sems, own_sems, rc_sems, rx_sems,
-     ry_sems, rz_sems, tr_sems, co_sems, fr_sems, sq_sems) = refs
+    (whole, rows_out, given, grad_mixed, grad_gated, hidden, grad_stream1, grad_attended, grad_stream0,
+     z_sems, y_sems, c_sems, own_sems, rc_sems, rx_sems,
+     ry_sems, rz_sems, tr_sems, co_sems, fr_sems, hd_sems, sq_sems) = refs
     p = Place(z_size, y_size, 2)
     n, me, x = p.n, p.me, p.x
     length, width = stream0.shape
+    hidden_width = hidden.shape[1]
     own_rows = code_out.shape[0]
+    gate_at, out_at, down_at, qkv_at, gain_at = range(5)
+    late = [qkv_at, gain_at]
+    halved = [k for k in (down_at, gate_at, out_at) if split[k]]
+    plain = [k for k in (down_at, gate_at, out_at) if not split[k]]
+    for k in range(count - 1):
+        pltpu.make_async_copy(weights[k], grads[k], own_sems.at[k]).start()
     p.greet(True)
     mate = (me, 1 - x)
     spread = Spread(p, whole, z_sems, y_sems, c_sems)
+    send(head_one, head_two, hd_sems, (), mate)
+
+    def weight(k):
+        pltpu.make_async_copy(weights[k], grads[k], own_sems.at[k]).wait()
 
     def slot_of(dz, dy):
         return dz * y_size + dy
 
     order = [(dz, dy) for dz in range(z_size - 1, -1, -1) for dy in range(y_size - 1, -1, -1)]
-    halved = [k for k in range(early) if split[k]]
-    plain = [k for k in range(early) if not split[k]]
-    late = [qkv_at, gain_at]
 
     def block_of(k, f):
-        if k == qkv_at:
-            rows = counts[k]
-            return grad_qkv.at[pl.ds(pl.multiple_of(f * rows, rows), rows)]
-        return gain_blocks.at[f] if k == gain_at else grads[k].at[f]
+        rows = counts[k]
+        return grads[k].at[pl.ds(pl.multiple_of(f * rows, rows), rows)]
 
     def to_twin(kinds):
         for dz, dy in order:
             slot = slot_of(dz, dy)
             for k in kinds:
                 send(block_of(k, p.at(dz, dy, 1)), core_in[k].at[slot], rc_sems, (k, slot), p.twin())
-                pltpu.make_async_copy(
-                    block_of(k, p.at(dz, dy)), accs[k].at[slot], own_sems.at[k, slot]
-                ).start()
-
-    to_twin(halved)
-    to_twin(plain)
-
-    def part(k, which):
-        rows = counts[k] // 2
-        return pl.ds(pl.multiple_of(which * rows, rows), rows)
+
+    def half_of(k, ref, which):
+        columns = sums[k].shape[1] // 2
+        return ref.at[:, pl.ds(pl.multiple_of(which * columns, columns), columns)]
 
     def ref_of(k, ref, which):
-        return ref.at[part(k, which)] if split[k] else ref
+        return half_of(k, ref, which) if split[k] else ref
 
     def twin_sums(kinds, dz):
         def body(dy, carry):
             slot = slot_of(dz, dy)
             for k in kinds:
-                pltpu.make_async_copy(accs[k].at[slot], accs[k].at[slot], own_sems.at[k, slot]).wait()
                 arrival(core_in[k].at[slot], rc_sems, (k, slot))
-                accs[k][slot] = (accs[k][slot].astype(F32) + core_in[k][slot].astype(F32)).astype(BF)
+                own = block_of(k, p.at(dz, dy))[...].astype(F32)
+                core_in[k][slot] = (own + core_in[k][slot].astype(F32)).astype(BF)
                 if split[k]:
-                    send(accs[k].at[slot, part(k, 1 - x)], x_in[k].at[slot], rx_sems, (k, slot), mate)
+                    send(half_of(k, core_in[k].at[slot], 1 - x), x_in[k].at[slot], rx_sems, (k, slot), mate)
             return carry
 
         lax.fori_loop(0, y_size, body, 0)
+
+    def y_slot(dz, dy):
+        return dz * (y_size - 1) + dy - 1
 
     def send_y(kinds, dz):
         for dy in range(1, y_size):
-            slot = slot_of(dz, dy)
             for k in kinds:
-                source = ref_of(k, accs[k].at[slot], x)
-                send(source, y_in[k].at[slot], ry_sems, (k, slot), (p.at(0, dy), x))
+                source = ref_of(k, core_in[k].at[slot_of(dz, dy)], x)
+                at = y_slot(dz, dy)
+                send(source, y_in[k].at[at], ry_sems, (k, at), (p.at(0, dy), x))
 
     def take_x(dz):
         def body(dy, carry):
             slot = slot_of(dz, dy)
             for k in halved:
                 arrival(x_in[k].at[slot], rx_sems, (k, slot))
-                mine = accs[k].at[slot, part(k, x)]
+                mine = half_of(k, core_in[k].at[slot], x)
                 mine[...] = (mine[...].astype(F32) + x_in[k][slot].astype(F32)).astype(BF)
             return carry
 
@@ -834,18 +836,85 @@
 
     def take_y(kinds, dz):
         for k in kinds:
-            mine = ref_of(k, accs[k].at[slot_of(dz, 0)], x)
+            mine = ref_of(k, core_in[k].at[slot_of(dz, 0)], x)
             total = mine[...].astype(F32)
             for dy in range(1, y_size):
-                slot = slot_of(dz, dy)
-                arrival(y_in[k].at[slot], ry_sems, (k, slot))
-                total = total + y_in[k][slot].astype(F32)
+                at = y_slot(dz, dy)
+                arrival(y_in[k].at[at], ry_sems, (k, at))
+                total = total + y_in[k][at].astype(F32)
             mine[...] = total.astype(BF)
             if dz:
-                send(mine, z_in[k].at[dz], rz_sems, (k, dz), (p.at(dz, 0), x))
+                send(mine, z_in[k].at[dz - 1], rz_sems, (k, dz - 1), (p.at(dz, 0), x))
+
+    def settle(kinds):
+        for k in kinds:
+            mine = ref_of(k, core_in[k].at[0], x)
+            total = mine[...].astype(F32)
+            for dz in range(1, z_size):
+                arrival(z_in[k].at[dz - 1], rz_sems, (k, dz - 1))
+                total = total + z_in[k][dz - 1].astype(F32)
+            source = ref_of(k, trade[k].at[0], x)
+            source[...] = total.astype(BF)
+            target = source if split[k] else trade[k].at[1]
+            send(source, target, tr_sems, (k,), mate)
+
+    def collect(kinds):
+        summed = jnp.zeros((1, 1), F32)
+        for k in kinds:
+            if split[k]:
+                arrival(half_of(k, trade[k].at[0], 1 - x), tr_sems, (k,))
+                total = trade[k][0].astype(F32)
+            else:
+                arrival(trade[k].at[1], tr_sems, (k,))
+                total = trade[k][0].astype(F32) + trade[k][1].astype(F32)
+            sums[k][...] = total
+            summed = summed + square(total)
+        return summed
 
     def square(value):
         return jnp.sum(jnp.sum(value * value, 0, keepdims=True), 1, keepdims=True)
+
+    def norm_back(stream, row, grad_out):
+        inverse = lax.rsqrt(jnp.mean(stream * stream, -1, keepdims=True) + NORM_EPS)
+        weighted = grad_out * gains[row : row + 1, :]
+        inner = jnp.mean(weighted * stream, -1, keepdims=True)
+        grad = inverse * weighted - stream * (inverse * inverse * inverse) * inner
+        return grad, jnp.sum(grad_out * stream * inverse, 0, keepdims=True)
+
+    grad_stream2, gain_three = norm_back(stream2[...], 2, grad_normed3[...])
+    grad_stream1[...] = grad_stream2
+    grad_stream0[...] = grad_stream2.astype(BF)
+    weight(gate_at)
+    weight(down_at)
+    step = 512
+    for at in range(0, hidden_width, step):
+        gate = product(normed2[...], grads[gate_at][at : at + step, :], BY_LANES)
+        up = product(normed2[...], grads[gate_at][hidden_width + at : hidden_width + at + step, :], BY_LANES)
+        back = jnp.dot(grad_stream0[...], grads[down_at][:, at : at + step], preferred_element_type=F32)
+        sigma = 1.0 / (1.0 + jnp.exp(-gate))
+        hidden[:, at : at + step] = (gate * sigma * up).astype(BF)
+        grad_gated[:, at : at + step] = (back * up * sigma * (1.0 + gate * (1.0 - sigma))).astype(BF)
+        grad_gated[:, hidden_width + at : hidden_width + at + step] = (back * gate * sigma).astype(BF)
+    for at in range(0, hidden_width, step):
+        grads[down_at][:, at : at + step] = product(
+            grad_stream0[...], hidden[:, at : at + step], BY_ROWS
+        ).astype(BF)
+    to_twin([down_at])
+    grad_normed2 = jnp.dot(grad_gated[...], grads[gate_at][...], preferred_element_type=F32)
+    for at in range(0, 2 * hidden_width, step):
+        grads[gate_at][at : at + step, :] = product(
+            grad_gated[:, at : at + step], normed2[...], BY_ROWS
+        ).astype(BF)
+    to_twin([gate_at])
+    grad_middle, gain_two = norm_back(stream1[...], 1, grad_normed2)
+    grad_stream1[...] = grad_stream1[...] + grad_middle
+    grad_stream0[...] = grad_stream1[...].astype(BF)
+    weight(out_at)
+    grad_attended[...] = jnp.dot(
+        grad_stream0[...], grads[out_at][...], preferred_element_type=F32
+    ).astype(BF)
+    grads[out_at][...] = product(grad_stream0[...], attended[...], BY_ROWS).astype(BF)
+    to_twin([out_at])
 
     lane = lax.broadcasted_iota(jnp.int32, (length, 128), 1)
     low = lax.rem(lane, HEAD_DIM) < HEAD_DIM // 2
@@ -859,7 +928,8 @@
         return grad * turn[0] + other
 
     def pair(j, carry):
-        at = pl.ds(pl.multiple_of(j * 128, 128), 128)
+        base = pl.multiple_of(j * 128, 128)
+        at = pl.ds(base, 128)
         q, k, v, grad = queries[:, at], keys[:, at], values[:, at], grad_attended[:, at]
         q_two, grad_two = both_heads(q), both_heads(grad)
         probs = attention_probs(q_two, k)
@@ -870,66 +940,37 @@
         grad_q = one_row(jnp.dot(grad_scores, k, preferred_element_type=F32))
         grad_k = product(grad_scores, q_two, BY_ROWS)
         grad_mixed[:, at] = turn_back(grad_q * scale).astype(BF)
-        base = pl.multiple_of(j * 128, 128)
         grad_mixed[:, pl.ds(width + base, 128)] = turn_back(grad_k * scale).astype(BF)
         grad_mixed[:, pl.ds(2 * width + base, 128)] = grad_v.astype(BF)
         return carry
 
-    def settle(kinds):
-        for k in kinds:
-            mine = ref_of(k, accs[k].at[0], x)
-            total = mine[...].astype(F32)
-            for dz in range(1, z_size):
-                arrival(z_in[k].at[dz], rz_sems, (k, dz))
-                total = total + z_in[k][dz].astype(F32)
-            source = ref_of(k, trade[k].at[0], x)
-            source[...] = total.astype(BF)
-            target = trade[k].at[0, part(k, x)] if split[k] else trade[k].at[1]
-            send(source, target, tr_sems, (k,), mate)
-
-    def collect(kinds):
-        summed = jnp.zeros((1, 1), F32)
-        for k in kinds:
-            if split[k]:
-                arrival(trade[k].at[0, part(k, 1 - x)], tr_sems, (k,))
-                total = trade[k][0].astype(F32)
-            else:
-                arrival(trade[k].at[1], tr_sems, (k,))
-                total = trade[k][0].astype(F32) + trade[k][1].astype(F32)
-            sums[k][...] = total
-            summed = summed + square(total)
-        return summed
-
     pairs = width // 128
     for s in range(z_size):
         dz = z_size - 1 - s
-        lax.fori_loop(s * pairs // z_size, (s + 1) * pairs // z_size, pair, 0)
         twin_sums(halved, dz)
         twin_sums(plain, dz)
         send_y(plain, dz)
-
-    grad_out = jnp.dot(grad_mixed[...], qkv_w[...], preferred_element_type=F32)
-    stream = stream0[...]
-    inverse = lax.rsqrt(jnp.mean(stream * stream, -1, keepdims=True) + NORM_EPS)
-    weighted = grad_out * gains[3:4, :]
-    inner = jnp.mean(weighted * stream, -1, keepdims=True)
-    grad_first = inverse * weighted - stream * (inverse * inverse * inverse) * inner
+        lax.fori_loop(s * pairs // z_size, (s + 1) * pairs // z_size, pair, 0)
+
+    weight(qkv_at)
+    grad_normed1 = jnp.dot(grad_mixed[...], grads[qkv_at][...], preferred_element_type=F32)
+    grad_first, gain_one = norm_back(stream0[...], 0, grad_normed1)
     grad_stream0[...] = (grad_stream1[...] + grad_first).astype(BF)
     spread.start(grad_stream0)
     whole[me] = grad_stream0[...]
-    gain_one = jnp.sum(grad_out * stream * inverse, 0, keepdims=True)
-    third = grad_qkv.shape[0] // 6
-    for r in range(6):
-        at = pl.ds(r * third, third)
-        grad_qkv[at, :] = product(grad_mixed[:, r * third : (r + 1) * third], normed1[...], BY_ROWS).astype(BF)
+    step = 3 * width // 6
+    for at in range(0, 3 * width, step):
+        grads[qkv_at][at : at + step, :] = product(
+            grad_mixed[:, at : at + step], normed1[...], BY_ROWS
+        ).astype(BF)
     row = lax.broadcasted_iota(jnp.int32, (16, width), 0)
-    spare = jnp.concatenate([gains[...], gains[...]], 0)
-    all_gains = jnp.where(row == 0, gain_one, jnp.where(row < 3, spare, 0.0))
+    all_gains = jnp.where(row == 2, gain_three, 0.0)
+    all_gains = jnp.where(row == 0, gain_one, jnp.where(row == 1, gain_two, all_gains))
 
     def gain_block(f, carry):
         turned = pltpu.roll(all_gains, lax.rem(width - f * own_width, width), 1)[:, :128]
         own = lax.broadcasted_iota(jnp.int32, turned.shape, 1) < own_width
-        gain_blocks[f] = jnp.where(own, turned, 0.0).astype(BF)
+        block_of(gain_at, f)[...] = jnp.where(own, turned, 0.0).astype(BF)
         return carry
 
     lax.fori_loop(0, n, gain_block, 0)
@@ -948,7 +989,7 @@
     for z in range(z_size):
         spread.take_twin(z)
 
-    rows_out[x] = whole[:, 0:8, :].astype(F32)
+    rows_out[x] = whole[:, 0:16, :].astype(F32)[:, 0, :]
     send(rows_out.at[x], rows_out.at[x], fr_sems, (), mate)
 
     blocks = 4
@@ -975,32 +1016,29 @@
         lax.fori_loop(r * blocks // z_size, (r + 1) * blocks // z_size, code_block, 0)
         take_y(halved, z_size - 1 - r)
         take_y(late, z_size - 1 - r)
-    settle(halved + plain)
-
+    settle(plain + halved)
+
+    arrival(head_two, hd_sems, ())
     total_squares = square(head_one[...].astype(F32) + head_two[...].astype(F32))
 
     arrival(rows_out.at[1 - x], fr_sems, ())
-    firsts = rows_out[:, :, 0, :].reshape(2 * n, width)
+    firsts = rows_out[...].reshape(2 * n, width)
     shift = lax.rem(width - me * own_width, width)
     firsts = pltpu.roll(firsts, shift, 1)[:, :128]
     firsts = jnp.where(lax.broadcasted_iota(jnp.int32, firsts.shape, 1) < own_width, firsts, 0.0)
     classes = facts[:, :, 4, :].reshape(2 * n, 128)[:, 0:1]
     class_iota = lax.broadcasted_iota(jnp.int32, (2 * n, class_sum.shape[1]), 1).astype(F32)
     hot = jnp.where(class_iota == classes, 1.0, 0.0).astype(BF)
-    class_grad = lax.dot_general(
-        firsts.astype(BF), hot, (((0,), (0,)), ((), ())), preferred_element_type=F32
-    )
+    class_grad = product(firsts.astype(BF), hot, BY_ROWS)
     class_sum[...] = class_grad
     total_squares = total_squares + square(class_grad)
 
-    total_squares = total_squares + collect(halved + plain)
+    total_squares = total_squares + collect(plain + halved)
     settle(late)
     for r in range(blocks):
         at = pl.ds(r * rows, rows)
         arrival(code_in.at[at], co_sems, (r,))
-        total = code_out[at].astype(F32) + code_in[at].astype(F32)
-        code_sum[at] = total
-        total_squares = total_squares + square(total)
+        total_squares = total_squares + square(code_out[at].astype(F32) + code_in[at].astype(F32))
     total_squares = total_squares + collect(late)
 
     given[me] = jnp.broadcast_to(total_squares, (8, 128))
@@ -1008,6 +1046,7 @@
         send(given.at[me], given.at[me], sq_sems, (k,), (lax.rem(me + k, n), x))
 
     spread.finish()
+    departure(head_one, hd_sems, ())
     departure(rows_out.at[x], fr_sems, ())
     for r in range(blocks):
         departure(code_out.at[pl.ds(r * rows, rows)], co_sems, (r,))
@@ -1015,14 +1054,14 @@
         departure(ref_of(k, trade[k].at[0], x), tr_sems, (k,))
         for dz in range(z_size):
             if dz:
-                departure(z_in[k].at[dz], rz_sems, (k, dz))
+                departure(z_in[k].at[dz - 1], rz_sems, (k, dz - 1))
             for dy in range(y_size):
                 slot = slot_of(dz, dy)
                 departure(core_in[k].at[slot], rc_sems, (k, slot))
                 if split[k]:
                     departure(x_in[k].at[slot], rx_sems, (k, slot))
                 if dy:
-                    departure(y_in[k].at[slot], ry_sems, (k, slot))
+                    departure(y_in[k].at[y_slot(dz, dy)], ry_sems, (k, y_slot(dz, dy)))
     for k in range(1, n):
         arrival(given.at[0], sq_sems, (k,))
     squares[...] = jnp.sum(given[...], 0)
@@ -1030,54 +1069,47 @@
         departure(given.at[0], sq_sems, (k,))
 
 
-def tail_scratch(n, length, width, own_rows, shapes, split):
+def tail_phase(layer, facts, head_one, weights, split, class_rows, own_width, n):
     z_size, y_size = geometry(n)
-    spots = z_size * y_size
-    count = len(shapes)
+    length, width = layer[0].shape
+    hidden_width = weights[2].shape[1]
+    own_rows = head_one.shape[0]
+    shapes = [(w.shape[0] // n, w.shape[1]) for w in weights] + [(16, 128)]
+    count, spots = len(shapes), z_size * y_size
+    halves = [(s[0], s[1] // 2) if h else s for s, h in zip(shapes, split)]
     dma = pltpu.SemaphoreType.DMA
-    halves = [(s[0] // 2, s[1]) if h else s for s, h in zip(shapes, split)]
-    buffers = [((spots,) + s, BF) for s in shapes] * 2
+    buffers = [((n * s[0], s[1]), BF) for s in shapes]
+    buffers += [((spots,) + s, BF) for s in shapes]
     buffers += [((spots,) + s if h else (16, 128), BF) for s, h in zip(halves, split)]
-    buffers += [((spots,) + s, BF) for s in halves]
-    buffers += [((z_size,) + s, BF) for s in halves]
+    buffers += [((z_size * (y_size - 1),) + s, BF) for s in halves]
+    buffers += [((z_size - 1,) + s, BF) for s in halves]
     buffers += [((2,) + s, BF) for s in shapes]
-    buffers += [((n, length, width), BF), ((own_rows, width), BF), ((own_rows, width), BF),
-                ((2, n, 8, width), F32), ((n, 8, 128), F32), ((length, 3 * width), BF),
-                ((3 * width, width), BF), ((n, 16, 128), BF), ((length, width), BF)]
+    buffers += [((n, length, width), BF), ((2, n, width), F32), ((n, 8, 128), F32),
+                ((length, 3 * width), BF), ((length, 2 * hidden_width), BF), ((length, hidden_width), BF),
+                ((length, width), F32), ((length, width), BF), ((length, width), BF)]
     sems = [
         dma((2, 2, z_size)), dma((2, z_size, y_size)), dma((2, z_size, y_size)),
-        dma((count, spots)), dma((2, count, spots)), dma((2, count, spots)), dma((2, count, spots)),
-        dma((2, count, z_size)), dma((2, count)), dma((2, 4)), dma((2,)), dma((2, n)),
+        dma((count,)), dma((2, count, spots)), dma((2, count, spots)), dma((2, count, spots)),
+        dma((2, count, z_size)), dma((2, count)), dma((2, 4)), dma((2,)), dma((2,)), dma((2, n)),
     ]
-    return buffers, sems
-
-
-def tail_phase(layer, facts, heads, grads, late, split, class_rows, own_width, n):
-    z_size, y_size = geometry(n)
-    length, width = layer[0].shape
-    own_rows = heads[0].shape[0]
-    shapes = [g.shape[1:] for g in grads] + late
-    buffers, sems = tail_scratch(n, length, width, own_rows, shapes, split)
     vmem, hbm = pl.BlockSpec(memory_space=pltpu.VMEM), pl.BlockSpec(memory_space=pl.ANY)
     counts = tuple(s[0] for s in shapes)
+    half = jax.ShapeDtypeStruct((own_rows, width), BF)
     outs = pl.pallas_call(
         functools.partial(tail_kernel, z_size, y_size, own_width, split, counts),
         out_shape=[jax.ShapeDtypeStruct(s, F32) for s in shapes]
-        + [
-            jax.ShapeDtypeStruct((own_rows, width), F32),
-            jax.ShapeDtypeStruct((128, class_rows), F32),
-            jax.ShapeDtypeStruct((8, 128), F32),
-        ],
-        in_specs=[vmem] * (len(layer) + 3) + [hbm] * len(grads),
-        out_specs=[vmem] * (len(shapes) + 3),
+        + [half, half, jax.ShapeDtypeStruct((128, class_rows), F32), half,
+           jax.ShapeDtypeStruct((8, 128), F32)],
+        in_specs=[vmem] * (len(layer) + 2) + [hbm] * len(weights),
+        out_specs=[vmem] * (count + 5),
         scratch_shapes=[pltpu.VMEM(shape, kind) for shape, kind in buffers] + sems,
         compiler_params=pltpu.CompilerParams(
             collective_id=2, has_side_effects=True, vmem_limit_bytes=60 * 2**20
         ),
         name="tail",
-    )(*layer, facts, *heads, *grads)
-    many = len(shapes)
-    return outs[:many], outs[many], outs[many + 1], outs[many + 2][0, 0]
+    )(*layer, facts, head_one, *weights)
+    code_one, code_two, class_sum, head_two, squares = outs[count:]
+    return outs[:count], (code_one, code_two), class_sum, head_two, squares[0, 0]
 
 
 BY_ROWS = (((0,), (0,)), ((), ()))
@@ -1111,8 +1143,8 @@
 
 
 def layer_kernel(stream0, gains, turn, qkv_hbm, out_hbm, gate_hbm, down_hbm,
-                 normed1, queries, keys, values, attended, stream1, normed2, gated, hidden, stream2, normed3,
-                 qkv_w, out_w, gate_w, down_w, sems):
+                 normed1, queries, keys, values, attended, stream1, normed2, stream2, normed3,
+                 hidden, qkv_w, out_w, gate_w, down_w, sems):
     moves = [
         pltpu.make_async_copy(src, dst, sems.at[i])
         for i, (src, dst) in enumerate(
@@ -1161,8 +1193,6 @@
     for at in range(0, hidden_width, step):
         gate = product(normed2[...], gate_w[at : at + step, :], BY_LANES)
         up = product(normed2[...], gate_w[hidden_width + at : hidden_width + at + step, :], BY_LANES)
-        gated[:, at : at + step] = gate
-        gated[:, hidden_width + at : hidden_width + at + step] = up
         hidden[:, at : at + step] = (gate * (1.0 / (1.0 + jnp.exp(-gate))) * up).astype(BF)
     moves[3].wait()
     stream2[...] = stream1[...] + product(hidden[...], down_w[...], BY_LANES)
@@ -1174,14 +1204,14 @@
     hidden_width = down_w.shape[1]
     vmem, hbm = pl.BlockSpec(memory_space=pltpu.VMEM), pl.BlockSpec(memory_space=pl.ANY)
     half, full = jax.ShapeDtypeStruct((length, width), BF), jax.ShapeDtypeStruct((length, width), F32)
-    outs = [half] * 5 + [full, half, jax.ShapeDtypeStruct((length, 2 * hidden_width), F32)]
-    outs += [jax.ShapeDtypeStruct((length, hidden_width), BF), full, half]
+    outs = [half] * 5 + [full, half, full, half]
     return pl.pallas_call(
         layer_kernel,
         out_shape=outs,
         in_specs=[vmem] * 3 + [hbm] * 4,
         out_specs=[vmem] * len(outs),
-        scratch_shapes=[pltpu.VMEM(w.shape, BF) for w in (qkv_w, out_w, gate_w, down_w)]
+        scratch_shapes=[pltpu.VMEM((length, hidden_width), BF)]
+        + [pltpu.VMEM(w.shape, BF) for w in (qkv_w, out_w, gate_w, down_w)]
         + [pltpu.SemaphoreType.DMA((4,))],
         compiler_params=pltpu.CompilerParams(vmem_limit_bytes=56 * 2**20),
         name="layer",
@@ -1261,26 +1291,18 @@
     cosine, sine = rotary_tables(length, HEAD_DIM)
     turn = jnp.stack([jnp.concatenate([t, t], -1) for t in (cosine, sine)])
     split4 = (batch, length, heads, HEAD_DIM)
+    gain_rows = jnp.pad(gains32, ((0, 5), (0, 0)))
     kept = layer_forward(
-        stream0[0], jnp.pad(gains32, ((0, 5), (0, 0))), turn, qkv_w, out_w, gate_w, down_w
+        stream0[0], gain_rows, turn, qkv_w, out_w, gate_w, down_w
     )
-    (normed1, queries, keys_rot, values, attended, stream1, normed2, gated, hidden, stream2, normed3) = (
+    (normed1, queries, keys_rot, values, attended, stream1, normed2, stream2, normed3) = (
         t[None] for t in kept
     )
-    gate_part = gated[..., :hidden_width]
-    up_part = gated[..., hidden_width:]
-    inverse1, inverse2, inverse3 = (
-        lax.rsqrt(jnp.mean(t * t, -1, keepdims=True) + NORM_EPS) for t in (stream0, stream1, stream2)
-    )
-
     head_b = head_weight.astype(BF)
     in_kernel = reps == 2 and size_of(head_scratch(n, length, width, own_rows, reps)[0]) < 52 * 2**20
     if in_kernel:
         grad_normed3, grad_head, totals = head_phase(normed3[0], head_weight, every_fact, reps, n)
-        grad_normed3 = grad_normed3[None]
         loss_sum, token_count = totals[0, 0], totals[1, 0]
-        head_pair = (grad_head, lax.ppermute(grad_head, "rep", [(0, 1), (1, 0)]))
-        grad_head = head_pair[0].astype(F32) + head_pair[1].astype(F32)
     else:
         token_count = lax.psum(jnp.sum(all_counted), "rep")
         normed3_all = lax.all_gather(normed3, "fsdp", axis=0, tiled=True).reshape(tokens, width)
@@ -1302,44 +1324,48 @@
         grad_normed3 = grad_normed3.astype(F32)
         grad_head = dot("tv,td->vd", grad_logits, normed3_all)
 
-    grad_stream2, gain_three = norm_backward(stream2, inverse3, gains32[2], grad_normed3)
-    grad_branch = grad_stream2.astype(BF)
-    grad_down = dot("btd,btf->df", grad_branch, hidden)
-    grad_hidden = dot("btd,df->btf", grad_branch, down_w)
-    sigma = jax.nn.sigmoid(gate_part)
-    grad_gate = grad_hidden * up_part * sigma * (1.0 + gate_part * (1.0 - sigma))
-    grad_up = grad_hidden * gate_part * sigma
-    grad_gated = jnp.concatenate([grad_gate, grad_up], -1).astype(BF)
-    grad_gate_up = dot("btf,btd->fd", grad_gated, normed2)
-    grad_normed2 = dot("btf,fd->btd", grad_gated, gate_w)
-    grad_middle, gain_two = norm_backward(stream1, inverse2, gains32[1], grad_normed2)
-    grad_stream1 = grad_stream2 + grad_middle
-    grad_attn = grad_stream1.astype(BF)
-    grad_out = dot("bte,btd->ed", grad_attn, attended)
-    grad_attended = dot("bte,ed->btd", grad_attn, out_w).astype(BF)
     if in_kernel:
-        flat = [t[0] for t in (queries, keys_rot, values, grad_attended)]
-        no_gain = jnp.zeros((width,), F32)
-        gain_rows = jnp.stack([no_gain, gain_two, gain_three, gains32[0]] + [no_gain] * 4)
-        layer = flat + [turn, qkv_w, stream0[0], normed1[0], grad_stream1[0], gain_rows]
-        blocks = [
-            g.astype(BF).reshape(n, -1, g.shape[-1]) for g in (grad_gate_up, grad_out, grad_down)
-        ]
-        sums, grad_codes, grad_classes, squares = tail_phase(
+        kinds = (queries, keys_rot, values, attended, normed1, normed2, stream0, stream1, stream2)
+        layer = [t[0] for t in kinds] + [grad_normed3, turn, gain_rows]
+        sums, codes, grad_classes, head_two, squares = tail_phase(
             layer,
             every_fact,
-            head_pair,
-            blocks,
-            [qkv_weight.shape, (16, 128)],
-            (True, False, False, False, False),
+            grad_head,
+            [gate_w, out_w, down_w, qkv_w],
+            (True, True, False, False, False),
             table_rows + -table_rows % 128,
             own_width,
             n,
+        )
+        grad_codes, grad_head = (
+            one.astype(F32) + two.astype(F32) for one, two in (codes, (grad_head, head_two))
         )
         grad_gate_up, grad_out, grad_down, grad_qkv, gain_part = sums
         grad_gains = gain_part[:3, :own_width]
         grad_classes = grad_classes[:own_width, :table_rows].T
     else:
+        gated = dot("btd,fd->btf", normed2, gate_w)
+        gate_part = gated[..., :hidden_width]
+        up_part = gated[..., hidden_width:]
+        hidden = (jax.nn.silu(gate_part) * up_part).astype(BF)
+        inverse1, inverse2, inverse3 = (
+            lax.rsqrt(jnp.mean(t * t, -1, keepdims=True) + NORM_EPS) for t in (stream0, stream1, stream2)
+        )
+        grad_stream2, gain_three = norm_backward(stream2, inverse3, gains32[2], grad_normed3)
+        grad_branch = grad_stream2.astype(BF)
+        grad_down = dot("btd,btf->df", grad_branch, hidden)
+        grad_hidden = dot("btd,df->btf", grad_branch, down_w)
+        sigma = jax.nn.sigmoid(gate_part)
+        grad_gate = grad_hidden * up_part * sigma * (1.0 + gate_part * (1.0 - sigma))
+        grad_up = grad_hidden * gate_part * sigma
+        grad_gated = jnp.concatenate([grad_gate, grad_up], -1).astype(BF)
+        grad_gate_up = dot("btf,btd->fd", grad_gated, normed2)
+        grad_normed2 = dot("btf,fd->btd", grad_gated, gate_w)
+        grad_middle, gain_two = norm_backward(stream1, inverse2, gains32[1], grad_normed2)
+        grad_stream1 = grad_stream2 + grad_middle
+        grad_attn = grad_stream1.astype(BF)
+        grad_out = dot("bte,btd->ed", grad_attn, attended)
+        grad_attended = dot("bte,ed->btd", grad_attn, out_w).astype(BF)
         queries, keys_rot, values, grad_attended = (
             t.reshape(split4) for t in (queries, keys_rot, values, grad_attended)
         )

time: 456 us -> 426 us (0.934)
  matrix products: 20.9 us -> 0 us
  other arithmetic: 32.7 us -> 26.4 us
    dot_general x6 -> x0, matrix products: 20.9 us -> none  [dot(): return jnp.einsum(subscripts, left, right, preferred_element_type=F32)]
    pallas_call x1, Pallas kernels: 144 us -> 149 us  [tail_phase(): pl.pallas_call(functools.partial(tail_kernel, z_size, y_size, own_width,...]
  transfers between devices with their start and end apart: 1 -> 0, of which waited for: 1 -> 0; matrix products, arithmetic and copies ran while one was open for 7% -> 0% of each run, Pallas kernels for 0% -> 0%
where the time goes in v6:
time: 426 us; the launch traced here: 418 us
  Pallas kernels  380 us (89%)
  other arithmetic  26.4 us (6%)
  local copies, waits for them, and re-layouts  6.32 us (1%)
  between operations  5.25 us (1%)
    pallas_call x1, Pallas kernels, tail_phase(): pl.pallas_call(functools.partial(tail_kernel, z_size, y_size, own_width,...  149 us
    pallas_call x1, Pallas kernels, head_phase(): pl.pallas_call(functools.partial(head_kernel, z_size, y_size, reps), out_...  116 us
    pallas_call x1, Pallas kernels, front(): pl.pallas_call(functools.partial(front_kernel, z_size, y_size, reps, own_...  101 us
    sub x8, other arithmetic, adam_update(): weight - rate * (first_hat / (jnp.sqrt(second_hat) + ADAM_EPS) + decay *...  21.1 us
    pallas_call x1, Pallas kernels, layer_forward(): pl.pallas_call(layer_kernel, out_shape=outs, in_specs=[vmem] * 3 + [hbm]...  14.9 us

profile of v6, /device:TPU:0, one launch (start us, length us, event | category | flops | bytes accessed | tf_op | source)
XLA Modules:
  0.0 418.2 jit_solution(6208666766086441760)
XLA Ops:
  2.6 0.1 add_convert_fusion.1
  2.7 0.7 convert_element_type.57
  3.4 0.7 convert_element_type.55
  4.1 0.8 add_convert_fusion
  4.8 0.6 fusion.9.facts
  5.4 0.9 convert_bitcast_fusion
  6.4 0.7 pad.22.class_b
  7.1 100.7 %front.1 = (bf16[16,256,768]{2,1,0:T(8,128)(2,1)}, bf16[16,144,768]{2,1,0:T(8,128)(2,1)}, bf16[16,48,768]{2,1,0:T(8,128)(2,1)}, bf16[16,48,2048]{2,1,0:T(8,128)(...) custom-call(f32[8,128]{1,0:T(8,128)} %fusion.9.facts, f32[1024,768]{1,0:T(8,128)} %code_table.1, ...), custom_call_target="tpu_custom_call" | custom-call | tf_op jit(solution)/shard_map/front/pallas_call | solution.py:138
  107.8 0.8 dynamic-slice_bitcast_fusion
  108.6 0.1 reshape.120
  108.7 0.6 pad.23.gains
  109.3 0.5 fusion.8
  109.8 0.3 maximum_bitcast_fusion
  110.1 0.7 pad_maximum_fusion.turn
  110.8 14.9 %layer.1 = (bf16[256,768]{1,0:T(8,128)(2,1)}, bf16[256,768]{1,0:T(8,128)(2,1)}, bf16[256,768]{1,0:T(8,128)(2,1)}, bf16[256,768]{1,0:T(8,128)(2,1)}, bf16[256,768...) custom-call(f32[256,768]{1,0:T(8,128)} %get-tuple-element.55.stream0, ...), custom_call_target="tpu_custom_call" | custom-call | tf_op jit(solution)/shard_map/layer/pallas_call | solution.py:1208
  125.7 115.6 %head.1 = (f32[256,768]{1,0:T(8,128)}, bf16[1024,768]{1,0:T(8,128)(2,1)}, f32[8,128]{1,0:T(8,128)}) custom-call(bf16[256,768]{1,0:T(8,128)(2,1)} %get-tuple-element.61.normed3, f32[1024,768]{1,0:T(8,128)} %head_weight.1, f32[2,16,8,128]{3,2,1,0:T(8,128)} %get-tuple-element.56.facts), custom_call_target="tpu_custom_call" | custom-call | tf_op jit(solution)/shard_map/head/pallas_call | solution.py:729
  241.4 1.3 fusion.20
  242.7 149.1 %tail.1 = (f32[256,768]{1,0:T(8,128)}, f32[48,768]{1,0:T(8,128)}, f32[48,2048]{1,0:T(8,128)}, f32[144,768]{1,0:T(8,128)}, f32[16,128]{1,0:T(8,128)}, /*index=5*/...) custom-call(bf16[256,768]{1,0:T(8,128)(2,1)} %get-tuple-element.63.q, ...), custom_call_target="tpu_custom_call" | custom-call | tf_op jit(solution)/shard_map/tail/pallas_call | solution.py:1098
  391.7 1.2 slice.25
  393.7 0.0 copy-start.9
  393.7 0.0 copy-start.6
  393.7 0.0 copy-start.14
  393.9 7.9 %multiply_subtract_fusion.1 = (f32[1024,768]{1,0:T(8,128)}, f32[1024,768]{1,0:T(8,128)}, f32[1024,768]{1,0:T(8,128)}) fusion(f32[1024,768]{1,0:T(8,128)S(1)} %copy-done, f32[]{:T(128)S(6)} %min_shard_map.3, bf16[1024,768]{1,0:T(8,128)(2,1)} %get-tuple-element.75, bf16[1024,768]{1,0:T(8,128)(2,1)} %get-tuple-element.74, f32[1024,768]{1,0:T(8,128)} %param.33, ...), kind=kLoop, calls=%fused_computation.8 | loop fusion | flops 14155776 | bytes 22020100 | tf_op jit(solution)/shard_map/sub | solution.py:1226
  401.8 2.0 multiply_subtract_fusion.5
  403.8 1.3 multiply_subtract_fusion.3
  405.1 0.8 multiply_subtract_fusion.6
  406.0 1.9 multiply_subtract_fusion.2
  407.9 1.2 multiply_subtract_fusion.4
  409.1 0.4 copy-done.2
  409.5 1.0 copy-done.3
  410.6 4.8 %multiply_subtract_fusion = (f32[1024,768]{1,0:T(8,128)}, f32[1024,768]{1,0:T(8,128)}, f32[1024,768]{1,0:T(8,128)}) fusion(f32[1024,768]{1,0:T(8,128)S(1)} %copy-done.1, f32[]{:T(128)S(6)} %min_shard_map.3, bf16[1024,768]{1,0:T(8,128)(2,1)S(1)} %copy-done.7, bf16[1024,768]{1,0:T(8,128)(2,1)S(1)} %copy-done.2, f32[1024,768]{1,0:T(8,128)S(1)} %copy-done.3, ...), kind=kLoop, calls=%fused_computation.6 | loop fusion | flops 14155776 | bytes 22020100 | tf_op jit(solution)/shard_map/sub | solution.py:1226
  415.4 1.3 multiply_subtract_fusion.7
  (55 shorter events, 0.2 us)
Async XLA Ops:
  242.6 151.0 %copy-start = (f32[1024,768]{1,0:T(8,128)S(1)}, f32[1024,768]{1,0:T(8,128)}, u32[]{:S(2)}) copy-start(f32[1024,768]{1,0:T(8,128)} %code_table.1) | copy-start | bytes 9437188
  393.7 8.1 %copy-start.9 = (f32[1001,48]{0,1:T(8,128)S(1)}, f32[1001,48]{0,1:T(8,128)}, u32[]{:S(2)}) copy-start(f32[1001,48]{0,1:T(8,128)} %param.35) | copy-start | bytes 576580
  393.7 8.1 %copy-start.20 = (f32[1001,48]{0,1:T(8,128)S(1)}, f32[1001,48]{0,1:T(8,128)}, u32[]{:S(2)}) copy-start(f32[1001,48]{0,1:T(8,128)} %param.36) | copy-start | bytes 576580
  393.7 8.1 %copy-start.21 = (f32[1001,48]{0,1:T(8,128)S(1)}, f32[1001,48]{0,1:T(8,128)}, u32[]{:S(2)}) copy-start(f32[1001,48]{0,1:T(8,128)} %param.37) | copy-start | bytes 576580
  393.7 10.1 %copy-start.6 = (f32[144,768]{1,0:T(8,128)S(1)}, f32[144,768]{1,0:T(8,128)}, u32[]{:S(2)}) copy-start(f32[144,768]{1,0:T(8,128)} %refs_1_.1) | copy-start | bytes 1327108
  393.7 10.1 %copy-start.14 = (f32[144,768]{1,0:T(8,128)S(1)}, f32[144,768]{1,0:T(8,128)}, u32[]{:S(2)}) copy-start(f32[144,768]{1,0:T(8,128)} %param.39) | copy-start | bytes 1327108
  393.7 10.0 %copy-start.15 = (f32[144,768]{1,0:T(8,128)S(1)}, f32[144,768]{1,0:T(8,128)}, u32[]{:S(2)}) copy-start(f32[144,768]{1,0:T(8,128)} %param.40) | copy-start | bytes 1327108
  393.7 10.0 %copy-start.16 = (f32[144,768]{1,0:T(8,128)S(1)}, f32[144,768]{1,0:T(8,128)}, u32[]{:S(2)}) copy-start(f32[144,768]{1,0:T(8,128)} %get-tuple-element.77) | copy-start | bytes 1327108
  393.8 11.4 %copy-start.13 = (f32[48,768]{1,0:T(8,128)S(1)}, f32[48,768]{1,0:T(8,128)}, u32[]{:S(2)}) copy-start(f32[48,768]{1,0:T(8,128)} %refs_2_.1) | copy-start | bytes 442372
  393.8 11.3 %copy-start.22 = (f32[48,768]{1,0:T(8,128)S(1)}, f32[48,768]{1,0:T(8,128)}, u32[]{:S(2)}) copy-start(f32[48,768]{1,0:T(8,128)} %param.42) | copy-start | bytes 442372
  393.8 11.3 %copy-start.23 = (f32[48,768]{1,0:T(8,128)S(1)}, f32[48,768]{1,0:T(8,128)}, u32[]{:S(2)}) copy-start(f32[48,768]{1,0:T(8,128)} %param.43) | copy-start | bytes 442372
  393.8 11.3 %copy-start.24 = (f32[48,768]{1,0:T(8,128)S(1)}, f32[48,768]{1,0:T(8,128)}, u32[]{:S(2)}) copy-start(f32[48,768]{1,0:T(8,128)} %get-tuple-element.78) | copy-start | bytes 442372
  393.8 12.2 %copy-start.10 = (f32[256,768]{1,0:T(8,128)S(1)}, f32[256,768]{1,0:T(8,128)}, u32[]{:S(2)}) copy-start(f32[256,768]{1,0:T(8,128)} %param.45) | copy-start | bytes 2359300
  393.8 12.2 %copy-start.11 = (f32[256,768]{1,0:T(8,128)S(1)}, f32[256,768]{1,0:T(8,128)}, u32[]{:S(2)}) copy-start(f32[256,768]{1,0:T(8,128)} %param.46) | copy-start | bytes 2359300
  393.8 12.1 %copy-start.12 = (f32[256,768]{1,0:T(8,128)S(1)}, f32[256,768]{1,0:T(8,128)}, u32[]{:S(2)}) copy-start(f32[256,768]{1,0:T(8,128)} %get-tuple-element.79) | copy-start | bytes 2359300
  393.8 14.0 %copy-start.17 = (f32[48,2048]{1,0:T(8,128)S(1)}, f32[48,2048]{1,0:T(8,128)}, u32[]{:S(2)}) copy-start(f32[48,2048]{1,0:T(8,128)} %param.48) | copy-start | bytes 1179652
  393.8 14.0 %copy-start.18 = (f32[48,2048]{1,0:T(8,128)S(1)}, f32[48,2048]{1,0:T(8,128)}, u32[]{:S(2)}) copy-start(f32[48,2048]{1,0:T(8,128)} %param.49) | copy-start | bytes 1179652
  393.9 14.0 %copy-start.19 = (f32[48,2048]{1,0:T(8,128)S(1)}, f32[48,2048]{1,0:T(8,128)}, u32[]{:S(2)}) copy-start(f32[48,2048]{1,0:T(8,128)} %get-tuple-element.80) | copy-start | bytes 1179652
  401.7 4.2 %copy-start.5 = (f32[256,768]{1,0:T(8,128)S(1)}, f32[256,768]{1,0:T(8,128)}, u32[]{:S(2)}) copy-start(f32[256,768]{1,0:T(8,128)} %refs_0_.1) | copy-start | bytes 2359300
  401.8 7.4 %copy-start.7 = (bf16[1024,768]{1,0:T(8,128)(2,1)S(1)}, bf16[1024,768]{1,0:T(8,128)(2,1)}, u32[]{:S(2)}) copy-start(bf16[1024,768]{1,0:T(8,128)(2,1)} %get-tuple-element.81) | copy-start | bytes 4718596
  403.8 5.3 %copy-start.4 = (f32[1024,768]{1,0:T(8,128)S(1)}, f32[1024,768]{1,0:T(8,128)}, u32[]{:S(2)}) copy-start(f32[1024,768]{1,0:T(8,128)} %param.52) | copy-start | bytes 9437188
  405.1 2.8 copy-start.8
  406.0 3.1 copy-start.1
  406.0 3.5 copy-start.2
  406.0 4.5 %copy-start.3 = (f32[1024,768]{1,0:T(8,128)S(1)}, f32[1024,768]{1,0:T(8,128)}, u32[]{:S(2)}) copy-start(f32[1024,768]{1,0:T(8,128)} %param.51) | copy-start | bytes 9437188
  410.6 4.8 %copy-start.25 = (f32[3,48]{1,0:T(4,128)S(1)}, f32[3,48]{1,0:T(4,128)}, u32[]{:S(2)}) copy-start(f32[3,48]{1,0:T(4,128)} %param.53) | copy-start | bytes 1732
  410.6 4.8 %copy-start.26 = (f32[3,48]{1,0:T(4,128)S(1)}, f32[3,48]{1,0:T(4,128)}, u32[]{:S(2)}) copy-start(f32[3,48]{1,0:T(4,128)} %param.54) | copy-start | bytes 1732
  410.6 4.8 %copy-start.27 = (f32[3,48]{1,0:T(4,128)S(1)}, f32[3,48]{1,0:T(4,128)}, u32[]{:S(2)}) copy-start(f32[3,48]{1,0:T(4,128)} %param.55) | copy-start | bytes 1732

commit v7 on v6

--- a/solution.py
+++ b/solution.py
@@ -600,17 +600,10 @@
 
     last = z_size - 1
 
-    def far(j):
-        return last - j // y_size, lax.rem(j, y_size)
-
-    def first_pass(j, carry):
-        dz, dyy = far(j)
-        dy = y_size - 1 - dyy
+    def for_twin(dz, dy):
         slot = dz * y_size + dy
         backward(p.at(dz, dy, 1), core_out.at[slot])
         send(core_out.at[slot], core_in.at[slot], rc_sems, (slot,), p.twin())
-        backward(p.at(dz, dy), acc.at[slot])
-        return carry
 
     def twin_sum(slot):
         arrival(core_in.at[slot], rc_sems, (slot,))
@@ -625,26 +618,39 @@
         acc[slot] = total.astype(BF)
 
     def round_of(g, carry):
-        dz = last - g
-
-        def per_dy(i, c):
-            return first_pass(g * y_size + i, c)
-
-        lax.fori_loop(0, y_size, per_dy, 0)
-        for dy in range(y_size - 1, -1, -1):
-            slot = dz * y_size + dy
-            twin_sum(slot)
-            if dy:
-                send(acc.at[slot], y_in.at[dz, dy], ry_sems, (dz, dy), (p.at(0, dy), x))
+        dz, near = last - g, last - g + 1
+
+        @pl.when(g < z_size)
+        def _():
+            for dy in range(1, y_size):
+                for_twin(dz, dy)
+                backward(p.at(dz, dy), acc.at[dz * y_size + dy])
 
         @pl.when(g >= 1)
         def _():
-            y_sum(dz + 1)
-            send(acc.at[(dz + 1) * y_size], z_in.at[dz + 1], rz_sems, (dz + 1,), (p.at(dz + 1, 0), x))
+            for_twin(near, 0)
+
+        @pl.when(g < z_size)
+        def _():
+            for dy in range(1, y_size):
+                slot = dz * y_size + dy
+                twin_sum(slot)
+                send(acc.at[slot], y_in.at[dz, dy], ry_sems, (dz, dy), (p.at(0, dy), x))
+
+        @pl.when(g >= 1)
+        def _():
+            slot = near * y_size
+            backward(p.at(near, 0), acc.at[slot])
+            twin_sum(slot)
+
+            @pl.when(near >= 1)
+            def _():
+                y_sum(near)
+                send(acc.at[slot], z_in.at[near], rz_sems, (near,), (p.at(near, 0), x))
 
         return carry
 
-    lax.fori_loop(0, z_size, round_of, 0)
+    lax.fori_loop(0, z_size + 1, round_of, 0)
 
     blocks = 4
     rows = own_rows // blocks
@@ -656,7 +662,7 @@
                 (((0,), (0,)), ((), ())), preferred_element_type=F32,
             )
 
-        total = lax.fori_loop(0, n, add, jnp.zeros((rows, width), F32))
+        total = lax.fori_loop(0, n, add, jnp.zeros((rows, width), F32), unroll=4)
         grad_head[r * rows : (r + 1) * rows] = total.astype(BF)
     y_sum(0)
     total = acc[0].astype(F32)
@@ -1006,7 +1012,7 @@
             ).astype(BF)
             return total + jnp.dot(hot, whole[image], preferred_element_type=F32)
 
-        total = lax.fori_loop(0, n, add, jnp.zeros((rows, width), F32))
+        total = lax.fori_loop(0, n, add, jnp.zeros((rows, width), F32), unroll=4)
         at = pl.ds(pl.multiple_of(r * rows, rows), rows)
         code_out[at] = total.astype(BF)
         send(code_out.at[at], code_in.at[at], co_sems, (r,), mate)

time: 426 us -> 415 us (0.974)
  Pallas kernels: 380 us -> 369 us
    pallas_call x1, Pallas kernels: 116 us -> 107 us  [head_phase(): pl.pallas_call(functools.partial(head_kernel, z_size, y_size, reps), out_...]
where the time goes in v7:
time: 415 us; the launch traced here: 407 us
  Pallas kernels  369 us (89%)
  other arithmetic  26.4 us (6%)
  local copies, waits for them, and re-layouts  6.32 us (2%)
  between operations  5.25 us (1%)
    pallas_call x1, Pallas kernels, tail_phase(): pl.pallas_call(functools.partial(tail_kernel, z_size, y_size, own_width,...  146 us
    pallas_call x1, Pallas kernels, head_phase(): pl.pallas_call(functools.partial(head_kernel, z_size, y_size, reps), out_...  107 us
    pallas_call x1, Pallas kernels, front(): pl.pallas_call(functools.partial(front_kernel, z_size, y_size, reps, own_...  101 us
    sub x8, other arithmetic, adam_update(): weight - rate * (first_hat / (jnp.sqrt(second_hat) + ADAM_EPS) + decay *...  21.1 us
    pallas_call x1, Pallas kernels, layer_forward(): pl.pallas_call(layer_kernel, out_shape=outs, in_specs=[vmem] * 3 + [hbm]...  14.9 us

profile of v7, /device:TPU:0, one launch (start us, length us, event | category | flops | bytes accessed | tf_op | source)
XLA Modules:
  0.0 407.0 jit_solution(12054808984151618091)
XLA Ops:
  2.6 0.1 add_convert_fusion.1
  2.7 0.7 convert_element_type.57
  3.4 0.7 convert_element_type.55
  4.1 0.8 add_convert_fusion
  4.8 0.6 fusion.9.facts
  5.4 0.9 convert_bitcast_fusion
  6.4 0.7 pad.22.class_b
  7.1 100.7 %front.1 = (bf16[16,256,768]{2,1,0:T(8,128)(2,1)}, bf16[16,144,768]{2,1,0:T(8,128)(2,1)}, bf16[16,48,768]{2,1,0:T(8,128)(2,1)}, bf16[16,48,2048]{2,1,0:T(8,128)(...) custom-call(f32[8,128]{1,0:T(8,128)} %fusion.9.facts, f32[1024,768]{1,0:T(8,128)} %code_table.1, ...), custom_call_target="tpu_custom_call" | custom-call | tf_op jit(solution)/shard_map/front/pallas_call | solution.py:138
  107.8 0.8 dynamic-slice_bitcast_fusion
  108.6 0.1 reshape.120
  108.7 0.6 pad.23.gains
  109.3 0.5 fusion.8
  109.8 0.3 maximum_bitcast_fusion
  110.1 0.7 pad_maximum_fusion.turn
  110.8 14.9 %layer.1 = (bf16[256,768]{1,0:T(8,128)(2,1)}, bf16[256,768]{1,0:T(8,128)(2,1)}, bf16[256,768]{1,0:T(8,128)(2,1)}, bf16[256,768]{1,0:T(8,128)(2,1)}, bf16[256,768...) custom-call(f32[256,768]{1,0:T(8,128)} %get-tuple-element.55.stream0, ...), custom_call_target="tpu_custom_call" | custom-call | tf_op jit(solution)/shard_map/layer/pallas_call | solution.py:1214
  125.7 107.5 %head.1 = (f32[256,768]{1,0:T(8,128)}, bf16[1024,768]{1,0:T(8,128)(2,1)}, f32[8,128]{1,0:T(8,128)}) custom-call(bf16[256,768]{1,0:T(8,128)(2,1)} %get-tuple-element.61.normed3, f32[1024,768]{1,0:T(8,128)} %head_weight.1, f32[2,16,8,128]{3,2,1,0:T(8,128)} %get-tuple-element.56.facts), custom_call_target="tpu_custom_call" | custom-call | tf_op jit(solution)/shard_map/head/pallas_call | solution.py:735
  233.2 1.3 fusion.20
  234.5 146.0 %tail.1 = (f32[256,768]{1,0:T(8,128)}, f32[48,768]{1,0:T(8,128)}, f32[48,2048]{1,0:T(8,128)}, f32[144,768]{1,0:T(8,128)}, f32[16,128]{1,0:T(8,128)}, /*index=5*/...) custom-call(bf16[256,768]{1,0:T(8,128)(2,1)} %get-tuple-element.63.q, ...), custom_call_target="tpu_custom_call" | custom-call | tf_op jit(solution)/shard_map/tail/pallas_call | solution.py:1104
  380.5 1.2 slice.25
  382.5 0.0 copy-start.21
  382.5 0.0 copy-start.6
  382.5 0.0 copy-start.13
  382.7 7.9 %multiply_subtract_fusion.1 = (f32[1024,768]{1,0:T(8,128)}, f32[1024,768]{1,0:T(8,128)}, f32[1024,768]{1,0:T(8,128)}) fusion(f32[1024,768]{1,0:T(8,128)S(1)} %copy-done, f32[]{:T(128)S(6)} %min_shard_map.3, bf16[1024,768]{1,0:T(8,128)(2,1)} %get-tuple-element.75, bf16[1024,768]{1,0:T(8,128)(2,1)} %get-tuple-element.74, f32[1024,768]{1,0:T(8,128)} %param.33, ...), kind=kLoop, calls=%fused_computation.8 | loop fusion | flops 14155776 | bytes 22020100 | tf_op jit(solution)/shard_map/sub | solution.py:1232
  390.6 2.0 multiply_subtract_fusion.5
  392.6 1.3 multiply_subtract_fusion.3
  393.9 0.8 multiply_subtract_fusion.6
  394.8 1.9 multiply_subtract_fusion.2
  396.7 1.2 multiply_subtract_fusion.4
  397.9 0.4 copy-done.2
  398.3 1.0 copy-done.3
  399.4 4.8 %multiply_subtract_fusion = (f32[1024,768]{1,0:T(8,128)}, f32[1024,768]{1,0:T(8,128)}, f32[1024,768]{1,0:T(8,128)}) fusion(f32[1024,768]{1,0:T(8,128)S(1)} %copy-done.1, f32[]{:T(128)S(6)} %min_shard_map.3, bf16[1024,768]{1,0:T(8,128)(2,1)S(1)} %copy-done.7, bf16[1024,768]{1,0:T(8,128)(2,1)S(1)} %copy-done.2, f32[1024,768]{1,0:T(8,128)S(1)} %copy-done.3, ...), kind=kLoop, calls=%fused_computation.6 | loop fusion | flops 14155776 | bytes 22020100 | tf_op jit(solution)/shard_map/sub | solution.py:1232
  404.1 1.3 multiply_subtract_fusion.7
  (55 shorter events, 0.2 us)
Async XLA Ops:
  234.5 147.9 %copy-start = (f32[1024,768]{1,0:T(8,128)S(1)}, f32[1024,768]{1,0:T(8,128)}, u32[]{:S(2)}) copy-start(f32[1024,768]{1,0:T(8,128)} %code_table.1) | copy-start | bytes 9437188
  382.5 8.1 %copy-start.9 = (f32[1001,48]{0,1:T(8,128)S(1)}, f32[1001,48]{0,1:T(8,128)}, u32[]{:S(2)}) copy-start(f32[1001,48]{0,1:T(8,128)} %param.35) | copy-start | bytes 576580
  382.5 8.1 %copy-start.20 = (f32[1001,48]{0,1:T(8,128)S(1)}, f32[1001,48]{0,1:T(8,128)}, u32[]{:S(2)}) copy-start(f32[1001,48]{0,1:T(8,128)} %param.36) | copy-start | bytes 576580
  382.5 8.1 %copy-start.21 = (f32[1001,48]{0,1:T(8,128)S(1)}, f32[1001,48]{0,1:T(8,128)}, u32[]{:S(2)}) copy-start(f32[1001,48]{0,1:T(8,128)} %param.37) | copy-start | bytes 576580
  382.5 10.1 %copy-start.6 = (f32[144,768]{1,0:T(8,128)S(1)}, f32[144,768]{1,0:T(8,128)}, u32[]{:S(2)}) copy-start(f32[144,768]{1,0:T(8,128)} %refs_1_.1) | copy-start | bytes 1327108
  382.5 10.1 %copy-start.14 = (f32[144,768]{1,0:T(8,128)S(1)}, f32[144,768]{1,0:T(8,128)}, u32[]{:S(2)}) copy-start(f32[144,768]{1,0:T(8,128)} %param.39) | copy-start | bytes 1327108
  382.5 10.0 %copy-start.15 = (f32[144,768]{1,0:T(8,128)S(1)}, f32[144,768]{1,0:T(8,128)}, u32[]{:S(2)}) copy-start(f32[144,768]{1,0:T(8,128)} %param.40) | copy-start | bytes 1327108
  382.5 10.0 %copy-start.16 = (f32[144,768]{1,0:T(8,128)S(1)}, f32[144,768]{1,0:T(8,128)}, u32[]{:S(2)}) copy-start(f32[144,768]{1,0:T(8,128)} %get-tuple-element.77) | copy-start | bytes 1327108
  382.5 11.4 %copy-start.13 = (f32[48,768]{1,0:T(8,128)S(1)}, f32[48,768]{1,0:T(8,128)}, u32[]{:S(2)}) copy-start(f32[48,768]{1,0:T(8,128)} %refs_2_.1) | copy-start | bytes 442372
  382.6 11.3 %copy-start.22 = (f32[48,768]{1,0:T(8,128)S(1)}, f32[48,768]{1,0:T(8,128)}, u32[]{:S(2)}) copy-start(f32[48,768]{1,0:T(8,128)} %param.42) | copy-start | bytes 442372
  382.6 11.3 %copy-start.23 = (f32[48,768]{1,0:T(8,128)S(1)}, f32[48,768]{1,0:T(8,128)}, u32[]{:S(2)}) copy-start(f32[48,768]{1,0:T(8,128)} %param.43) | copy-start | bytes 442372
  382.6 11.3 %copy-start.24 = (f32[48,768]{1,0:T(8,128)S(1)}, f32[48,768]{1,0:T(8,128)}, u32[]{:S(2)}) copy-start(f32[48,768]{1,0:T(8,128)} %get-tuple-element.78) | copy-start | bytes 442372
  382.6 12.2 %copy-start.10 = (f32[256,768]{1,0:T(8,128)S(1)}, f32[256,768]{1,0:T(8,128)}, u32[]{:S(2)}) copy-start(f32[256,768]{1,0:T(8,128)} %param.45) | copy-start | bytes 2359300
  382.6 12.2 %copy-start.11 = (f32[256,768]{1,0:T(8,128)S(1)}, f32[256,768]{1,0:T(8,128)}, u32[]{:S(2)}) copy-start(f32[256,768]{1,0:T(8,128)} %param.46) | copy-start | bytes 2359300
  382.6 12.1 %copy-start.12 = (f32[256,768]{1,0:T(8,128)S(1)}, f32[256,768]{1,0:T(8,128)}, u32[]{:S(2)}) copy-start(f32[256,768]{1,0:T(8,128)} %get-tuple-element.79) | copy-start | bytes 2359300
  382.6 14.0 %copy-start.17 = (f32[48,2048]{1,0:T(8,128)S(1)}, f32[48,2048]{1,0:T(8,128)}, u32[]{:S(2)}) copy-start(f32[48,2048]{1,0:T(8,128)} %param.48) | copy-start | bytes 1179652
  382.6 14.0 %copy-start.18 = (f32[48,2048]{1,0:T(8,128)S(1)}, f32[48,2048]{1,0:T(8,128)}, u32[]{:S(2)}) copy-start(f32[48,2048]{1,0:T(8,128)} %param.49) | copy-start | bytes 1179652
  382.6 14.0 %copy-start.19 = (f32[48,2048]{1,0:T(8,128)S(1)}, f32[48,2048]{1,0:T(8,128)}, u32[]{:S(2)}) copy-start(f32[48,2048]{1,0:T(8,128)} %get-tuple-element.80) | copy-start | bytes 1179652
  390.5 4.2 %copy-start.5 = (f32[256,768]{1,0:T(8,128)S(1)}, f32[256,768]{1,0:T(8,128)}, u32[]{:S(2)}) copy-start(f32[256,768]{1,0:T(8,128)} %refs_0_.1) | copy-start | bytes 2359300
  390.6 7.4 %copy-start.7 = (bf16[1024,768]{1,0:T(8,128)(2,1)S(1)}, bf16[1024,768]{1,0:T(8,128)(2,1)}, u32[]{:S(2)}) copy-start(bf16[1024,768]{1,0:T(8,128)(2,1)} %get-tuple-element.81) | copy-start | bytes 4718596
  392.6 5.3 %copy-start.4 = (f32[1024,768]{1,0:T(8,128)S(1)}, f32[1024,768]{1,0:T(8,128)}, u32[]{:S(2)}) copy-start(f32[1024,768]{1,0:T(8,128)} %param.52) | copy-start | bytes 9437188
  393.9 2.8 copy-start.8
  394.8 3.1 copy-start.1
  394.8 3.5 copy-start.2
  394.8 4.5 %copy-start.3 = (f32[1024,768]{1,0:T(8,128)S(1)}, f32[1024,768]{1,0:T(8,128)}, u32[]{:S(2)}) copy-start(f32[1024,768]{1,0:T(8,128)} %param.51) | copy-start | bytes 9437188
  399.3 4.8 %copy-start.25 = (f32[3,48]{1,0:T(4,128)S(1)}, f32[3,48]{1,0:T(4,128)}, u32[]{:S(2)}) copy-start(f32[3,48]{1,0:T(4,128)} %param.53) | copy-start | bytes 1732
  399.3 4.8 %copy-start.26 = (f32[3,48]{1,0:T(4,128)S(1)}, f32[3,48]{1,0:T(4,128)}, u32[]{:S(2)}) copy-start(f32[3,48]{1,0:T(4,128)} %param.54) | copy-start | bytes 1732
  399.4 4.8 %copy-start.27 = (f32[3,48]{1,0:T(4,128)S(1)}, f32[3,48]{1,0:T(4,128)}, u32[]{:S(2)}) copy-start(f32[3,48]{1,0:T(4,128)} %param.55) | copy-start | bytes 1732

commit v8 on v7

--- a/solution.py
+++ b/solution.py
@@ -1190,7 +1190,7 @@
         attended[:, at] = one_row(jnp.dot(probs, v, preferred_element_type=F32)).astype(BF)
         return carry
 
-    lax.fori_loop(0, width // 128, pair, 0)
+    lax.fori_loop(0, width // 128, pair, 0, unroll=2)
     moves[1].wait()
     stream1[...] = stream0[...] + product(attended[...], out_w[...], BY_LANES)
     normed2[...] = rms(stream1[...], 1)

time: 415 us -> 414 us (level)
  no operation moved by 1% of the time
where the time goes in v8:
time: 414 us; the launch traced here: 407 us
  Pallas kernels  369 us (89%)
  other arithmetic  26.4 us (6%)
  local copies, waits for them, and re-layouts  6.32 us (2%)
  between operations  5.25 us (1%)
    pallas_call x1, Pallas kernels, tail_phase(): pl.pallas_call(functools.partial(tail_kernel, z_size, y_size, own_width,...  146 us
    pallas_call x1, Pallas kernels, head_phase(): pl.pallas_call(functools.partial(head_kernel, z_size, y_size, reps), out_...  107 us
    pallas_call x1, Pallas kernels, front(): pl.pallas_call(functools.partial(front_kernel, z_size, y_size, reps, own_...  101 us
    sub x8, other arithmetic, adam_update(): weight - rate * (first_hat / (jnp.sqrt(second_hat) + ADAM_EPS) + decay *...  21.1 us
    pallas_call x1, Pallas kernels, layer_forward(): pl.pallas_call(layer_kernel, out_shape=outs, in_specs=[vmem] * 3 + [hbm]...  14.5 us

profile of v8, /device:TPU:0, one launch (start us, length us, event | category | flops | bytes accessed | tf_op | source)
XLA Modules:
  0.0 406.6 jit_solution(4680483719081355742)
XLA Ops:
  2.6 0.1 add_convert_fusion.1
  2.7 0.7 convert_element_type.57
  3.4 0.7 convert_element_type.55
  4.1 0.8 add_convert_fusion
  4.8 0.6 fusion.9.facts
  5.4 0.9 convert_bitcast_fusion
  6.4 0.7 pad.22.class_b
  7.1 100.7 %front.1 = (bf16[16,256,768]{2,1,0:T(8,128)(2,1)}, bf16[16,144,768]{2,1,0:T(8,128)(2,1)}, bf16[16,48,768]{2,1,0:T(8,128)(2,1)}, bf16[16,48,2048]{2,1,0:T(8,128)(...) custom-call(f32[8,128]{1,0:T(8,128)} %fusion.9.facts, f32[1024,768]{1,0:T(8,128)} %code_table.1, ...), custom_call_target="tpu_custom_call" | custom-call | tf_op jit(solution)/shard_map/front/pallas_call | solution.py:138
  107.8 0.8 dynamic-slice_bitcast_fusion
  108.6 0.1 reshape.120
  108.7 0.6 pad.23.gains
  109.3 0.5 fusion.8
  109.8 0.3 maximum_bitcast_fusion
  110.1 0.7 pad_maximum_fusion.turn
  110.8 14.5 %layer.1 = (bf16[256,768]{1,0:T(8,128)(2,1)}, bf16[256,768]{1,0:T(8,128)(2,1)}, bf16[256,768]{1,0:T(8,128)(2,1)}, bf16[256,768]{1,0:T(8,128)(2,1)}, bf16[256,768...) custom-call(f32[256,768]{1,0:T(8,128)} %get-tuple-element.55.stream0, ...), custom_call_target="tpu_custom_call" | custom-call | tf_op jit(solution)/shard_map/layer/pallas_call | solution.py:1214
  125.3 107.5 %head.1 = (f32[256,768]{1,0:T(8,128)}, bf16[1024,768]{1,0:T(8,128)(2,1)}, f32[8,128]{1,0:T(8,128)}) custom-call(bf16[256,768]{1,0:T(8,128)(2,1)} %get-tuple-element.61.normed3, f32[1024,768]{1,0:T(8,128)} %head_weight.1, f32[2,16,8,128]{3,2,1,0:T(8,128)} %get-tuple-element.56.facts), custom_call_target="tpu_custom_call" | custom-call | tf_op jit(solution)/shard_map/head/pallas_call | solution.py:735
  232.8 1.3 fusion.20
  234.1 146.0 %tail.1 = (f32[256,768]{1,0:T(8,128)}, f32[48,768]{1,0:T(8,128)}, f32[48,2048]{1,0:T(8,128)}, f32[144,768]{1,0:T(8,128)}, f32[16,128]{1,0:T(8,128)}, /*index=5*/...) custom-call(bf16[256,768]{1,0:T(8,128)(2,1)} %get-tuple-element.63.q, ...), custom_call_target="tpu_custom_call" | custom-call | tf_op jit(solution)/shard_map/tail/pallas_call | solution.py:1104
  380.1 1.2 slice.25
  382.0 0.0 copy-start.9
  382.1 0.0 copy-start.20
  382.1 0.0 copy-start.14
  382.2 7.9 %multiply_subtract_fusion.1 = (f32[1024,768]{1,0:T(8,128)}, f32[1024,768]{1,0:T(8,128)}, f32[1024,768]{1,0:T(8,128)}) fusion(f32[1024,768]{1,0:T(8,128)S(1)} %copy-done, f32[]{:T(128)S(6)} %min_shard_map.3, bf16[1024,768]{1,0:T(8,128)(2,1)} %get-tuple-element.75, bf16[1024,768]{1,0:T(8,128)(2,1)} %get-tuple-element.74, f32[1024,768]{1,0:T(8,128)} %param.33, ...), kind=kLoop, calls=%fused_computation.8 | loop fusion | flops 14155776 | bytes 22020100 | tf_op jit(solution)/shard_map/sub | solution.py:1232
  390.2 2.0 multiply_subtract_fusion.5
  392.2 1.3 multiply_subtract_fusion.3
  393.5 0.8 multiply_subtract_fusion.6
  394.4 1.9 multiply_subtract_fusion.2
  396.3 1.2 multiply_subtract_fusion.4
  397.5 0.4 copy-done.2
  397.9 1.0 copy-done.3
  398.9 4.8 %multiply_subtract_fusion = (f32[1024,768]{1,0:T(8,128)}, f32[1024,768]{1,0:T(8,128)}, f32[1024,768]{1,0:T(8,128)}) fusion(f32[1024,768]{1,0:T(8,128)S(1)} %copy-done.1, f32[]{:T(128)S(6)} %min_shard_map.3, bf16[1024,768]{1,0:T(8,128)(2,1)S(1)} %copy-done.7, bf16[1024,768]{1,0:T(8,128)(2,1)S(1)} %copy-done.2, f32[1024,768]{1,0:T(8,128)S(1)} %copy-done.3, ...), kind=kLoop, calls=%fused_computation.6 | loop fusion | flops 14155776 | bytes 22020100 | tf_op jit(solution)/shard_map/sub | solution.py:1232
  403.7 1.3 multiply_subtract_fusion.7
  (55 shorter events, 0.2 us)
Async XLA Ops:
  234.1 147.9 %copy-start = (f32[1024,768]{1,0:T(8,128)S(1)}, f32[1024,768]{1,0:T(8,128)}, u32[]{:S(2)}) copy-start(f32[1024,768]{1,0:T(8,128)} %code_table.1) | copy-start | bytes 9437188
  382.0 8.1 %copy-start.9 = (f32[1001,48]{0,1:T(8,128)S(1)}, f32[1001,48]{0,1:T(8,128)}, u32[]{:S(2)}) copy-start(f32[1001,48]{0,1:T(8,128)} %param.35) | copy-start | bytes 576580
  382.1 8.1 %copy-start.20 = (f32[1001,48]{0,1:T(8,128)S(1)}, f32[1001,48]{0,1:T(8,128)}, u32[]{:S(2)}) copy-start(f32[1001,48]{0,1:T(8,128)} %param.36) | copy-start | bytes 576580
  382.1 8.1 %copy-start.21 = (f32[1001,48]{0,1:T(8,128)S(1)}, f32[1001,48]{0,1:T(8,128)}, u32[]{:S(2)}) copy-start(f32[1001,48]{0,1:T(8,128)} %param.37) | copy-start | bytes 576580
  382.1 10.1 %copy-start.6 = (f32[144,768]{1,0:T(8,128)S(1)}, f32[144,768]{1,0:T(8,128)}, u32[]{:S(2)}) copy-start(f32[144,768]{1,0:T(8,128)} %refs_1_.1) | copy-start | bytes 1327108
  382.1 10.1 %copy-start.14 = (f32[144,768]{1,0:T(8,128)S(1)}, f32[144,768]{1,0:T(8,128)}, u32[]{:S(2)}) copy-start(f32[144,768]{1,0:T(8,128)} %param.39) | copy-start | bytes 1327108
  382.1 10.0 %copy-start.15 = (f32[144,768]{1,0:T(8,128)S(1)}, f32[144,768]{1,0:T(8,128)}, u32[]{:S(2)}) copy-start(f32[144,768]{1,0:T(8,128)} %param.40) | copy-start | bytes 1327108
  382.1 10.0 %copy-start.16 = (f32[144,768]{1,0:T(8,128)S(1)}, f32[144,768]{1,0:T(8,128)}, u32[]{:S(2)}) copy-start(f32[144,768]{1,0:T(8,128)} %get-tuple-element.77) | copy-start | bytes 1327108
  382.1 11.4 %copy-start.13 = (f32[48,768]{1,0:T(8,128)S(1)}, f32[48,768]{1,0:T(8,128)}, u32[]{:S(2)}) copy-start(f32[48,768]{1,0:T(8,128)} %refs_2_.1) | copy-start | bytes 442372
  382.1 11.3 %copy-start.22 = (f32[48,768]{1,0:T(8,128)S(1)}, f32[48,768]{1,0:T(8,128)}, u32[]{:S(2)}) copy-start(f32[48,768]{1,0:T(8,128)} %param.42) | copy-start | bytes 442372
  382.2 11.3 %copy-start.23 = (f32[48,768]{1,0:T(8,128)S(1)}, f32[48,768]{1,0:T(8,128)}, u32[]{:S(2)}) copy-start(f32[48,768]{1,0:T(8,128)} %param.43) | copy-start | bytes 442372
  382.2 11.3 %copy-start.24 = (f32[48,768]{1,0:T(8,128)S(1)}, f32[48,768]{1,0:T(8,128)}, u32[]{:S(2)}) copy-start(f32[48,768]{1,0:T(8,128)} %get-tuple-element.78) | copy-start | bytes 442372
  382.2 12.2 %copy-start.10 = (f32[256,768]{1,0:T(8,128)S(1)}, f32[256,768]{1,0:T(8,128)}, u32[]{:S(2)}) copy-start(f32[256,768]{1,0:T(8,128)} %param.45) | copy-start | bytes 2359300
  382.2 12.2 %copy-start.11 = (f32[256,768]{1,0:T(8,128)S(1)}, f32[256,768]{1,0:T(8,128)}, u32[]{:S(2)}) copy-start(f32[256,768]{1,0:T(8,128)} %param.46) | copy-start | bytes 2359300
  382.2 12.1 %copy-start.12 = (f32[256,768]{1,0:T(8,128)S(1)}, f32[256,768]{1,0:T(8,128)}, u32[]{:S(2)}) copy-start(f32[256,768]{1,0:T(8,128)} %get-tuple-element.79) | copy-start | bytes 2359300
  382.2 14.0 %copy-start.17 = (f32[48,2048]{1,0:T(8,128)S(1)}, f32[48,2048]{1,0:T(8,128)}, u32[]{:S(2)}) copy-start(f32[48,2048]{1,0:T(8,128)} %param.48) | copy-start | bytes 1179652
  382.2 14.0 %copy-start.18 = (f32[48,2048]{1,0:T(8,128)S(1)}, f32[48,2048]{1,0:T(8,128)}, u32[]{:S(2)}) copy-start(f32[48,2048]{1,0:T(8,128)} %param.49) | copy-start | bytes 1179652
  382.2 14.0 %copy-start.19 = (f32[48,2048]{1,0:T(8,128)S(1)}, f32[48,2048]{1,0:T(8,128)}, u32[]{:S(2)}) copy-start(f32[48,2048]{1,0:T(8,128)} %get-tuple-element.80) | copy-start | bytes 1179652
  390.1 4.2 %copy-start.5 = (f32[256,768]{1,0:T(8,128)S(1)}, f32[256,768]{1,0:T(8,128)}, u32[]{:S(2)}) copy-start(f32[256,768]{1,0:T(8,128)} %refs_0_.1) | copy-start | bytes 2359300
  390.1 7.4 %copy-start.7 = (bf16[1024,768]{1,0:T(8,128)(2,1)S(1)}, bf16[1024,768]{1,0:T(8,128)(2,1)}, u32[]{:S(2)}) copy-start(bf16[1024,768]{1,0:T(8,128)(2,1)} %get-tuple-element.81) | copy-start | bytes 4718596
  392.2 5.3 %copy-start.4 = (f32[1024,768]{1,0:T(8,128)S(1)}, f32[1024,768]{1,0:T(8,128)}, u32[]{:S(2)}) copy-start(f32[1024,768]{1,0:T(8,128)} %param.52) | copy-start | bytes 9437188
  393.5 2.8 copy-start.8
  394.4 3.1 copy-start.1
  394.4 3.5 copy-start.2
  394.4 4.5 %copy-start.3 = (f32[1024,768]{1,0:T(8,128)S(1)}, f32[1024,768]{1,0:T(8,128)}, u32[]{:S(2)}) copy-start(f32[1024,768]{1,0:T(8,128)} %param.51) | copy-start | bytes 9437188
  398.9 4.8 %copy-start.25 = (f32[3,48]{1,0:T(4,128)S(1)}, f32[3,48]{1,0:T(4,128)}, u32[]{:S(2)}) copy-start(f32[3,48]{1,0:T(4,128)} %param.53) | copy-start | bytes 1732
  398.9 4.8 %copy-start.26 = (f32[3,48]{1,0:T(4,128)S(1)}, f32[3,48]{1,0:T(4,128)}, u32[]{:S(2)}) copy-start(f32[3,48]{1,0:T(4,128)} %param.54) | copy-start | bytes 1732
  398.9 4.8 %copy-start.27 = (f32[3,48]{1,0:T(4,128)S(1)}, f32[3,48]{1,0:T(4,128)}, u32[]{:S(2)}) copy-start(f32[3,48]{1,0:T(4,128)} %param.55) | copy-start | bytes 1732
